TPU v7x, 128 devices: a whole 4x4x4 slice. The times are simulated.
128 devices in a mesh: dp: 4 (over x_lo, core), blk: 32 (over y, z, x_hi).
Axes of the slice: x: 4 (x_hi: 2, x_lo: 2; x = x_hi * 2 + x_lo), y: 4, z: 4, core: 2. Of those that a mesh axis runs over, the one named last changes fastest.
Arguments:
- tokens: bfloat16 [32768, 768], P(('dp', 'blk')), may hold values from -6 to 6
- attn_gain: bfloat16 [768], replicated, may hold values from 0.099609375 to 1.8984375
- attn_bias: bfloat16 [768], replicated, may hold values from -3 to 3
- mlp_gain: bfloat16 [768], replicated, may hold values from 0.099609375 to 1.8984375
- mlp_bias: bfloat16 [768], replicated, may hold values from -3 to 3
- qkv_weight: bfloat16 [768, 2304], replicated, may hold values from -0.21875 to 0.21875
- qkv_bias: bfloat16 [2304], replicated, may hold values from -3 to 3
- out_weight: bfloat16 [768, 768], replicated, may hold values from -1.75 to 1.75
- out_bias: bfloat16 [768], replicated, may hold values from -3 to 3
- up_weight: bfloat16 [768, 3072], replicated, may hold values from -0.21875 to 0.21875
- up_bias: bfloat16 [3072], replicated, may hold values from -3 to 3
- down_weight: bfloat16 [3072, 768], replicated, may hold values from -0.109375 to 0.109375
- down_bias: bfloat16 [768], replicated, may hold values from -3 to 3
- cotangent: bfloat16 [32768, 768], P(('dp', 'blk')), may hold values from -6 to 6
- doc_lengths: int32 [4, 16], P('dp'), may hold values from 1 to 4096, as said below
- span_order: int32 [4, 64], P('dp'), may hold values from 0 to 63, as said below
Outputs:
- mixed: bfloat16 [32768, 768], P(('dp', 'blk'))
- tokens_grad: float32 [32768, 768], P(('dp', 'blk'))
- grad_attn_gain: float32 [768], replicated
- grad_attn_bias: float32 [768], replicated
- grad_mlp_gain: float32 [768], replicated
- grad_mlp_bias: float32 [768], replicated
- grad_qkv_weight: float32 [768, 2304], replicated
- grad_qkv_bias: float32 [2304], replicated
- grad_out_weight: float32 [768, 768], replicated
- grad_out_bias: float32 [768], replicated
- grad_up_weight: float32 [768, 3072], replicated
- grad_up_bias: float32 [3072], replicated
- grad_down_weight: float32 [3072, 768], replicated
- grad_down_bias: float32 [768], replicated
- rms_output: float32 [], replicated
- rms_attention: float32 [], replicated
- rms_mlp: float32 [], replicated
Inputs may be any that keep to these rules, and one draw needn't show every extreme that they name: `doc_lengths`: in each row one sequence of 4096 tokens stands first or last; the other 15 hold at most 512 tokens each and together 4096, and one of them holds exactly 512. `span_order`: each row is a permutation of the 64 spans of 128 stream places; entries 2 i and 2 i + 1 are the spans of device i along blk, in that order in its rows; the first is under 64 / 2 and the two add up to 63.
All inputs are finite; a program needn't handle non-finite values.
Results may differ from a plain program's by a relative error of at most 0.011.
Values may be sent and summed in bfloat16 or wider, within the bound.
A program may use at most 192 MiB of HBM per device.

v0:
```python
import math

import jax
import jax.numpy as jnp
from jax import lax
from jax.sharding import PartitionSpec as P

HEADS = 12
HEAD_DIM = 64
ROTARY = 16


epsilon = 1e-05
masked_score = -1e30


def from_behind(block, axis, distance):
    devices = range(lax.axis_size(axis))
    route = [((i - distance) % len(devices), i) for i in devices]
    return lax.ppermute(block, axis, route)


def layer_norm(values, gain_vec, shift_vec):
    center = values - jnp.mean(values, axis=-1, keepdims=True)
    spread = jnp.mean(center * center, axis=-1, keepdims=True)
    return center * lax.rsqrt(spread + epsilon) * gain_vec + shift_vec


def rotary_tables(position, rotary_dims):
    half_dims = rotary_dims // 2
    steps_vec = jnp.arange(half_dims).astype(jnp.float32)
    inverse = jnp.exp(steps_vec * (-2.0 * math.log(10000.0) / rotary_dims))
    angles = position.astype(jnp.float32)[:, None] * inverse[None, :]
    return (jnp.cos(angles), jnp.sin(angles))


def rotate(values, cosine, sine_part):
    half_dims = cosine.shape[-1]
    first_half = values[..., :half_dims]
    second_half = values[..., half_dims : 2 * half_dims]
    cos_rows = cosine[:, None, :]
    sin_rows = sine_part[:, None, :]
    return jnp.concatenate(
        [
            first_half * cos_rows - second_half * sin_rows,
            second_half * cos_rows + first_half * sin_rows,
            values[..., 2 * half_dims :],
        ],
        axis=-1,
    )


def stream_rows(rows_global, order_row, piece_rows):
    slots = rows_global // piece_rows
    table = jnp.arange(order_row.shape[0], dtype=jnp.int32)
    span_ids = jnp.sum(jnp.where(slots[:, None] == table[None, :], order_row[None, :], 0), axis=1)
    return span_ids * piece_rows + rows_global % piece_rows


def segment_rows(stream, lengths_row):
    ends = jnp.cumsum(lengths_row)
    segment = jnp.sum((ends[None, :] <= stream[:, None]).astype(jnp.int32), axis=1)
    table = jnp.arange(lengths_row.shape[0], dtype=jnp.int32)
    starts = jnp.sum(
        jnp.where(segment[:, None] == table[None, :], (ends - lengths_row)[None, :], 0), axis=1
    )
    return (segment, stream - starts)


def gelu_exact(values):
    return jax.nn.gelu(values, approximate=False)


def allowed_pairs(query_meta, key_meta):
    same_doc = query_meta[1][:, None] == key_meta[1][None, :]
    return same_doc & (key_meta[0][None, :] <= query_meta[0][:, None])


def fold_blocks(carry, members, step_fn):
    count_rows = members[0].shape[0]
    width = math.gcd(count_rows, 512)
    groups = count_rows // width
    stacked = tuple((member.reshape((groups, width) + member.shape[1:]) for member in members))

    def inner(state, block_inputs):
        block_index, parts = block_inputs
        return (step_fn(state, parts, block_index * width), None)

    result, unused = lax.scan(inner, carry, (jnp.arange(groups, dtype=jnp.int32), stacked))
    return result


def on_device(
    tokens,
    attn_gain,
    attn_bias,
    mlp_gain,
    mlp_bias,
    qkv_weight,
    qkv_bias,
    out_weight,
    out_bias,
    up_weight,
    up_bias,
    down_weight,
    down_bias,
    cotangent,
    doc_lengths,
    span_order,
):
    count_dev = lax.axis_size("blk")
    my_index = lax.axis_index("blk")
    tok_rows = tokens.shape[0]
    width = tokens.shape[1]
    piece_rows = tok_rows // 2
    scale_val = HEAD_DIM ** (-0.5)
    order_row = span_order[0]
    lengths_row = doc_lengths[0]
    local_range = jnp.arange(tok_rows, dtype=jnp.int32)
    head_shape = (tok_rows, HEADS, HEAD_DIM)
    contract_rows = (((0,), (0,)), ((), ()))
    contract_cols = (((1,), (1,)), ((), ()))

    def describe(rows_global):
        stream = stream_rows(rows_global, order_row, piece_rows)
        segment, position = segment_rows(stream, lengths_row)
        return (stream, segment, position)

    def score_block(query_part, key_part):
        return (
            jnp.einsum("qhd,khd->hqk", query_part, key_part, preferred_element_type=jnp.float32)
            * scale_val
        )

    my_stream, my_segment, my_position = describe(my_index * tok_rows + local_range)
    my_meta = (my_stream, my_segment)
    inputs = tokens.astype(jnp.float32)
    h_attn, attn_norm_back = jax.vjp(
        layer_norm, inputs, attn_gain.astype(jnp.float32), attn_bias.astype(jnp.float32)
    )
    h_mlp, mlp_norm_back = jax.vjp(
        layer_norm, inputs, mlp_gain.astype(jnp.float32), mlp_bias.astype(jnp.float32)
    )
    h_attn_b = h_attn.astype(jnp.bfloat16)
    h_mlp_b = h_mlp.astype(jnp.bfloat16)
    mixed_qkv = jnp.dot(h_attn_b, qkv_weight, preferred_element_type=jnp.float32) + qkv_bias.astype(
        jnp.float32
    )
    cosine, sine_part = rotary_tables(my_position, ROTARY)

    def rotate_pair(query_in, key_in):
        return (rotate(query_in, cosine, sine_part), rotate(key_in, cosine, sine_part))

    rotated, rotate_back = jax.vjp(
        rotate_pair,
        mixed_qkv[:, :width].reshape(head_shape),
        mixed_qkv[:, width : 2 * width].reshape(head_shape),
    )
    query_b = rotated[0].astype(jnp.bfloat16)
    key_b = rotated[1].astype(jnp.bfloat16)
    value_b = mixed_qkv[:, 2 * width :].reshape(head_shape).astype(jnp.bfloat16)
    grad_att_b = (
        lax.dot_general(cotangent, out_weight, contract_cols, preferred_element_type=jnp.float32)
        .astype(jnp.bfloat16)
        .reshape(head_shape)
    )

    def stats_block(state, members, first_row):
        key_part = members[0]
        key_info = describe(first_row + jnp.arange(key_part.shape[0], dtype=jnp.int32))
        allowed = allowed_pairs(my_meta, (key_info[0], key_info[1]))
        top_now, total_now = state
        scores = score_block(query_b, key_part)
        top_new = jnp.maximum(
            top_now, jnp.max(jnp.where(allowed[None], scores, masked_score), axis=-1)
        )
        raised = jnp.where(allowed[None], jnp.exp(scores - top_new[..., None]), 0.0)
        return (top_new, total_now * jnp.exp(top_now - top_new) + jnp.sum(raised, axis=-1))

    start_top = jnp.full((HEADS, tok_rows), masked_score, jnp.float32)
    start_total = jnp.zeros((HEADS, tok_rows), jnp.float32)
    top_score, total_sum = fold_blocks(
        (start_top, start_total), (lax.all_gather(key_b, "blk", axis=0, tiled=True),), stats_block
    )
    log_total = top_score + jnp.log(total_sum)

    def output_block(state, members, first_row):
        key_part, value_part = members
        key_info = describe(first_row + jnp.arange(key_part.shape[0], dtype=jnp.int32))
        allowed = allowed_pairs(my_meta, (key_info[0], key_info[1]))
        out_now, delta_now = state
        scores = score_block(query_b, key_part)
        probs = jnp.where(allowed[None], jnp.exp(scores - log_total[..., None]), 0.0)
        out_new = out_now + jnp.einsum(
            "hqk,khd->qhd",
            probs.astype(jnp.bfloat16),
            value_part,
            preferred_element_type=jnp.float32,
        )
        grad_probs = jnp.einsum(
            "qhd,khd->hqk", grad_att_b, value_part, preferred_element_type=jnp.float32
        )
        return (out_new, delta_now + jnp.sum(probs * grad_probs, axis=-1))

    attended, delta = fold_blocks(
        (jnp.zeros(head_shape, jnp.float32), jnp.zeros((HEADS, tok_rows), jnp.float32)),
        (
            lax.all_gather(key_b, "blk", axis=0, tiled=True),
            lax.all_gather(value_b, "blk", axis=0, tiled=True),
        ),
        output_block,
    )
    attended_b = attended.reshape(tok_rows, width).astype(jnp.bfloat16)
    attn_branch = jnp.dot(
        attended_b, out_weight, preferred_element_type=jnp.float32
    ) + out_bias.astype(jnp.float32)
    pre_act = jnp.dot(h_mlp_b, up_weight, preferred_element_type=jnp.float32) + up_bias.astype(
        jnp.float32
    )
    hidden, gelu_back = jax.vjp(gelu_exact, pre_act)
    hidden_b = hidden.astype(jnp.bfloat16)
    mlp_branch = jnp.dot(
        hidden_b, down_weight, preferred_element_type=jnp.float32
    ) + down_bias.astype(jnp.float32)
    output = inputs + attn_branch + mlp_branch
    grad_out = cotangent.astype(jnp.float32)
    grad_out_weight = lax.dot_general(
        attended_b, cotangent, contract_rows, preferred_element_type=jnp.float32
    )
    grad_branch_bias = jnp.sum(grad_out, axis=0)
    grad_down_weight = lax.dot_general(
        hidden_b, cotangent, contract_rows, preferred_element_type=jnp.float32
    )
    grad_hidden = lax.dot_general(
        cotangent, down_weight, contract_cols, preferred_element_type=jnp.float32
    )
    grad_pre_b = gelu_back(grad_hidden)[0].astype(jnp.bfloat16)
    grad_up_weight = lax.dot_general(
        h_mlp_b, grad_pre_b, contract_rows, preferred_element_type=jnp.float32
    )
    grad_up_bias = jnp.sum(grad_pre_b.astype(jnp.float32), axis=0)
    grad_h_mlp = lax.dot_general(
        grad_pre_b, up_weight, contract_cols, preferred_element_type=jnp.float32
    )

    def back_block(
        query_part, grad_part, lse_part, delta_part, query_meta, key_part, value_part, key_meta
    ):
        allowed = allowed_pairs(query_meta, key_meta)
        scores = score_block(query_part, key_part)
        probs = jnp.where(allowed[None], jnp.exp(scores - lse_part[..., None]), 0.0)
        grad_probs = jnp.einsum(
            "qhd,khd->hqk", grad_part, value_part, preferred_element_type=jnp.float32
        )
        grad_scores = (probs * (grad_probs - delta_part[..., None])).astype(jnp.bfloat16)
        query_term = jnp.einsum(
            "hqk,khd->qhd", grad_scores, key_part, preferred_element_type=jnp.float32
        )
        key_term = jnp.einsum(
            "hqk,qhd->khd", grad_scores, query_part, preferred_element_type=jnp.float32
        )
        value_term = jnp.einsum(
            "hqk,qhd->khd",
            probs.astype(jnp.bfloat16),
            grad_part,
            preferred_element_type=jnp.float32,
        )
        return (query_term, key_term, value_term)

    def anchor_meta(step_index):
        anchor = (my_index - step_index) % count_dev
        info = describe(anchor * tok_rows + local_range)
        return (info[0], info[1])

    own_query, own_key, own_value = back_block(
        query_b, grad_att_b, log_total, delta, my_meta, key_b, value_b, my_meta
    )

    def send_key_grads(key_grads):
        return from_behind((key_grads[0], key_grads[1]), "blk", 1)

    def key_step(step_index, state):
        query_acc, moving, key_grads = state
        key_grads = send_key_grads(key_grads)
        moving = from_behind((moving[0], moving[1]), "blk", 1)
        query_term, key_term, value_term = back_block(
            query_b,
            grad_att_b,
            log_total,
            delta,
            my_meta,
            moving[0],
            moving[1],
            anchor_meta(step_index),
        )
        return (
            query_acc + query_term,
            moving,
            (key_grads[0] + key_term, key_grads[1] + value_term),
        )

    grad_query, moved, key_grads = lax.fori_loop(
        1, count_dev, key_step, (own_query, (key_b, value_b), (own_key, own_value))
    )
    key_grads = send_key_grads(key_grads)
    grad_key, grad_value = (key_grads[0], key_grads[1])
    grad_query_pre, grad_key_pre = rotate_back((grad_query * scale_val, grad_key * scale_val))
    grad_qkv_b = jnp.concatenate(
        [
            grad_query_pre.reshape(tok_rows, width),
            grad_key_pre.reshape(tok_rows, width),
            grad_value.reshape(tok_rows, width),
        ],
        axis=1,
    ).astype(jnp.bfloat16)
    grad_qkv_weight = lax.dot_general(
        h_attn_b, grad_qkv_b, contract_rows, preferred_element_type=jnp.float32
    )
    grad_qkv_bias = jnp.sum(grad_qkv_b.astype(jnp.float32), axis=0)
    grad_h_attn = lax.dot_general(
        grad_qkv_b, qkv_weight, contract_cols, preferred_element_type=jnp.float32
    )
    attn_in, grad_attn_gain, grad_attn_bias = attn_norm_back(grad_h_attn)
    mlp_in, grad_mlp_gain, grad_mlp_bias = mlp_norm_back(grad_h_mlp)
    tokens_grad = grad_out + attn_in + mlp_in
    summed = lax.psum(
        (
            grad_attn_gain,
            grad_attn_bias,
            grad_mlp_gain,
            grad_mlp_bias,
            grad_qkv_weight,
            grad_qkv_bias,
            grad_out_weight,
            grad_branch_bias,
            grad_up_weight,
            grad_up_bias,
            grad_down_weight,
            jnp.sum(output * output),
            jnp.sum(attn_branch * attn_branch),
            jnp.sum(mlp_branch * mlp_branch),
        ),
        ("dp", "blk"),
    )
    total_count = tok_rows * lax.axis_size("dp") * count_dev * width
    return (
        output.astype(jnp.bfloat16),
        tokens_grad,
        summed[0],
        summed[1],
        summed[2],
        summed[3],
        summed[4],
        summed[5],
        summed[6],
        summed[7],
        summed[8],
        summed[9],
        summed[10],
        summed[7],
        jnp.sqrt(summed[11] / total_count),
        jnp.sqrt(summed[12] / total_count),
        jnp.sqrt(summed[13] / total_count),
    )


def solution(mesh):
    return jax.shard_map(
        on_device,
        mesh=mesh,
        in_specs=(
            P(("dp", "blk"), None),
            P(),
            P(),
            P(),
            P(),
            P(),
            P(),
            P(),
            P(),
            P(),
            P(),
            P(),
            P(),
            P(("dp", "blk"), None),
            P("dp", None),
            P("dp", None),
        ),
        out_specs=(
            P(("dp", "blk"), None),
            P(("dp", "blk"), None),
            P(),
            P(),
            P(),
            P(),
            P(),
            P(),
            P(),
            P(),
            P(),
            P(),
            P(),
            P(),
            P(),
            P(),
            P(),
        ),
        check_vma=False,
    )
```

profile of v0, /device:TPU:1, one launch (start us, length us, event | category | flops | bytes accessed | tf_op | source)
XLA Modules:
  0.0 2751.9 jit_solution(11228919087712982407)
XLA Ops:
  52.6 11.0 convert_reduce_fusion.3
  70.6 74.0 %all-gather.3.cloned.1.call-done = bf16[8192,12,64]{0,2,1:T(8,128)(2,1)} async-done(((bf16[256,12,64]{0,2,1:T(8,128)(2,1)}), bf16[8192,12,64]{0,2,1:T(8,128)(2,1)}) %all-gather.3.cloned.1.call-update) | async-done | bytes 12582928 | tf_op jit(solution)/shard_map/all_gather | solution.py:209
  144.7 10.8 copy.73
  155.5 115.0 %all-gather.5.cloned.1.call-done = bf16[8192,12,64]{0,2,1:T(8,128)(2,1)} async-done(((bf16[256,12,64]{0,2,1:T(8,128)(2,1)}), bf16[8192,12,64]{0,2,1:T(8,128)(2,1)}) %all-gather.5.cloned.1.call-update) | async-done | bytes 12582928 | tf_op jit(solution)/shard_map/all_gather | solution.py:208
  270.5 10.8 copy.72
  281.8 246.7 %while.56 = (s32[]{:T(128)}, f32[12,256]{1,0:T(8,128)S(1)}, f32[12,256]{1,0:T(8,128)}, s32[256]{0:T(256)}, s32[1,16]{1,0:T(1,128)}, /*index=5*/s32[16]{0:T(128)}...) while((s32[]{:T(128)}, f32[12,256]{1,0:T(8,128)S(1)}, ...), condition=%wide.region_12.13_spmd.clone, body=%wide.region_7.12_spmd.clone.sunk | while | flops 212882432 | bytes 14959176 | solution.py:89
  530.3 266.3 %while.57 = (s32[]{:T(128)}, f32[256,12,64]{0,2,1:T(8,128)}, f32[12,256]{1,0:T(8,128)}, bf16[16,512,12,64]{1,3,2,0:T(8,128)(2,1)}, s32[256]{0:T(256)}, /*index=5...) while((s32[]{:T(128)}, f32[256,12,64]{0,2,1:T(8,128)}, ...), condition=%wide.region_17.18_spmd.clone, body=%wide.region_13.17_spmd.clone.sunk | while | flops 619062272 | bytes 51501380 | solution.py:89
  804.7 1612.2 %while.55 = (s32[]{:T(128)}, f32[256,12,64]{0,2,1:T(8,128)}, bf16[256,12,64]{0,2,1:T(8,128)(2,1)}, bf16[256,12,64]{0,2,1:T(8,128)(2,1)}, f32[256,12,64]{0,2,1:T(...) while((s32[]{:T(128)}, f32[256,12,64]{0,2,1:T(8,128)}, ...), condition=%wide.region_21.22_spmd.clone, body=%wide.region_18.21_spmd.clone.sunk | while | flops 512035840 | bytes 42368940 | solution.py:302
  847.5 14.4 collective-permute-done.3
  906.7 14.4 collective-permute-done.3
  927.6 9.6 collective-permute-done
  964.9 14.4 collective-permute-done.3
  984.8 10.1 collective-permute-done
  1022.2 14.4 collective-permute-done.3
  1042.1 10.1 collective-permute-done
  1078.6 14.4 collective-permute-done.3
  1098.5 10.1 collective-permute-done
  1134.1 14.4 collective-permute-done.3
  1154.0 10.1 collective-permute-done
  1188.7 14.4 collective-permute-done.3
  1208.5 10.1 collective-permute-done
  1242.3 14.4 collective-permute-done.3
  1262.1 10.1 collective-permute-done
  1295.0 14.4 collective-permute-done.3
  1314.8 10.1 collective-permute-done
  1346.8 14.4 collective-permute-done.3
  1366.6 10.1 collective-permute-done
  1397.6 14.4 collective-permute-done.3
  1417.5 10.1 collective-permute-done
  1447.5 14.4 collective-permute-done.3
  1467.4 10.7 collective-permute-done
  1497.3 14.4 collective-permute-done.3
  1517.1 11.6 collective-permute-done
  1547.0 14.4 collective-permute-done.3
  1566.8 12.4 collective-permute-done
  1596.6 14.4 collective-permute-done.3
  1616.5 13.3 collective-permute-done
  1646.4 14.4 collective-permute-done.3
  1666.2 14.2 collective-permute-done
  1696.1 14.4 collective-permute-done.3
  1715.9 14.6 collective-permute-done
  1746.0 14.2 collective-permute-done.3
  1765.6 14.6 collective-permute-done
  1796.5 13.4 collective-permute-done.3
  1815.3 14.6 collective-permute-done
  1847.1 12.5 collective-permute-done.3
  1865.0 14.6 collective-permute-done
  1897.6 11.7 collective-permute-done.3
  1914.7 14.6 collective-permute-done
  1948.2 10.8 collective-permute-done.3
  1964.4 14.6 collective-permute-done
  1998.8 10.0 collective-permute-done.3
  2014.1 14.6 collective-permute-done
  2063.9 14.6 collective-permute-done
  2113.6 14.6 collective-permute-done
  2163.3 14.6 collective-permute-done
  2213.0 14.6 collective-permute-done
  2263.0 14.6 collective-permute-done
  2314.1 14.6 collective-permute-done
  2366.3 14.6 collective-permute-done
  2426.9 15.8 collective-permute-done.4
  2472.9 93.6 %all-reduce.6 = (f32[768]{0:T(1024)}, f32[768]{0:T(1024)}, f32[768]{0:T(1024)}, f32[768]{0:T(1024)}, f32[2304]{0:T(1024)}, /*index=5*/f32[768]{0:T(1024)S(1)}, f32[3072]{0:T(1024)}, f32[]{:T(128)}, f32[]{:T(128)}, f32[]{:T(128)}) all-reduce(f32[768]{0:T(1024)} %get-tuple-element.956, ...), channel_id=1, replica_groups=mesh['dp'=4,'blk'=32] {'dp','blk'}, use_global_device_ids=true, to_apply=%region_27.28 | all-reduce | flops 9219 | bytes 73752 | tf_op jit(solution)/shard_map/psum | solution.py:326
  2568.6 151.3 %all-reduce.10.cloned.1.call-done = (f32[768,2304]{1,0:T(8,128)}, f32[768,768]{1,0:T(8,128)}, f32[768,3072]{1,0:T(8,128)}, f32[3072,768]{1,0:T(8,128)}) async-done(((f32[768,2304]{1,0:T(8,128)}, f32[768,768]{1,0:T(8,128)}, f32[768,3072]{1,0:T(8,128)}, f32[3072,768]{1,0:T(8,128)}), (f32[768,2304]{1,0:T(8,128)}, f32[768,768]{1,0:T(8,128)}, f32[768,3072]{1,0:T(8,128)}, ...) | async-done | bytes 28311568 | tf_op jit(solution)/shard_map/psum | solution.py:326
  2728.5 9.3 copy.118
  (1889 shorter events, 1527.1 us)
Async XLA Ops:
  7.2 137.5 %all-gather.3.cloned.1.call-start = ((), (), s32[]{:S(2)}) async-start(), calls=%async_computation | async-start | bytes 12976128 | tf_op jit(solution)/shard_map/all_gather | solution.py:209
  19.0 251.5 %all-gather.5.cloned.1.call-start = ((), (), s32[]{:S(2)}) async-start(), calls=%async_computation.1 | async-start | bytes 12976128 | tf_op jit(solution)/shard_map/all_gather | solution.py:208
  33.3 2686.6 %all-reduce.10.cloned.1.call-start = ((), (), s32[]{:S(2)}) async-start(), calls=%async_computation.2 | async-start | bytes 56623104 | tf_op jit(solution)/shard_map/psum | solution.py:326
  808.7 36.4 %collective-permute-start.2 = (f32[256,12,64]{0,2,1:T(8,128)}, f32[256,12,64]{0,2,1:T(8,128)}, u32[]{:S(2)}, u32[]{:S(2)}) collective-permute-start(f32[256,12,64]{0,2,1:T(8,128)} %get-tuple-element.1427), channel_id=1, source_target_pairs={{31,0},{0,1},{1,2},{2,3},{3,4},{4,5},{5,6},{6,7},{7,8},{8,9},{9,10... | collective-permute-start | bytes 2359304 | tf_op jit(solution)/shard_map/while/body/eval_jaxpr/ppermute | solution.py:20
  809.0 52.9 %collective-permute-start.3 = (f32[256,12,64]{0,2,1:T(8,128)}, f32[256,12,64]{0,2,1:T(8,128)}, u32[]{:S(2)}, u32[]{:S(2)}) collective-permute-start(f32[256,12,64]{0,2,1:T(8,128)} %get-tuple-element.1428), channel_id=1, source_target_pairs={{31,0},{0,1},{1,2},{2,3},{3,4},{4,5},{5,6},{6,7},{7,8},{8,9},{9,10... | collective-permute-start | bytes 2359304 | tf_op jit(solution)/shard_map/while/body/eval_jaxpr/ppermute | solution.py:20
  865.5 38.8 %collective-permute-start.2 = (f32[256,12,64]{0,2,1:T(8,128)}, f32[256,12,64]{0,2,1:T(8,128)}, u32[]{:S(2)}, u32[]{:S(2)}) collective-permute-start(f32[256,12,64]{0,2,1:T(8,128)} %get-tuple-element.1427), channel_id=1, source_target_pairs={{31,0},{0,1},{1,2},{2,3},{3,4},{4,5},{5,6},{6,7},{7,8},{8,9},{9,10... | collective-permute-start | bytes 2359304 | tf_op jit(solution)/shard_map/while/body/eval_jaxpr/ppermute | solution.py:20
  865.5 55.6 %collective-permute-start.3 = (f32[256,12,64]{0,2,1:T(8,128)}, f32[256,12,64]{0,2,1:T(8,128)}, u32[]{:S(2)}, u32[]{:S(2)}) collective-permute-start(f32[256,12,64]{0,2,1:T(8,128)} %get-tuple-element.1428), channel_id=1, source_target_pairs={{31,0},{0,1},{1,2},{2,3},{3,4},{4,5},{5,6},{6,7},{7,8},{8,9},{9,10... | collective-permute-start | bytes 2359304 | tf_op jit(solution)/shard_map/while/body/eval_jaxpr/ppermute | solution.py:20
  924.0 38.5 %collective-permute-start.2 = (f32[256,12,64]{0,2,1:T(8,128)}, f32[256,12,64]{0,2,1:T(8,128)}, u32[]{:S(2)}, u32[]{:S(2)}) collective-permute-start(f32[256,12,64]{0,2,1:T(8,128)} %get-tuple-element.1427), channel_id=1, source_target_pairs={{31,0},{0,1},{1,2},{2,3},{3,4},{4,5},{5,6},{6,7},{7,8},{8,9},{9,10... | collective-permute-start | bytes 2359304 | tf_op jit(solution)/shard_map/while/body/eval_jaxpr/ppermute | solution.py:20
  924.1 55.3 %collective-permute-start.3 = (f32[256,12,64]{0,2,1:T(8,128)}, f32[256,12,64]{0,2,1:T(8,128)}, u32[]{:S(2)}, u32[]{:S(2)}) collective-permute-start(f32[256,12,64]{0,2,1:T(8,128)} %get-tuple-element.1428), channel_id=1, source_target_pairs={{31,0},{0,1},{1,2},{2,3},{3,4},{4,5},{5,6},{6,7},{7,8},{8,9},{9,10... | collective-permute-start | bytes 2359304 | tf_op jit(solution)/shard_map/while/body/eval_jaxpr/ppermute | solution.py:20
  982.2 37.6 %collective-permute-start.2 = (f32[256,12,64]{0,2,1:T(8,128)}, f32[256,12,64]{0,2,1:T(8,128)}, u32[]{:S(2)}, u32[]{:S(2)}) collective-permute-start(f32[256,12,64]{0,2,1:T(8,128)} %get-tuple-element.1427), channel_id=1, source_target_pairs={{31,0},{0,1},{1,2},{2,3},{3,4},{4,5},{5,6},{6,7},{7,8},{8,9},{9,10... | collective-permute-start | bytes 2359304 | tf_op jit(solution)/shard_map/while/body/eval_jaxpr/ppermute | solution.py:20
  982.3 54.4 %collective-permute-start.3 = (f32[256,12,64]{0,2,1:T(8,128)}, f32[256,12,64]{0,2,1:T(8,128)}, u32[]{:S(2)}, u32[]{:S(2)}) collective-permute-start(f32[256,12,64]{0,2,1:T(8,128)} %get-tuple-element.1428), channel_id=1, source_target_pairs={{31,0},{0,1},{1,2},{2,3},{3,4},{4,5},{5,6},{6,7},{7,8},{8,9},{9,10... | collective-permute-start | bytes 2359304 | tf_op jit(solution)/shard_map/while/body/eval_jaxpr/ppermute | solution.py:20
  1039.5 36.7 %collective-permute-start.2 = (f32[256,12,64]{0,2,1:T(8,128)}, f32[256,12,64]{0,2,1:T(8,128)}, u32[]{:S(2)}, u32[]{:S(2)}) collective-permute-start(f32[256,12,64]{0,2,1:T(8,128)} %get-tuple-element.1427), channel_id=1, source_target_pairs={{31,0},{0,1},{1,2},{2,3},{3,4},{4,5},{5,6},{6,7},{7,8},{8,9},{9,10... | collective-permute-start | bytes 2359304 | tf_op jit(solution)/shard_map/while/body/eval_jaxpr/ppermute | solution.py:20
  1039.6 53.5 %collective-permute-start.3 = (f32[256,12,64]{0,2,1:T(8,128)}, f32[256,12,64]{0,2,1:T(8,128)}, u32[]{:S(2)}, u32[]{:S(2)}) collective-permute-start(f32[256,12,64]{0,2,1:T(8,128)} %get-tuple-element.1428), channel_id=1, source_target_pairs={{31,0},{0,1},{1,2},{2,3},{3,4},{4,5},{5,6},{6,7},{7,8},{8,9},{9,10... | collective-permute-start | bytes 2359304 | tf_op jit(solution)/shard_map/while/body/eval_jaxpr/ppermute | solution.py:20
  1095.9 35.8 %collective-permute-start.2 = (f32[256,12,64]{0,2,1:T(8,128)}, f32[256,12,64]{0,2,1:T(8,128)}, u32[]{:S(2)}, u32[]{:S(2)}) collective-permute-start(f32[256,12,64]{0,2,1:T(8,128)} %get-tuple-element.1427), channel_id=1, source_target_pairs={{31,0},{0,1},{1,2},{2,3},{3,4},{4,5},{5,6},{6,7},{7,8},{8,9},{9,10... | collective-permute-start | bytes 2359304 | tf_op jit(solution)/shard_map/while/body/eval_jaxpr/ppermute | solution.py:20
  1096.0 52.5 %collective-permute-start.3 = (f32[256,12,64]{0,2,1:T(8,128)}, f32[256,12,64]{0,2,1:T(8,128)}, u32[]{:S(2)}, u32[]{:S(2)}) collective-permute-start(f32[256,12,64]{0,2,1:T(8,128)} %get-tuple-element.1428), channel_id=1, source_target_pairs={{31,0},{0,1},{1,2},{2,3},{3,4},{4,5},{5,6},{6,7},{7,8},{8,9},{9,10... | collective-permute-start | bytes 2359304 | tf_op jit(solution)/shard_map/while/body/eval_jaxpr/ppermute | solution.py:20
  1151.4 34.8 %collective-permute-start.2 = (f32[256,12,64]{0,2,1:T(8,128)}, f32[256,12,64]{0,2,1:T(8,128)}, u32[]{:S(2)}, u32[]{:S(2)}) collective-permute-start(f32[256,12,64]{0,2,1:T(8,128)} %get-tuple-element.1427), channel_id=1, source_target_pairs={{31,0},{0,1},{1,2},{2,3},{3,4},{4,5},{5,6},{6,7},{7,8},{8,9},{9,10... | collective-permute-start | bytes 2359304 | tf_op jit(solution)/shard_map/while/body/eval_jaxpr/ppermute | solution.py:20
  1151.5 51.6 %collective-permute-start.3 = (f32[256,12,64]{0,2,1:T(8,128)}, f32[256,12,64]{0,2,1:T(8,128)}, u32[]{:S(2)}, u32[]{:S(2)}) collective-permute-start(f32[256,12,64]{0,2,1:T(8,128)} %get-tuple-element.1428), channel_id=1, source_target_pairs={{31,0},{0,1},{1,2},{2,3},{3,4},{4,5},{5,6},{6,7},{7,8},{8,9},{9,10... | collective-permute-start | bytes 2359304 | tf_op jit(solution)/shard_map/while/body/eval_jaxpr/ppermute | solution.py:20
  1205.9 33.9 %collective-permute-start.2 = (f32[256,12,64]{0,2,1:T(8,128)}, f32[256,12,64]{0,2,1:T(8,128)}, u32[]{:S(2)}, u32[]{:S(2)}) collective-permute-start(f32[256,12,64]{0,2,1:T(8,128)} %get-tuple-element.1427), channel_id=1, source_target_pairs={{31,0},{0,1},{1,2},{2,3},{3,4},{4,5},{5,6},{6,7},{7,8},{8,9},{9,10... | collective-permute-start | bytes 2359304 | tf_op jit(solution)/shard_map/while/body/eval_jaxpr/ppermute | solution.py:20
  1206.0 50.7 %collective-permute-start.3 = (f32[256,12,64]{0,2,1:T(8,128)}, f32[256,12,64]{0,2,1:T(8,128)}, u32[]{:S(2)}, u32[]{:S(2)}) collective-permute-start(f32[256,12,64]{0,2,1:T(8,128)} %get-tuple-element.1428), channel_id=1, source_target_pairs={{31,0},{0,1},{1,2},{2,3},{3,4},{4,5},{5,6},{6,7},{7,8},{8,9},{9,10... | collective-permute-start | bytes 2359304 | tf_op jit(solution)/shard_map/while/body/eval_jaxpr/ppermute | solution.py:20
  1259.6 33.0 %collective-permute-start.2 = (f32[256,12,64]{0,2,1:T(8,128)}, f32[256,12,64]{0,2,1:T(8,128)}, u32[]{:S(2)}, u32[]{:S(2)}) collective-permute-start(f32[256,12,64]{0,2,1:T(8,128)} %get-tuple-element.1427), channel_id=1, source_target_pairs={{31,0},{0,1},{1,2},{2,3},{3,4},{4,5},{5,6},{6,7},{7,8},{8,9},{9,10... | collective-permute-start | bytes 2359304 | tf_op jit(solution)/shard_map/while/body/eval_jaxpr/ppermute | solution.py:20
  1259.6 49.8 %collective-permute-start.3 = (f32[256,12,64]{0,2,1:T(8,128)}, f32[256,12,64]{0,2,1:T(8,128)}, u32[]{:S(2)}, u32[]{:S(2)}) collective-permute-start(f32[256,12,64]{0,2,1:T(8,128)} %get-tuple-element.1428), channel_id=1, source_target_pairs={{31,0},{0,1},{1,2},{2,3},{3,4},{4,5},{5,6},{6,7},{7,8},{8,9},{9,10... | collective-permute-start | bytes 2359304 | tf_op jit(solution)/shard_map/while/body/eval_jaxpr/ppermute | solution.py:20
  1312.3 32.1 %collective-permute-start.2 = (f32[256,12,64]{0,2,1:T(8,128)}, f32[256,12,64]{0,2,1:T(8,128)}, u32[]{:S(2)}, u32[]{:S(2)}) collective-permute-start(f32[256,12,64]{0,2,1:T(8,128)} %get-tuple-element.1427), channel_id=1, source_target_pairs={{31,0},{0,1},{1,2},{2,3},{3,4},{4,5},{5,6},{6,7},{7,8},{8,9},{9,10... | collective-permute-start | bytes 2359304 | tf_op jit(solution)/shard_map/while/body/eval_jaxpr/ppermute | solution.py:20
  1312.3 48.8 %collective-permute-start.3 = (f32[256,12,64]{0,2,1:T(8,128)}, f32[256,12,64]{0,2,1:T(8,128)}, u32[]{:S(2)}, u32[]{:S(2)}) collective-permute-start(f32[256,12,64]{0,2,1:T(8,128)} %get-tuple-element.1428), channel_id=1, source_target_pairs={{31,0},{0,1},{1,2},{2,3},{3,4},{4,5},{5,6},{6,7},{7,8},{8,9},{9,10... | collective-permute-start | bytes 2359304 | tf_op jit(solution)/shard_map/while/body/eval_jaxpr/ppermute | solution.py:20
  1364.0 31.2 %collective-permute-start.2 = (f32[256,12,64]{0,2,1:T(8,128)}, f32[256,12,64]{0,2,1:T(8,128)}, u32[]{:S(2)}, u32[]{:S(2)}) collective-permute-start(f32[256,12,64]{0,2,1:T(8,128)} %get-tuple-element.1427), channel_id=1, source_target_pairs={{31,0},{0,1},{1,2},{2,3},{3,4},{4,5},{5,6},{6,7},{7,8},{8,9},{9,10... | collective-permute-start | bytes 2359304 | tf_op jit(solution)/shard_map/while/body/eval_jaxpr/ppermute | solution.py:20
  1364.1 47.9 %collective-permute-start.3 = (f32[256,12,64]{0,2,1:T(8,128)}, f32[256,12,64]{0,2,1:T(8,128)}, u32[]{:S(2)}, u32[]{:S(2)}) collective-permute-start(f32[256,12,64]{0,2,1:T(8,128)} %get-tuple-element.1428), channel_id=1, source_target_pairs={{31,0},{0,1},{1,2},{2,3},{3,4},{4,5},{5,6},{6,7},{7,8},{8,9},{9,10... | collective-permute-start | bytes 2359304 | tf_op jit(solution)/shard_map/while/body/eval_jaxpr/ppermute | solution.py:20
  1414.9 30.2 %collective-permute-start.2 = (f32[256,12,64]{0,2,1:T(8,128)}, f32[256,12,64]{0,2,1:T(8,128)}, u32[]{:S(2)}, u32[]{:S(2)}) collective-permute-start(f32[256,12,64]{0,2,1:T(8,128)} %get-tuple-element.1427), channel_id=1, source_target_pairs={{31,0},{0,1},{1,2},{2,3},{3,4},{4,5},{5,6},{6,7},{7,8},{8,9},{9,10... | collective-permute-start | bytes 2359304 | tf_op jit(solution)/shard_map/while/body/eval_jaxpr/ppermute | solution.py:20
  1415.0 47.0 %collective-permute-start.3 = (f32[256,12,64]{0,2,1:T(8,128)}, f32[256,12,64]{0,2,1:T(8,128)}, u32[]{:S(2)}, u32[]{:S(2)}) collective-permute-start(f32[256,12,64]{0,2,1:T(8,128)} %get-tuple-element.1428), channel_id=1, source_target_pairs={{31,0},{0,1},{1,2},{2,3},{3,4},{4,5},{5,6},{6,7},{7,8},{8,9},{9,10... | collective-permute-start | bytes 2359304 | tf_op jit(solution)/shard_map/while/body/eval_jaxpr/ppermute | solution.py:20
  1464.8 30.0 %collective-permute-start.2 = (f32[256,12,64]{0,2,1:T(8,128)}, f32[256,12,64]{0,2,1:T(8,128)}, u32[]{:S(2)}, u32[]{:S(2)}) collective-permute-start(f32[256,12,64]{0,2,1:T(8,128)} %get-tuple-element.1427), channel_id=1, source_target_pairs={{31,0},{0,1},{1,2},{2,3},{3,4},{4,5},{5,6},{6,7},{7,8},{8,9},{9,10... | collective-permute-start | bytes 2359304 | tf_op jit(solution)/shard_map/while/body/eval_jaxpr/ppermute | solution.py:20
  1464.9 46.8 %collective-permute-start.3 = (f32[256,12,64]{0,2,1:T(8,128)}, f32[256,12,64]{0,2,1:T(8,128)}, u32[]{:S(2)}, u32[]{:S(2)}) collective-permute-start(f32[256,12,64]{0,2,1:T(8,128)} %get-tuple-element.1428), channel_id=1, source_target_pairs={{31,0},{0,1},{1,2},{2,3},{3,4},{4,5},{5,6},{6,7},{7,8},{8,9},{9,10... | collective-permute-start | bytes 2359304 | tf_op jit(solution)/shard_map/while/body/eval_jaxpr/ppermute | solution.py:20
  1514.5 30.0 %collective-permute-start.2 = (f32[256,12,64]{0,2,1:T(8,128)}, f32[256,12,64]{0,2,1:T(8,128)}, u32[]{:S(2)}, u32[]{:S(2)}) collective-permute-start(f32[256,12,64]{0,2,1:T(8,128)} %get-tuple-element.1427), channel_id=1, source_target_pairs={{31,0},{0,1},{1,2},{2,3},{3,4},{4,5},{5,6},{6,7},{7,8},{8,9},{9,10... | collective-permute-start | bytes 2359304 | tf_op jit(solution)/shard_map/while/body/eval_jaxpr/ppermute | solution.py:20
  1514.6 46.8 %collective-permute-start.3 = (f32[256,12,64]{0,2,1:T(8,128)}, f32[256,12,64]{0,2,1:T(8,128)}, u32[]{:S(2)}, u32[]{:S(2)}) collective-permute-start(f32[256,12,64]{0,2,1:T(8,128)} %get-tuple-element.1428), channel_id=1, source_target_pairs={{31,0},{0,1},{1,2},{2,3},{3,4},{4,5},{5,6},{6,7},{7,8},{8,9},{9,10... | collective-permute-start | bytes 2359304 | tf_op jit(solution)/shard_map/while/body/eval_jaxpr/ppermute | solution.py:20
  1564.2 30.0 %collective-permute-start.2 = (f32[256,12,64]{0,2,1:T(8,128)}, f32[256,12,64]{0,2,1:T(8,128)}, u32[]{:S(2)}, u32[]{:S(2)}) collective-permute-start(f32[256,12,64]{0,2,1:T(8,128)} %get-tuple-element.1427), channel_id=1, source_target_pairs={{31,0},{0,1},{1,2},{2,3},{3,4},{4,5},{5,6},{6,7},{7,8},{8,9},{9,10... | collective-permute-start | bytes 2359304 | tf_op jit(solution)/shard_map/while/body/eval_jaxpr/ppermute | solution.py:20
  1564.3 46.8 %collective-permute-start.3 = (f32[256,12,64]{0,2,1:T(8,128)}, f32[256,12,64]{0,2,1:T(8,128)}, u32[]{:S(2)}, u32[]{:S(2)}) collective-permute-start(f32[256,12,64]{0,2,1:T(8,128)} %get-tuple-element.1428), channel_id=1, source_target_pairs={{31,0},{0,1},{1,2},{2,3},{3,4},{4,5},{5,6},{6,7},{7,8},{8,9},{9,10... | collective-permute-start | bytes 2359304 | tf_op jit(solution)/shard_map/while/body/eval_jaxpr/ppermute | solution.py:20
  1613.9 30.0 %collective-permute-start.2 = (f32[256,12,64]{0,2,1:T(8,128)}, f32[256,12,64]{0,2,1:T(8,128)}, u32[]{:S(2)}, u32[]{:S(2)}) collective-permute-start(f32[256,12,64]{0,2,1:T(8,128)} %get-tuple-element.1427), channel_id=1, source_target_pairs={{31,0},{0,1},{1,2},{2,3},{3,4},{4,5},{5,6},{6,7},{7,8},{8,9},{9,10... | collective-permute-start | bytes 2359304 | tf_op jit(solution)/shard_map/while/body/eval_jaxpr/ppermute | solution.py:20
  1614.0 46.8 %collective-permute-start.3 = (f32[256,12,64]{0,2,1:T(8,128)}, f32[256,12,64]{0,2,1:T(8,128)}, u32[]{:S(2)}, u32[]{:S(2)}) collective-permute-start(f32[256,12,64]{0,2,1:T(8,128)} %get-tuple-element.1428), channel_id=1, source_target_pairs={{31,0},{0,1},{1,2},{2,3},{3,4},{4,5},{5,6},{6,7},{7,8},{8,9},{9,10... | collective-permute-start | bytes 2359304 | tf_op jit(solution)/shard_map/while/body/eval_jaxpr/ppermute | solution.py:20
  1663.7 46.8 %collective-permute-start.3 = (f32[256,12,64]{0,2,1:T(8,128)}, f32[256,12,64]{0,2,1:T(8,128)}, u32[]{:S(2)}, u32[]{:S(2)}) collective-permute-start(f32[256,12,64]{0,2,1:T(8,128)} %get-tuple-element.1428), channel_id=1, source_target_pairs={{31,0},{0,1},{1,2},{2,3},{3,4},{4,5},{5,6},{6,7},{7,8},{8,9},{9,10... | collective-permute-start | bytes 2359304 | tf_op jit(solution)/shard_map/while/body/eval_jaxpr/ppermute | solution.py:20
  1713.4 30.2 %collective-permute-start.2 = (f32[256,12,64]{0,2,1:T(8,128)}, f32[256,12,64]{0,2,1:T(8,128)}, u32[]{:S(2)}, u32[]{:S(2)}) collective-permute-start(f32[256,12,64]{0,2,1:T(8,128)} %get-tuple-element.1427), channel_id=1, source_target_pairs={{31,0},{0,1},{1,2},{2,3},{3,4},{4,5},{5,6},{6,7},{7,8},{8,9},{9,10... | collective-permute-start | bytes 2359304 | tf_op jit(solution)/shard_map/while/body/eval_jaxpr/ppermute | solution.py:20
  1713.4 46.8 %collective-permute-start.3 = (f32[256,12,64]{0,2,1:T(8,128)}, f32[256,12,64]{0,2,1:T(8,128)}, u32[]{:S(2)}, u32[]{:S(2)}) collective-permute-start(f32[256,12,64]{0,2,1:T(8,128)} %get-tuple-element.1428), channel_id=1, source_target_pairs={{31,0},{0,1},{1,2},{2,3},{3,4},{4,5},{5,6},{6,7},{7,8},{8,9},{9,10... | collective-permute-start | bytes 2359304 | tf_op jit(solution)/shard_map/while/body/eval_jaxpr/ppermute | solution.py:20
  1763.1 31.1 %collective-permute-start.2 = (f32[256,12,64]{0,2,1:T(8,128)}, f32[256,12,64]{0,2,1:T(8,128)}, u32[]{:S(2)}, u32[]{:S(2)}) collective-permute-start(f32[256,12,64]{0,2,1:T(8,128)} %get-tuple-element.1427), channel_id=1, source_target_pairs={{31,0},{0,1},{1,2},{2,3},{3,4},{4,5},{5,6},{6,7},{7,8},{8,9},{9,10... | collective-permute-start | bytes 2359304 | tf_op jit(solution)/shard_map/while/body/eval_jaxpr/ppermute | solution.py:20
  1763.1 46.8 %collective-permute-start.3 = (f32[256,12,64]{0,2,1:T(8,128)}, f32[256,12,64]{0,2,1:T(8,128)}, u32[]{:S(2)}, u32[]{:S(2)}) collective-permute-start(f32[256,12,64]{0,2,1:T(8,128)} %get-tuple-element.1428), channel_id=1, source_target_pairs={{31,0},{0,1},{1,2},{2,3},{3,4},{4,5},{5,6},{6,7},{7,8},{8,9},{9,10... | collective-permute-start | bytes 2359304 | tf_op jit(solution)/shard_map/while/body/eval_jaxpr/ppermute | solution.py:20
  1812.8 31.9 %collective-permute-start.2 = (f32[256,12,64]{0,2,1:T(8,128)}, f32[256,12,64]{0,2,1:T(8,128)}, u32[]{:S(2)}, u32[]{:S(2)}) collective-permute-start(f32[256,12,64]{0,2,1:T(8,128)} %get-tuple-element.1427), channel_id=1, source_target_pairs={{31,0},{0,1},{1,2},{2,3},{3,4},{4,5},{5,6},{6,7},{7,8},{8,9},{9,10... | collective-permute-start | bytes 2359304 | tf_op jit(solution)/shard_map/while/body/eval_jaxpr/ppermute | solution.py:20
  1812.8 46.8 %collective-permute-start.3 = (f32[256,12,64]{0,2,1:T(8,128)}, f32[256,12,64]{0,2,1:T(8,128)}, u32[]{:S(2)}, u32[]{:S(2)}) collective-permute-start(f32[256,12,64]{0,2,1:T(8,128)} %get-tuple-element.1428), channel_id=1, source_target_pairs={{31,0},{0,1},{1,2},{2,3},{3,4},{4,5},{5,6},{6,7},{7,8},{8,9},{9,10... | collective-permute-start | bytes 2359304 | tf_op jit(solution)/shard_map/while/body/eval_jaxpr/ppermute | solution.py:20
  1862.5 32.8 %collective-permute-start.2 = (f32[256,12,64]{0,2,1:T(8,128)}, f32[256,12,64]{0,2,1:T(8,128)}, u32[]{:S(2)}, u32[]{:S(2)}) collective-permute-start(f32[256,12,64]{0,2,1:T(8,128)} %get-tuple-element.1427), channel_id=1, source_target_pairs={{31,0},{0,1},{1,2},{2,3},{3,4},{4,5},{5,6},{6,7},{7,8},{8,9},{9,10... | collective-permute-start | bytes 2359304 | tf_op jit(solution)/shard_map/while/body/eval_jaxpr/ppermute | solution.py:20
  1862.5 46.8 %collective-permute-start.3 = (f32[256,12,64]{0,2,1:T(8,128)}, f32[256,12,64]{0,2,1:T(8,128)}, u32[]{:S(2)}, u32[]{:S(2)}) collective-permute-start(f32[256,12,64]{0,2,1:T(8,128)} %get-tuple-element.1428), channel_id=1, source_target_pairs={{31,0},{0,1},{1,2},{2,3},{3,4},{4,5},{5,6},{6,7},{7,8},{8,9},{9,10... | collective-permute-start | bytes 2359304 | tf_op jit(solution)/shard_map/while/body/eval_jaxpr/ppermute | solution.py:20
  1912.2 33.6 %collective-permute-start.2 = (f32[256,12,64]{0,2,1:T(8,128)}, f32[256,12,64]{0,2,1:T(8,128)}, u32[]{:S(2)}, u32[]{:S(2)}) collective-permute-start(f32[256,12,64]{0,2,1:T(8,128)} %get-tuple-element.1427), channel_id=1, source_target_pairs={{31,0},{0,1},{1,2},{2,3},{3,4},{4,5},{5,6},{6,7},{7,8},{8,9},{9,10... | collective-permute-start | bytes 2359304 | tf_op jit(solution)/shard_map/while/body/eval_jaxpr/ppermute | solution.py:20
  1912.2 46.8 %collective-permute-start.3 = (f32[256,12,64]{0,2,1:T(8,128)}, f32[256,12,64]{0,2,1:T(8,128)}, u32[]{:S(2)}, u32[]{:S(2)}) collective-permute-start(f32[256,12,64]{0,2,1:T(8,128)} %get-tuple-element.1428), channel_id=1, source_target_pairs={{31,0},{0,1},{1,2},{2,3},{3,4},{4,5},{5,6},{6,7},{7,8},{8,9},{9,10... | collective-permute-start | bytes 2359304 | tf_op jit(solution)/shard_map/while/body/eval_jaxpr/ppermute | solution.py:20
  1961.9 34.5 %collective-permute-start.2 = (f32[256,12,64]{0,2,1:T(8,128)}, f32[256,12,64]{0,2,1:T(8,128)}, u32[]{:S(2)}, u32[]{:S(2)}) collective-permute-start(f32[256,12,64]{0,2,1:T(8,128)} %get-tuple-element.1427), channel_id=1, source_target_pairs={{31,0},{0,1},{1,2},{2,3},{3,4},{4,5},{5,6},{6,7},{7,8},{8,9},{9,10... | collective-permute-start | bytes 2359304 | tf_op jit(solution)/shard_map/while/body/eval_jaxpr/ppermute | solution.py:20
  1962.0 46.8 %collective-permute-start.3 = (f32[256,12,64]{0,2,1:T(8,128)}, f32[256,12,64]{0,2,1:T(8,128)}, u32[]{:S(2)}, u32[]{:S(2)}) collective-permute-start(f32[256,12,64]{0,2,1:T(8,128)} %get-tuple-element.1428), channel_id=1, source_target_pairs={{31,0},{0,1},{1,2},{2,3},{3,4},{4,5},{5,6},{6,7},{7,8},{8,9},{9,10... | collective-permute-start | bytes 2359304 | tf_op jit(solution)/shard_map/while/body/eval_jaxpr/ppermute | solution.py:20
  2011.6 35.3 %collective-permute-start.2 = (f32[256,12,64]{0,2,1:T(8,128)}, f32[256,12,64]{0,2,1:T(8,128)}, u32[]{:S(2)}, u32[]{:S(2)}) collective-permute-start(f32[256,12,64]{0,2,1:T(8,128)} %get-tuple-element.1427), channel_id=1, source_target_pairs={{31,0},{0,1},{1,2},{2,3},{3,4},{4,5},{5,6},{6,7},{7,8},{8,9},{9,10... | collective-permute-start | bytes 2359304 | tf_op jit(solution)/shard_map/while/body/eval_jaxpr/ppermute | solution.py:20
  2011.7 46.8 %collective-permute-start.3 = (f32[256,12,64]{0,2,1:T(8,128)}, f32[256,12,64]{0,2,1:T(8,128)}, u32[]{:S(2)}, u32[]{:S(2)}) collective-permute-start(f32[256,12,64]{0,2,1:T(8,128)} %get-tuple-element.1428), channel_id=1, source_target_pairs={{31,0},{0,1},{1,2},{2,3},{3,4},{4,5},{5,6},{6,7},{7,8},{8,9},{9,10... | collective-permute-start | bytes 2359304 | tf_op jit(solution)/shard_map/while/body/eval_jaxpr/ppermute | solution.py:20
  2061.3 36.2 %collective-permute-start.2 = (f32[256,12,64]{0,2,1:T(8,128)}, f32[256,12,64]{0,2,1:T(8,128)}, u32[]{:S(2)}, u32[]{:S(2)}) collective-permute-start(f32[256,12,64]{0,2,1:T(8,128)} %get-tuple-element.1427), channel_id=1, source_target_pairs={{31,0},{0,1},{1,2},{2,3},{3,4},{4,5},{5,6},{6,7},{7,8},{8,9},{9,10... | collective-permute-start | bytes 2359304 | tf_op jit(solution)/shard_map/while/body/eval_jaxpr/ppermute | solution.py:20
  2061.4 46.8 %collective-permute-start.3 = (f32[256,12,64]{0,2,1:T(8,128)}, f32[256,12,64]{0,2,1:T(8,128)}, u32[]{:S(2)}, u32[]{:S(2)}) collective-permute-start(f32[256,12,64]{0,2,1:T(8,128)} %get-tuple-element.1428), channel_id=1, source_target_pairs={{31,0},{0,1},{1,2},{2,3},{3,4},{4,5},{5,6},{6,7},{7,8},{8,9},{9,10... | collective-permute-start | bytes 2359304 | tf_op jit(solution)/shard_map/while/body/eval_jaxpr/ppermute | solution.py:20
  2111.0 37.0 %collective-permute-start.2 = (f32[256,12,64]{0,2,1:T(8,128)}, f32[256,12,64]{0,2,1:T(8,128)}, u32[]{:S(2)}, u32[]{:S(2)}) collective-permute-start(f32[256,12,64]{0,2,1:T(8,128)} %get-tuple-element.1427), channel_id=1, source_target_pairs={{31,0},{0,1},{1,2},{2,3},{3,4},{4,5},{5,6},{6,7},{7,8},{8,9},{9,10... | collective-permute-start | bytes 2359304 | tf_op jit(solution)/shard_map/while/body/eval_jaxpr/ppermute | solution.py:20
  2111.1 46.8 %collective-permute-start.3 = (f32[256,12,64]{0,2,1:T(8,128)}, f32[256,12,64]{0,2,1:T(8,128)}, u32[]{:S(2)}, u32[]{:S(2)}) collective-permute-start(f32[256,12,64]{0,2,1:T(8,128)} %get-tuple-element.1428), channel_id=1, source_target_pairs={{31,0},{0,1},{1,2},{2,3},{3,4},{4,5},{5,6},{6,7},{7,8},{8,9},{9,10... | collective-permute-start | bytes 2359304 | tf_op jit(solution)/shard_map/while/body/eval_jaxpr/ppermute | solution.py:20
  2160.7 37.9 %collective-permute-start.2 = (f32[256,12,64]{0,2,1:T(8,128)}, f32[256,12,64]{0,2,1:T(8,128)}, u32[]{:S(2)}, u32[]{:S(2)}) collective-permute-start(f32[256,12,64]{0,2,1:T(8,128)} %get-tuple-element.1427), channel_id=1, source_target_pairs={{31,0},{0,1},{1,2},{2,3},{3,4},{4,5},{5,6},{6,7},{7,8},{8,9},{9,10... | collective-permute-start | bytes 2359304 | tf_op jit(solution)/shard_map/while/body/eval_jaxpr/ppermute | solution.py:20
  2160.8 46.8 %collective-permute-start.3 = (f32[256,12,64]{0,2,1:T(8,128)}, f32[256,12,64]{0,2,1:T(8,128)}, u32[]{:S(2)}, u32[]{:S(2)}) collective-permute-start(f32[256,12,64]{0,2,1:T(8,128)} %get-tuple-element.1428), channel_id=1, source_target_pairs={{31,0},{0,1},{1,2},{2,3},{3,4},{4,5},{5,6},{6,7},{7,8},{8,9},{9,10... | collective-permute-start | bytes 2359304 | tf_op jit(solution)/shard_map/while/body/eval_jaxpr/ppermute | solution.py:20
  2210.4 38.8 %collective-permute-start.2 = (f32[256,12,64]{0,2,1:T(8,128)}, f32[256,12,64]{0,2,1:T(8,128)}, u32[]{:S(2)}, u32[]{:S(2)}) collective-permute-start(f32[256,12,64]{0,2,1:T(8,128)} %get-tuple-element.1427), channel_id=1, source_target_pairs={{31,0},{0,1},{1,2},{2,3},{3,4},{4,5},{5,6},{6,7},{7,8},{8,9},{9,10... | collective-permute-start | bytes 2359304 | tf_op jit(solution)/shard_map/while/body/eval_jaxpr/ppermute | solution.py:20
  2210.5 47.1 %collective-permute-start.3 = (f32[256,12,64]{0,2,1:T(8,128)}, f32[256,12,64]{0,2,1:T(8,128)}, u32[]{:S(2)}, u32[]{:S(2)}) collective-permute-start(f32[256,12,64]{0,2,1:T(8,128)} %get-tuple-element.1428), channel_id=1, source_target_pairs={{31,0},{0,1},{1,2},{2,3},{3,4},{4,5},{5,6},{6,7},{7,8},{8,9},{9,10... | collective-permute-start | bytes 2359304 | tf_op jit(solution)/shard_map/while/body/eval_jaxpr/ppermute | solution.py:20
  2260.4 39.8 %collective-permute-start.2 = (f32[256,12,64]{0,2,1:T(8,128)}, f32[256,12,64]{0,2,1:T(8,128)}, u32[]{:S(2)}, u32[]{:S(2)}) collective-permute-start(f32[256,12,64]{0,2,1:T(8,128)} %get-tuple-element.1427), channel_id=1, source_target_pairs={{31,0},{0,1},{1,2},{2,3},{3,4},{4,5},{5,6},{6,7},{7,8},{8,9},{9,10... | collective-permute-start | bytes 2359304 | tf_op jit(solution)/shard_map/while/body/eval_jaxpr/ppermute | solution.py:20
  2260.5 48.2 %collective-permute-start.3 = (f32[256,12,64]{0,2,1:T(8,128)}, f32[256,12,64]{0,2,1:T(8,128)}, u32[]{:S(2)}, u32[]{:S(2)}) collective-permute-start(f32[256,12,64]{0,2,1:T(8,128)} %get-tuple-element.1428), channel_id=1, source_target_pairs={{31,0},{0,1},{1,2},{2,3},{3,4},{4,5},{5,6},{6,7},{7,8},{8,9},{9,10... | collective-permute-start | bytes 2359304 | tf_op jit(solution)/shard_map/while/body/eval_jaxpr/ppermute | solution.py:20
  2311.5 40.9 %collective-permute-start.2 = (f32[256,12,64]{0,2,1:T(8,128)}, f32[256,12,64]{0,2,1:T(8,128)}, u32[]{:S(2)}, u32[]{:S(2)}) collective-permute-start(f32[256,12,64]{0,2,1:T(8,128)} %get-tuple-element.1427), channel_id=1, source_target_pairs={{31,0},{0,1},{1,2},{2,3},{3,4},{4,5},{5,6},{6,7},{7,8},{8,9},{9,10... | collective-permute-start | bytes 2359304 | tf_op jit(solution)/shard_map/while/body/eval_jaxpr/ppermute | solution.py:20
  2311.6 49.3 %collective-permute-start.3 = (f32[256,12,64]{0,2,1:T(8,128)}, f32[256,12,64]{0,2,1:T(8,128)}, u32[]{:S(2)}, u32[]{:S(2)}) collective-permute-start(f32[256,12,64]{0,2,1:T(8,128)} %get-tuple-element.1428), channel_id=1, source_target_pairs={{31,0},{0,1},{1,2},{2,3},{3,4},{4,5},{5,6},{6,7},{7,8},{8,9},{9,10... | collective-permute-start | bytes 2359304 | tf_op jit(solution)/shard_map/while/body/eval_jaxpr/ppermute | solution.py:20
  2363.7 42.1 %collective-permute-start.2 = (f32[256,12,64]{0,2,1:T(8,128)}, f32[256,12,64]{0,2,1:T(8,128)}, u32[]{:S(2)}, u32[]{:S(2)}) collective-permute-start(f32[256,12,64]{0,2,1:T(8,128)} %get-tuple-element.1427), channel_id=1, source_target_pairs={{31,0},{0,1},{1,2},{2,3},{3,4},{4,5},{5,6},{6,7},{7,8},{8,9},{9,10... | collective-permute-start | bytes 2359304 | tf_op jit(solution)/shard_map/while/body/eval_jaxpr/ppermute | solution.py:20
  2363.8 50.3 %collective-permute-start.3 = (f32[256,12,64]{0,2,1:T(8,128)}, f32[256,12,64]{0,2,1:T(8,128)}, u32[]{:S(2)}, u32[]{:S(2)}) collective-permute-start(f32[256,12,64]{0,2,1:T(8,128)} %get-tuple-element.1428), channel_id=1, source_target_pairs={{31,0},{0,1},{1,2},{2,3},{3,4},{4,5},{5,6},{6,7},{7,8},{8,9},{9,10... | collective-permute-start | bytes 2359304 | tf_op jit(solution)/shard_map/while/body/eval_jaxpr/ppermute | solution.py:20
  (512 other events, 5471.1 us)
Sparse Core Ops, SparseCore 0:
  19.1 125.4 all-gather.2
  148.0 122.4 all-gather.4
  2456.3 263.5 all-reduce.9
where the time goes:
time: 2770 us; the launch traced here: 2750 us
  waiting for transfers between devices  1420 us (51%)
  matrix products  716 us (26%)
  other arithmetic  227 us (8%)
  local copies, waits for them, and re-layouts  225 us (8%)
  blocking collectives  93.6 us (3%)
    ppermute x126, waiting for transfers between devices, from_behind(): return lax.ppermute(block, axis, route)  1080 us
    dot_general x64, matrix products, score_block(): jnp.einsum('qhd,khd->hqk', query_part, key_part, preferred_element_type=j...  229 us
    psum x1, waiting for transfers between devices, on_device(): lax.psum((grad_attn_gain, grad_attn_bias, grad_mlp_gain, grad_mlp_bias, g...  151 us
    while x836, local copies, waits for them, and re-layouts  132 us
    all_gather x1, waiting for transfers between devices, on_device(): lax.all_gather(key_b, 'blk', axis=0, tiled=True)  115 us
    psum x1, blocking collectives, on_device(): lax.psum((grad_attn_gain, grad_attn_bias, grad_mlp_gain, grad_mlp_bias, g...  93.6 us
    dot_general x32, matrix products, back_block(): jnp.einsum('hqk,qhd->khd', probs.astype(jnp.bfloat16), grad_part, preferr...  89.5 us
    dot_general x16, matrix products, output_block(): jnp.einsum('hqk,khd->qhd', probs.astype(jnp.bfloat16), value_part, prefer...  88.6 us
  transfers between devices with their start and end apart: 129, of which 129 were waited for; matrix products, arithmetic and copies ran while one was open for 19% of the time, Pallas kernels for 0%

commit v1 on v0

v1 whole, which is shorter than its diff:
```python
import functools
import math

import jax
import jax.numpy as jnp
from jax import lax
from jax.experimental import pallas as pl
from jax.experimental.pallas import tpu as pltpu
from jax.sharding import PartitionSpec as P


D = 768
HEADS = 12
ROT = 16
FF = 3072
HALF = 4096
SPANS = 32
LROWS = 192
SROWS = 448
EPS = 1e-05
NEG = -1e30
SMALL = 80
BF = jnp.bfloat16
F32 = jnp.float32
MESH = pl.DeviceIdType.MESH
NT = (((1,), (1,)), ((), ()))
TN = (((0,), (0,)), ((), ()))


def mm(a, b):
    return jnp.dot(a, b, preferred_element_type=F32)


def mm_nt(a, b):
    return lax.dot_general(a, b, NT, preferred_element_type=F32)


def mm_tn(a, b):
    return lax.dot_general(a, b, TN, preferred_element_type=F32)


def halves(ref, off):
    first = ref[pl.ds(pl.multiple_of(off, 128), 128), :]
    second = ref[pl.ds(pl.multiple_of(128 - off, 128), 128), :]
    return jnp.concatenate([first, second], axis=0)


def low_lanes(shape):
    return lax.broadcasted_iota(jnp.int32, shape, 1) < 64


def swap64(v):
    return pltpu.roll(v, 64, 1)


def turn(v, c, s1, s2, sign):
    return v * c + sign * (pltpu.roll(v, 120, 1) * s1 + pltpu.roll(v, 8, 1) * s2)


def dp_shift(dp):
    return 2 * lax.rem(dp, 2) + dp // 2


def role(dp, me):
    y, z, part = me // 8, lax.rem(me // 2, 4), lax.rem(me, 2)
    q = lax.rem(z - y - dp_shift(dp) + 12, 4)
    return y, z, part, q


def pre_kernel(scal, tok, cot, again, abias, mgain, mbias, wqkv, bqkv, wout, c_ref, s1_ref, s2_ref,
               long_o, short_o, ha_o, hm_o):
    off = scal[0]
    x = halves(tok, off).astype(F32)
    dy = halves(cot, off)
    center = x - jnp.mean(x, axis=-1, keepdims=True)
    spread = jnp.mean(center * center, axis=-1, keepdims=True)
    z = center * lax.rsqrt(spread + EPS)
    ha = (z * again[...].astype(F32) + abias[...].astype(F32)).astype(BF)
    ha_o[...] = ha
    hm_o[...] = (z * mgain[...].astype(F32) + mbias[...].astype(F32)).astype(BF)
    cosine, s1, s2 = c_ref[...], s1_ref[...], s2_ref[...]
    low = low_lanes((256, 128))

    def put(head, kv, qg):
        long_o[2 * head, 0:128, :] = kv[0:128]
        long_o[2 * head + 1, 0:128, :] = kv[0:128]
        long_o[2 * head, 128:192, :] = qg[0:64]
        long_o[2 * head + 1, 128:192, :] = qg[64:128]
        pair, kind = head // 3, head % 3
        if kind == 1:
            for part in range(2):
                short_o[2 * pair + part, 256:384, :] = kv[128:256]
                short_o[2 * pair + part, 384:448, :] = qg[128 + 64 * part : 192 + 64 * part]
        else:
            slot = 2 * pair + kind // 2
            short_o[slot, 0:128, :] = kv[128:256]
            short_o[slot, 128:256, :] = qg[128:256]

    for wide in range(3):
        cols = slice(256 * wide, 256 * wide + 256)
        q2 = mm(ha, wqkv[:, cols]) + bqkv[:, cols].astype(F32)
        k2 = mm(ha, wqkv[:, 768 + 256 * wide : 1024 + 256 * wide])
        k2 = k2 + bqkv[:, 768 + 256 * wide : 1024 + 256 * wide].astype(F32)
        v2 = mm(ha, wqkv[:, 1536 + 256 * wide : 1792 + 256 * wide])
        v2 = v2 + bqkv[:, 1536 + 256 * wide : 1792 + 256 * wide].astype(F32)
        g2 = mm_nt(dy, wout[cols, :])
        for b in range(2):
            lanes = slice(128 * b, 128 * b + 128)
            q = turn(q2[:, lanes], cosine, s1, s2, 1.0).astype(BF).astype(F32) * 0.125
            k = turn(k2[:, lanes], cosine, s1, s2, 1.0)
            v, g = v2[:, lanes], g2[:, lanes]
            head = 4 * wide + 2 * b
            put(head, jnp.where(low, k, swap64(v)).astype(BF), jnp.where(low, q, swap64(g)).astype(BF))
            put(head + 1, jnp.where(low, swap64(k), v).astype(BF), jnp.where(low, swap64(q), g).astype(BF))


def vm(n):
    return [pl.BlockSpec(memory_space=pltpu.VMEM)] * n


def sm():
    return pl.BlockSpec(memory_space=pltpu.SMEM)


def pre_call(*args):
    return pl.pallas_call(
        pre_kernel,
        out_shape=(
            jax.ShapeDtypeStruct((24, LROWS, 128), BF),
            jax.ShapeDtypeStruct((8, SROWS, 128), BF),
            jax.ShapeDtypeStruct((256, D), BF),
            jax.ShapeDtypeStruct((256, D), BF),
        ),
        in_specs=[sm()] + vm(12),
        out_specs=vm(4),
        compiler_params=pltpu.CompilerParams(vmem_limit_bytes=48 << 20),
    )(*args)


def group_barrier(dp, me):
    bar = pltpu.get_barrier_semaphore()

    @pl.loop(1, 32)
    def _(i):
        pl.semaphore_signal(bar, inc=1, device_id=(dp, lax.rem(me + i, 32)), device_id_type=MESH)

    pl.semaphore_wait(bar, 31)


def walk(y, z, part, i):
    y2 = lax.rem(y + i // 8, 4)
    z2 = lax.rem(z + lax.rem(i // 2, 4), 4)
    p2 = lax.rem(part + lax.rem(i, 2), 2)
    return y2, z2, p2, y2 * 8 + z2 * 2 + p2


def out_kernel(l_ref, s_ref, lrx, srx, send_sem, recv_sem):
    dp, me = lax.axis_index("dp"), lax.axis_index("blk")
    shift = dp_shift(dp)
    group_barrier(dp, me)
    y, z, part, mine = role(dp, me)

    def copies(i, run):
        y2, z2, p2, d = walk(y, z, part, i)
        q = lax.rem(z2 - y2 - shift + 12, 4)

        @pl.when(q == 3)
        def _():
            run(s_ref.at[y2 * 2 + p2], srx.at[me], recv_sem.at[1], d)

        @pl.when(q != 3)
        def _():
            run(l_ref.at[(y2 * 3 + q) * 2 + p2], lrx.at[me], recv_sem.at[0], d)

    def remote(i, src, dst, sem, d):
        return pltpu.make_async_remote_copy(
            src, dst, send_sem.at[i], sem, device_id=(dp, d), device_id_type=MESH
        )

    copies(0, lambda src, dst, sem, d: pltpu.make_async_copy(src, dst, sem).start())

    @pl.loop(1, 32)
    def _(i):
        copies(i, lambda src, dst, sem, d: remote(i, src, dst, sem, d).start())

    @pl.when(mine == 3)
    def _():
        pltpu.make_async_copy(srx, srx, recv_sem.at[1]).wait()

    @pl.when(mine != 3)
    def _():
        pltpu.make_async_copy(lrx, lrx, recv_sem.at[0]).wait()

    @pl.loop(1, 32)
    def _(i):
        copies(i, lambda src, dst, sem, d: remote(i, src, dst, sem, d).wait_send())


def back_kernel(l_ref, s_ref, lrx, srx, send_sem, recv_sem):
    dp, me = lax.axis_index("dp"), lax.axis_index("blk")
    group_barrier(dp, me)
    y, z, part, mine = role(dp, me)

    def copies(i, run):
        y2, z2, p2, d = walk(y, z, part, i)

        @pl.when(mine == 3)
        def _():
            run(s_ref.at[d], srx.at[y * 2 + part], recv_sem.at[1], d)

        @pl.when(mine != 3)
        def _():
            run(l_ref.at[d], lrx.at[(y * 3 + mine) * 2 + part], recv_sem.at[0], d)

    def remote(i, src, dst, sem, d):
        return pltpu.make_async_remote_copy(
            src, dst, send_sem.at[i], sem, device_id=(dp, d), device_id_type=MESH
        )

    copies(0, lambda src, dst, sem, d: pltpu.make_async_copy(src, dst, sem).start())

    @pl.loop(1, 32)
    def _(i):
        copies(i, lambda src, dst, sem, d: remote(i, src, dst, sem, d).start())

    pltpu.make_async_copy(srx, srx, recv_sem.at[1]).wait()
    pltpu.make_async_copy(lrx, lrx, recv_sem.at[0]).wait()

    @pl.loop(1, 32)
    def _(i):
        copies(i, lambda src, dst, sem, d: remote(i, src, dst, sem, d).wait_send())


def exchange(kernel, cid, shapes, long_in, short_in):
    return pl.pallas_call(
        kernel,
        out_shape=tuple(jax.ShapeDtypeStruct(s, BF) for s in shapes),
        in_specs=vm(2),
        out_specs=vm(2),
        scratch_shapes=[pltpu.SemaphoreType.DMA((32,)), pltpu.SemaphoreType.DMA((2,))],
        compiler_params=pltpu.CompilerParams(
            collective_id=cid, has_side_effects=True, vmem_limit_bytes=40 << 20
        ),
    )(long_in, short_in)


def attend_kernel(scal, lrx, srx, starts_full, starts_half, ltx, stx, kv, kvt, qg, qo, dkv, sc):
    part = scal[2]
    lowq = low_lanes((256, 128))

    def fold(v, op):
        return op(v.reshape(v.shape[0] // 8, 8, v.shape[1]), axis=0)

    def load_tile(row):
        tile = qg[pl.ds(pl.multiple_of(row, 256), 256), :]
        zero = jnp.zeros_like(tile)
        gt = tile.astype(F32).T[64:128]
        return jnp.where(lowq, tile, zero), jnp.where(lowq, zero, tile), gt

    def store_tile(row, dqt, ot):
        both = jnp.concatenate([dqt * 0.125, ot], axis=0)
        qo[pl.ds(pl.multiple_of(row, 256), 256), :] = both.T.astype(BF)

    def key_rows(start, n):
        return lax.broadcasted_iota(jnp.int32, (n, 256), 0) + start

    def strided_places(t):
        col = lax.broadcasted_iota(jnp.int32, (1, 256), 1)
        return (4 * t + col // 64) * 128 + 64 * part + lax.rem(col, 64)

    def flip_all():
        @pl.loop(0, 32)
        def _(i):
            rows = pl.ds(pl.multiple_of(i * 128, 128), 128)
            kvt[:, rows] = kv[rows, :].astype(F32).T.astype(BF)

    @pl.when(scal[1] == 0)
    def _():
        @pl.loop(0, 32)
        def _(i):
            src = scal[8 + i]
            kv[pl.ds(pl.multiple_of(i * 128, 128), 128), :] = lrx[src, 0:128, :]
            qg[pl.ds(pl.multiple_of(i * 64, 64), 64), :] = lrx[src, 128:192, :]

        flip_all()
        dkv[...] = jnp.zeros_like(dkv)

        @pl.loop(0, 8)
        def _(t):
            qz, zg, gt = load_tile(t * 256)

            def chunk(c):
                return pl.ds(pl.multiple_of(c * 512, 512), 512)

            def score(c, m8):
                s = mm_nt(kv[chunk(c), :], qz)
                sc[chunk(c), :] = s
                return jnp.maximum(m8, fold(s, jnp.max))

            m8 = lax.fori_loop(0, t, score, jnp.full((8, 256), NEG, F32))
            s = mm_nt(kv[chunk(t), :], qz)
            s = jnp.where(key_rows(t * 512, 512) <= strided_places(t), s, NEG)
            sc[chunk(t), :] = s
            m8 = jnp.maximum(m8, fold(s, jnp.max))
            m = jnp.max(m8, axis=0, keepdims=True)

            def weigh(c, carry):
                l8, ot = carry
                p = jnp.exp(sc[chunk(c), :] - m)
                return l8 + fold(p, jnp.sum), ot + mm(kvt[64:128, chunk(c)], p.astype(BF))

            l8, ot = lax.fori_loop(
                0, t + 1, weigh, (jnp.zeros((8, 256), F32), jnp.zeros((64, 256), F32))
            )
            total = jnp.sum(l8, axis=0, keepdims=True)
            ot = ot * (1.0 / total)
            lse = m + jnp.log(total)
            delta = jnp.sum(gt * ot, axis=0, keepdims=True)

            def grads(c, dqt):
                p = jnp.exp(sc[chunk(c), :] - lse)
                ds = (p * (mm_nt(kv[chunk(c), :], zg) - delta)).astype(BF)
                dkv[chunk(c), :] += mm(ds, qz) + mm(p.astype(BF), zg)
                return dqt + mm(kvt[0:64, chunk(c)], ds)

            dqt = lax.fori_loop(0, t + 1, grads, jnp.zeros((64, 256), F32))
            store_tile(t * 256, dqt, ot)

        @pl.loop(0, 32)
        def _(i):
            rel = scal[40 + i]
            ltx[i, 0:128, :] = dkv[pl.ds(pl.multiple_of(rel * 128, 128), 128), :].astype(BF)
            ltx[i, 128:192, :] = qo[pl.ds(pl.multiple_of(rel * 64, 64), 64), :]

    def short_tile(row, start, n, places, begin):
        qz, zg, gt = load_tile(row)
        keys = pl.ds(pl.multiple_of(start, 256), n)
        k = kv[keys, :]
        place = key_rows(start, n)
        s = jnp.where((place <= places) & (place >= begin), mm_nt(k, qz), NEG)
        m = jnp.max(fold(s, jnp.max), axis=0, keepdims=True)
        e = jnp.exp(s - m)
        inv = 1.0 / jnp.sum(fold(e, jnp.sum), axis=0, keepdims=True)
        p = e * inv
        pb = p.astype(BF)
        ot = mm(kvt[64:128, keys], pb)
        delta = jnp.sum(gt * ot, axis=0, keepdims=True)
        ds = (p * (mm_nt(k, zg) - delta)).astype(BF)
        dkv[keys, :] += mm(ds, qz) + mm(pb, zg)
        dqt = mm(kvt[0:64, keys], ds)
        store_tile(row, dqt, ot)

    @pl.when(scal[1] == 1)
    def _():
        @pl.loop(0, 32)
        def _(i):
            src = scal[8 + 31 - i]
            kv[pl.ds(pl.multiple_of(i * 128, 128), 128), :] = srx[src, 0:128, :]
            qg[pl.ds(pl.multiple_of(i * 128, 128), 128), :] = srx[src, 128:256, :]

        flip_all()
        dkv[...] = jnp.zeros_like(dkv)

        @pl.loop(0, 16)
        def _(t):
            places = lax.broadcasted_iota(jnp.int32, (1, 256), 1) + 256 * t
            short_tile(t * 256, jnp.maximum(256 * t - 512, 0), 768, places, starts_full[pl.ds(t, 1), :])

        @pl.loop(0, 32)
        def _(i):
            rel = 31 - scal[40 + i]
            rows = pl.ds(pl.multiple_of(rel * 128, 128), 128)
            stx[i, 0:128, :] = dkv[rows, :].astype(BF)
            stx[i, 128:256, :] = qo[rows, :]

        @pl.loop(0, 32)
        def _(i):
            src = scal[8 + 31 - i]
            kv[pl.ds(pl.multiple_of(i * 128, 128), 128), :] = srx[src, 256:384, :]
            qg[pl.ds(pl.multiple_of(i * 64, 64), 64), :] = srx[src, 384:448, :]

        flip_all()
        dkv[...] = jnp.zeros_like(dkv)

        @pl.loop(0, 8)
        def _(t):
            short_tile(
                t * 256, jnp.maximum(512 * t - 512, 0), 1024, strided_places(t), starts_half[pl.ds(t, 1), :]
            )

        @pl.loop(0, 32)
        def _(i):
            rel = 31 - scal[40 + i]
            stx[i, 256:384, :] = dkv[pl.ds(pl.multiple_of(rel * 128, 128), 128), :].astype(BF)
            stx[i, 384:448, :] = qo[pl.ds(pl.multiple_of(rel * 64, 64), 64), :]


def attend_call(scal, lrx, srx, starts_full, starts_half):
    return pl.pallas_call(
        attend_kernel,
        out_shape=(
            jax.ShapeDtypeStruct((32, LROWS, 128), BF),
            jax.ShapeDtypeStruct((32, SROWS, 128), BF),
        ),
        in_specs=[sm()] + vm(4),
        out_specs=vm(2),
        scratch_shapes=[
            pltpu.VMEM((HALF, 128), BF),
            pltpu.VMEM((128, HALF), BF),
            pltpu.VMEM((HALF, 128), BF),
            pltpu.VMEM((HALF, 128), BF),
            pltpu.VMEM((HALF, 128), F32),
            pltpu.VMEM((HALF, 256), F32),
        ],
        compiler_params=pltpu.CompilerParams(vmem_limit_bytes=48 << 20),
    )(scal, lrx, srx, starts_full, starts_half)


def gelu_both(u):
    phi = 0.5 * (1.0 + lax.erf(u * (1.0 / math.sqrt(2.0))))
    density = jnp.exp(-0.5 * u * u) * (1.0 / math.sqrt(2.0 * math.pi))
    return u * phi, phi + u * density


def mlp_kernel(scal, hm, cot, up, upb, down, downb, grads_o, dh_o, branch_o, ub_o, hmt, dy):
    i = pl.program_id(0)

    @pl.when(i == 0)
    def _():
        hmt[...] = hm[...].astype(F32).T.astype(BF)
        dy[...] = halves(cot, scal[0])
        dh_o[...] = jnp.zeros_like(dh_o)
        branch_o[...] = jnp.broadcast_to(downb[...].astype(F32), branch_o.shape)

    u = mm(hm[...], up[...]) + upb[...].astype(F32)
    value, slope = gelu_both(u)
    hid = value.astype(BF)
    branch_o[...] += mm(hid, down[...])
    gu = mm_nt(dy[...], down[...]) * slope
    gub = gu.astype(BF)
    sums = jnp.sum(gub.astype(F32), axis=0, keepdims=True)
    for c in range(4):
        ub_o[pl.ds(4 * i + c, 1), :] = sums[:, 128 * c : 128 * c + 128]
    dh_o[...] += mm_nt(gub, up[...])
    gup = mm(hmt[...], gub).astype(BF)
    for c in range(4):
        grads_o[768 * c : 768 * c + 768, :] = gup[:, 128 * c : 128 * c + 128]
    gdown = mm_tn(hid, dy[...]).astype(BF)
    for c in range(6):
        grads_o[3072 + 512 * c : 3584 + 512 * c, :] = gdown[:, 128 * c : 128 * c + 128]


def mlp_call(scal, hm, cot, up, upb, down, downb):
    whole = lambda shape: pl.BlockSpec(shape, lambda i: (0, 0))
    return pl.pallas_call(
        mlp_kernel,
        grid=(6,),
        out_shape=(
            jax.ShapeDtypeStruct((36864, 128), BF),
            jax.ShapeDtypeStruct((256, D), F32),
            jax.ShapeDtypeStruct((256, D), F32),
            jax.ShapeDtypeStruct((24, 128), F32),
        ),
        in_specs=[
            sm(),
            whole((256, D)),
            whole((256, D)),
            pl.BlockSpec((D, 512), lambda i: (0, i)),
            pl.BlockSpec((1, 512), lambda i: (0, i)),
            pl.BlockSpec((512, D), lambda i: (i, 0)),
            whole((1, D)),
        ],
        out_specs=[
            pl.BlockSpec((6144, 128), lambda i: (i, 0)),
            whole((256, D)),
            whole((256, D)),
            whole((24, 128)),
        ],
        scratch_shapes=[pltpu.VMEM((D, 256), BF), pltpu.VMEM((256, D), BF)],
        compiler_params=pltpu.CompilerParams(vmem_limit_bytes=48 << 20),
    )(scal, hm, cot, up, upb, down, downb)


def post_kernel(scal, tok, cot, ha, again, mgain, wqkv, wout, outb, c_ref, s1_ref, s2_ref, lret, sret,
                dmlp, mlp, ub, mixed_o, tgrad_o, grads_o, small_o, gqkv, att):
    off = scal[0]
    cosine, s1, s2 = c_ref[...], s1_ref[...], s2_ref[...]
    low = low_lanes((256, 128))

    def f(v):
        return v.astype(F32)

    def gather(head):
        pair, kind = head // 3, head % 3
        kv_l = f(lret[2 * head, 0:128, :]) + f(lret[2 * head + 1, 0:128, :])
        qo_l = [f(lret[2 * head, 128:192, :]), f(lret[2 * head + 1, 128:192, :])]
        if kind == 1:
            kv_s = f(sret[2 * pair, 256:384, :]) + f(sret[2 * pair + 1, 256:384, :])
            qo_s = [f(sret[2 * pair, 384:448, :]), f(sret[2 * pair + 1, 384:448, :])]
        else:
            slot = 2 * pair + kind // 2
            kv_s = f(sret[slot, 0:128, :])
            qo_s = [f(sret[slot, 128:256, :])]
        return jnp.concatenate([kv_l, kv_s], axis=0), jnp.concatenate(qo_l + qo_s, axis=0)

    for j in range(6):
        kv_a, qo_a = gather(2 * j)
        kv_b, qo_b = gather(2 * j + 1)
        dq = jnp.where(low, qo_a, swap64(qo_b))
        ov = jnp.where(low, swap64(qo_a), qo_b)
        dk = jnp.where(low, kv_a, swap64(kv_b))
        dv = jnp.where(low, swap64(kv_a), kv_b)
        cols = slice(128 * j, 128 * j + 128)
        att[:, cols] = ov.astype(BF)
        gqkv[:, cols] = turn(dq, cosine, s1, s2, -1.0).astype(BF)
        gqkv[:, 768 + 128 * j : 896 + 128 * j] = turn(dk, cosine, s1, s2, -1.0).astype(BF)
        gqkv[:, 1536 + 128 * j : 1664 + 128 * j] = dv.astype(BF)

    x = f(halves(tok, off))
    dy_b = halves(cot, off)
    dy = f(dy_b)
    attn = mm(att[...], wout[...]) + f(outb[...])
    y = x + attn + mlp[...]
    mixed = y.astype(BF)
    first = pl.ds(pl.multiple_of(off, 128), 128)
    second = pl.ds(pl.multiple_of(128 - off, 128), 128)
    mixed_o[first, :] = mixed[0:128]
    mixed_o[second, :] = mixed[128:256]

    def rows(v, at, n):
        for c in range(n):
            small_o[at + c : at + c + 1, :] = v[:, 128 * c : 128 * c + 128]

    def square(v, at):
        s = jnp.sum(v * v, axis=0, keepdims=True)
        t = s[:, 0:128]
        for c in range(1, 6):
            t = t + s[:, 128 * c : 128 * c + 128]
        small_o[at : at + 1, :] = t

    small_o[72:80, :] = jnp.zeros((8, 128), F32)
    square(y, 72)
    square(attn, 73)
    square(mlp[...], 74)
    rows(jnp.sum(dy, axis=0, keepdims=True), 42, 6)
    small_o[48:72, :] = ub[...]

    attT = f(att[...]).T.astype(BF)
    haT = f(ha[...]).T.astype(BF)
    for w in range(3):
        t = mm(attT, dy_b[:, 256 * w : 256 * w + 256]).astype(BF)
        for b in range(2):
            grads_o[768 * (18 + 2 * w + b) : 768 * (19 + 2 * w + b), :] = t[:, 128 * b : 128 * b + 128]
    d_attn = jnp.zeros((256, D), F32)
    for w in range(9):
        cols = slice(256 * w, 256 * w + 256)
        part = gqkv[:, cols]
        rows(jnp.sum(f(part), axis=0, keepdims=True), 24 + 2 * w, 2)
        t = mm(haT, part).astype(BF)
        for b in range(2):
            grads_o[768 * (2 * w + b) : 768 * (2 * w + b + 1), :] = t[:, 128 * b : 128 * b + 128]
        d_attn = d_attn + mm_nt(part, wqkv[:, cols])

    center = x - jnp.mean(x, axis=-1, keepdims=True)
    r = lax.rsqrt(jnp.mean(center * center, axis=-1, keepdims=True) + EPS)
    z = center * r

    def norm_back(d, gain, at):
        rows(jnp.sum(d * z, axis=0, keepdims=True), at, 6)
        rows(jnp.sum(d, axis=0, keepdims=True), at + 6, 6)
        e = d * f(gain[...])
        return r * (
            e - jnp.mean(e, axis=-1, keepdims=True) - z * jnp.mean(e * z, axis=-1, keepdims=True)
        )

    total = dy + norm_back(d_attn, again, 0) + norm_back(dmlp[...], mgain, 12)
    tgrad_o[first, :] = total[0:128]
    tgrad_o[second, :] = total[128:256]


def post_call(*args):
    return pl.pallas_call(
        post_kernel,
        out_shape=(
            jax.ShapeDtypeStruct((256, D), BF),
            jax.ShapeDtypeStruct((256, D), F32),
            jax.ShapeDtypeStruct((18432, 128), BF),
            jax.ShapeDtypeStruct((SMALL, 128), F32),
        ),
        in_specs=[sm()] + vm(16),
        out_specs=vm(4),
        scratch_shapes=[pltpu.VMEM((256, 3 * D), BF), pltpu.VMEM((256, D), BF)],
        compiler_params=pltpu.CompilerParams(vmem_limit_bytes=56 << 20),
    )(*args)


def place_id(core, x, y, z):
    return (lax.rem(x, 2) * 2 + core, y * 8 + z * 2 + x // 2)


def cube_partners():
    dp, blk = lax.axis_index("dp"), lax.axis_index("blk")
    core = lax.rem(dp, 2)
    at = {"x": lax.rem(blk, 2) * 2 + dp // 2, "y": blk // 8, "z": lax.rem(blk // 2, 4)}
    out = []
    for axis in ("x", "y", "z"):
        v = at[axis]
        hi, lo = v // 2, lax.rem(v, 2)
        for nv, bit in ((v + 1 - 2 * lo, lax.rem(hi + lo, 2)), (3 - v, hi)):
            there = dict(at)
            there[axis] = nv
            out.append((place_id(core, there["x"], there["y"], there["z"]), bit))
    return core, place_id(1 - core, at["x"], at["y"], at["z"]), out


def sum_kernel(rows, steps, f_ref, s_ref, a_ref, so_ref, rx0, *rest):
    rxs, rxe, srx = rest[:steps], rest[steps], rest[steps + 1]
    (core_s, core_r, rs_s, rs_r, ex_s, ex_r, ag_s, ag_r, fin_s, fin_r, sm_s, sm_r, loc) = rest[steps + 2 :]
    part, half_rows = rows // 12, rows // 2
    core, other, partners = cube_partners()
    bar = pltpu.get_barrier_semaphore()
    for d in [other] + [q[0] for q in partners]:
        pl.semaphore_signal(bar, inc=1, device_id=d, device_id_type=MESH)
    pl.semaphore_wait(bar, 7)

    def remote(src, dst, ss, rs, d):
        return pltpu.make_async_remote_copy(src, dst, ss, rs, device_id=d, device_id_type=MESH)

    base = [pl.multiple_of(core * half_rows + p * part, 16) for p in range(6)]
    obase = [pl.multiple_of((1 - core) * half_rows + p * part, 16) for p in range(6)]

    def add(off, n, src):
        w = 96
        while n % w:
            w //= 2

        @pl.loop(0, n // w)
        def _(i):
            here = pl.ds(pl.multiple_of(off + i * w, 16), w)
            there = pl.ds(pl.multiple_of(i * w, 16), w)
            f_ref[here, :] = (f_ref[here, :].astype(F32) + src[there, :].astype(F32)).astype(BF)

    small_to = [other] + [q[0] for q in partners]
    so_ref[...] = s_ref[...]

    def small_copy(t):
        return remote(so_ref, srx.at[t], sm_s.at[t], sm_r.at[t], small_to[t])

    def small_finish(t):
        small_copy(t).wait()
        so_ref[...] += srx[t]

    pend = [
        remote(f_ref.at[pl.ds(obase[p], part)], rx0.at[p], core_s.at[p], core_r.at[p], other)
        for p in range(6)
    ]
    small_copy(0).start()
    for p in range(6):
        pend[p].start()
    offs, size = list(base), part
    for t in range(steps):
        h = size // 2
        for p in range(6):
            pend[p].wait_recv()
            add(offs[p], size, (rx0 if t == 0 else rxs[t - 1]).at[p])
            dev, bit = partners[(p + t) % 6]
            out = pl.multiple_of(offs[p] + (1 - bit) * h, 16)
            c = remote(f_ref.at[pl.ds(out, h)], rxs[t].at[p], rs_s.at[t, p], rs_r.at[t, p], dev)
            c.start()
            pend[p].wait_send()
            pend[p] = c
            offs[p] = pl.multiple_of(offs[p] + bit * h, 16)
        small_finish(t)
        small_copy(t + 1).start()
        size = h
    both = []
    for p in range(6):
        pend[p].wait_recv()
        add(offs[p], size, rxs[steps - 1].at[p])
        c = remote(
            f_ref.at[pl.ds(offs[p], size)], rxe.at[p], ex_s.at[p], ex_r.at[p], partners[(p + steps) % 6][0]
        )
        c.start()
        pend[p].wait_send()
        both.append(c)
    small_finish(steps)
    small_copy(steps + 1).start()
    own = []
    for p in range(6):
        both[p].wait()
        add(offs[p], size, rxe.at[p])
        here = pl.ds(offs[p], size)
        c = pltpu.make_async_copy(f_ref.at[here], a_ref.at[here], loc.at[p])
        c.start()
        own.append(c)
    for p in range(6):
        own[p].wait()
    prev = [None] * 6
    for t in reversed(range(steps)):
        for p in range(6):
            if prev[p] is not None:
                prev[p].wait()
            dev, bit = partners[(p + t) % 6]
            here = pl.ds(offs[p], size)
            prev[p] = remote(a_ref.at[here], a_ref.at[here], ag_s.at[t, p], ag_r.at[t, p], dev)
            prev[p].start()
            offs[p] = pl.multiple_of(offs[p] - bit * size, 16)
        size *= 2
    last = []
    for p in range(6):
        prev[p].wait()
        here = pl.ds(base[p], part)
        c = remote(a_ref.at[here], a_ref.at[here], fin_s.at[p], fin_r.at[p], other)
        c.start()
        last.append(c)
    small_finish(steps + 1)
    for p in range(6):
        last[p].wait()


def sum_call(f, s, cid):
    rows, steps = f.shape[0], 5
    part = rows // 12
    dma = pltpu.SemaphoreType.DMA
    return pl.pallas_call(
        functools.partial(sum_kernel, rows, steps),
        out_shape=(jax.ShapeDtypeStruct(f.shape, BF), jax.ShapeDtypeStruct(s.shape, F32)),
        in_specs=vm(2),
        out_specs=[pl.BlockSpec(memory_space=pl.ANY)] + vm(1),
        scratch_shapes=[pltpu.VMEM((6, part, 128), BF)]
        + [pltpu.VMEM((6, part >> (t + 1), 128), BF) for t in range(steps)]
        + [pltpu.VMEM((6, part >> steps, 128), BF), pltpu.VMEM((7,) + s.shape, F32)]
        + [dma((6,)), dma((6,)), dma((steps, 6)), dma((steps, 6)), dma((6,)), dma((6,))]
        + [dma((steps, 6)), dma((steps, 6)), dma((6,)), dma((6,)), dma((7,)), dma((7,)), dma((6,))],
        compiler_params=pltpu.CompilerParams(
            collective_id=cid, has_side_effects=True, vmem_limit_bytes=56 << 20
        ),
    )(f, s)


def unpack_mlp_kernel(a, up_o, down_o):
    for c in range(4):
        up_o[:, 128 * c : 128 * c + 128] = a[768 * c : 768 * c + 768, :].astype(F32)
    for c in range(6):
        down_o[:, 128 * c : 128 * c + 128] = a[3072 + 512 * c : 3584 + 512 * c, :].astype(F32)


def unpack_mlp(a):
    return pl.pallas_call(
        unpack_mlp_kernel,
        grid=(6,),
        out_shape=(jax.ShapeDtypeStruct((D, FF), F32), jax.ShapeDtypeStruct((FF, D), F32)),
        in_specs=[pl.BlockSpec((6144, 128), lambda i: (i, 0))],
        out_specs=[pl.BlockSpec((D, 512), lambda i: (0, i)), pl.BlockSpec((512, D), lambda i: (i, 0))],
        compiler_params=pltpu.CompilerParams(vmem_limit_bytes=48 << 20),
    )(a)


def unpack_attn_kernel(a, b, qkv_o, out_o):
    for c in range(6):
        qkv_o[:, 128 * c : 128 * c + 128] = a[768 * c : 768 * c + 768, :].astype(F32)
    for c in range(2):
        out_o[:, 128 * c : 128 * c + 128] = b[768 * c : 768 * c + 768, :].astype(F32)


def unpack_attn(a):
    return pl.pallas_call(
        unpack_attn_kernel,
        grid=(3,),
        out_shape=(jax.ShapeDtypeStruct((D, 3 * D), F32), jax.ShapeDtypeStruct((D, D), F32)),
        in_specs=[
            pl.BlockSpec((4608, 128), lambda i: (i, 0)),
            pl.BlockSpec((1536, 128), lambda i: (9 + i, 0)),
        ],
        out_specs=[pl.BlockSpec((D, 768), lambda i: (0, i)), pl.BlockSpec((D, 256), lambda i: (0, i))],
        compiler_params=pltpu.CompilerParams(vmem_limit_bytes=48 << 20),
    )(a, a)


def on_device(tokens, attn_gain, attn_bias, mlp_gain, mlp_bias, qkv_weight, qkv_bias, out_weight, out_bias,
              up_weight, up_bias, down_weight, down_bias, cotangent, doc_lengths, span_order):
    dp, me = lax.axis_index("dp"), lax.axis_index("blk")
    y, z, part, q = role(dp, me)
    lengths, order = doc_lengths[0], span_order[0]
    first_long = lengths[0] > 512
    spans = order.reshape(SPANS, 2)[:, 0]
    long_span = jnp.where(first_long, spans, 31 - spans)
    index = jnp.arange(SPANS, dtype=jnp.int32)
    source = jnp.sum(jnp.where(long_span[None, :] == index[:, None], index[None, :], 0), axis=1)
    mine = jnp.sum(jnp.where(index == me, long_span, 0))
    head = jnp.stack(
        [jnp.where(first_long, 0, 128), jnp.where(q == 3, 1, 0), part, mine, mine, mine, mine, mine]
    )
    scal = jnp.concatenate([head, source, long_span]).astype(jnp.int32)

    ends = jnp.cumsum(jnp.where(first_long, lengths[1:], lengths[:-1])).astype(jnp.int32)

    def begin_of(place):
        return jnp.max(jnp.where(ends[:, None] <= place[None, :], ends[:, None], 0), axis=0)

    starts = begin_of(jnp.arange(HALF, dtype=jnp.int32))
    starts_full = starts.reshape(16, 256)
    pieces = starts.reshape(32, 2, 64)
    starts_half = jnp.where(part == 0, pieces[:, 0], pieces[:, 1]).reshape(8, 256)

    lane = jnp.arange(128, dtype=jnp.int32)
    row = jnp.arange(128, dtype=jnp.int32)
    short_place = (31 - mine) * 128 + row
    position = jnp.concatenate([mine * 128 + row, short_place - begin_of(short_place)])
    inverse = jnp.exp((lane % 8).astype(F32) * (-2.0 * math.log(10000.0) / ROT))
    angle = position.astype(F32)[:, None] * inverse[None, :]
    dim = (lane % 64)[None, :]
    sine = jnp.sin(angle)
    c_tab = jnp.where(dim < ROT, jnp.cos(angle), 1.0)
    s1_tab = jnp.where(dim < ROT // 2, -sine, 0.0)
    s2_tab = jnp.where((dim >= ROT // 2) & (dim < ROT), sine, 0.0)

    line = lambda v: v.reshape(1, -1)
    again, abias, mgain, mbias = line(attn_gain), line(attn_bias), line(mlp_gain), line(mlp_bias)
    long_tx, short_tx, ha, hm = pre_call(
        scal, tokens, cotangent, again, abias, mgain, mbias, qkv_weight, line(qkv_bias), out_weight,
        c_tab, s1_tab, s2_tab,
    )
    long_rx, short_rx = exchange(out_kernel, 0, ((32, LROWS, 128), (32, SROWS, 128)), long_tx, short_tx)
    mlp_grads, dmlp, mlp_branch, ub = mlp_call(
        scal, hm, cotangent, up_weight, line(up_bias), down_weight, line(down_bias)
    )
    long_back, short_back = attend_call(scal, long_rx, short_rx, starts_full, starts_half)
    long_ret, short_ret = exchange(
        back_kernel, 1, ((24, LROWS, 128), (8, SROWS, 128)), long_back, short_back
    )
    mixed, tokens_grad, attn_grads, small = post_call(
        scal, tokens, cotangent, ha, again, mgain, qkv_weight, out_weight, line(out_bias), c_tab, s1_tab, s2_tab,
        long_ret, short_ret, dmlp, mlp_branch, ub,
    )
    mlp_sum, unused = sum_call(mlp_grads, jnp.zeros((8, 128), F32), 2)
    attn_sum, small_sum = sum_call(attn_grads, small, 3)
    grad_up, grad_down = unpack_mlp(mlp_sum)
    grad_qkv, grad_out = unpack_attn(attn_sum)

    def vector(at, n):
        return small_sum[at : at + n].reshape(128 * n)

    roots = jnp.sqrt(jnp.sum(small_sum[72:75], axis=1) / (D * 256 * 128))
    branch_bias = vector(42, 6)
    return (
        mixed, tokens_grad, vector(0, 6), vector(6, 6), vector(12, 6), vector(18, 6), grad_qkv, vector(24, 18),
        grad_out, branch_bias, grad_up, vector(48, 24), grad_down, branch_bias, roots[0], roots[1], roots[2],
    )


def solution(mesh):
    rows, split = P(("dp", "blk"), None), P("dp", None)
    return jax.shard_map(
        on_device,
        mesh=mesh,
        in_specs=(rows,) + (P(),) * 12 + (rows, split, split),
        out_specs=(rows, rows) + (P(),) * 15,
        check_vma=False,
    )
```

time: 2770 us -> 341 us (0.12)
  waiting for transfers between devices: 1420 us -> 0 us
  matrix products: 716 us -> 0 us
  Pallas kernels: 0 us -> 308 us
  other arithmetic: 227 us -> 4.08 us
  local copies, waits for them, and re-layouts: 225 us -> 25.1 us
  blocking collectives: 93.6 us -> 0 us
    ppermute x126 -> x0, waiting for transfers between devices: 1080 us -> none  [from_behind(): return lax.ppermute(block, axis, route)]
    dot_general x236 -> x0, matrix products: 716 us -> none  [the longest x64 229 us: score_block(): jnp.einsum('qhd,khd->hqk', query_part, key_part, preferred_element_type=j...]
    pallas_call x0 -> x10, Pallas kernels: none -> 308 us  [the longest x2 142 us: sum_call(): pl.pallas_call(functools.partial(sum_kernel, rows, steps), out_shape=(jax...]
    all_gather x2 -> x0, waiting for transfers between devices: 189 us -> none  [the longest x1 115 us: on_device(): lax.all_gather(key_b, 'blk', axis=0, tiled=True)]
    psum x1 -> x0, waiting for transfers between devices: 151 us -> none  [on_device(): lax.psum((grad_attn_gain, grad_attn_bias, grad_mlp_gain, grad_mlp_bias, g...]
    reduce_sum x149 -> x3, other arithmetic: 144 us -> 0.87 us  [the longest x1 0.65 us: on_device(): mine = jnp.sum(jnp.where(index == me, long_span, 0))]
    while x836 -> x0, local copies, waits for them, and re-layouts: 132 us -> none
    psum x1 -> x0, blocking collectives: 93.6 us -> none  [on_device(): lax.psum((grad_attn_gain, grad_attn_bias, grad_mlp_gain, grad_mlp_bias, g...]
  transfers between devices with their start and end apart: 129 -> 0, of which waited for: 129 -> 0; matrix products, arithmetic and copies ran while one was open for 19% -> 0% of each run, Pallas kernels for 0% -> 0%
where the time goes in v1:
time: 341 us
  Pallas kernels  308 us (90%)
  local copies, waits for them, and re-layouts  25.1 us (7%)
  other arithmetic  4.08 us (1%)
    pallas_call x2, Pallas kernels, sum_call(): pl.pallas_call(functools.partial(sum_kernel, rows, steps), out_shape=(jax...  142 us
    pallas_call x2, Pallas kernels, exchange(): pl.pallas_call(kernel, out_shape=tuple((jax.ShapeDtypeStruct(s, BF) for s...  82.1 us
    pallas_call x1, Pallas kernels, attend_call(): pl.pallas_call(attend_kernel, out_shape=(jax.ShapeDtypeStruct((32, LROWS,...  42.1 us
    unnamed x50, local copies, waits for them, and re-layouts  14.4 us
    pallas_call x1, Pallas kernels, mlp_call(): pl.pallas_call(mlp_kernel, grid=(6,), out_shape=(jax.ShapeDtypeStruct((36...  13.2 us
    pallas_call x1, Pallas kernels, unpack_mlp(): pl.pallas_call(unpack_mlp_kernel, grid=(6,), out_shape=(jax.ShapeDtypeStr...  11.1 us
    pallas_call x1, Pallas kernels, post_call(): pl.pallas_call(post_kernel, out_shape=(jax.ShapeDtypeStruct((256, D), BF)...  10 us

profile of v1, /device:TPU:1, one launch (start us, length us, event | category | flops | bytes accessed | tf_op | source)
XLA Modules:
  0.0 340.6 jit_solution(5712386936693271128)
XLA Ops:
  1.4 0.5 broadcast.141
  1.9 1.3 reduce.9
  3.2 0.1 reshape_squeeze.3
  3.3 0.1 slice_reduce_fusion
  3.4 0.6 fusion.6
  4.1 0.1 select_reduce_fusion.1
  4.2 3.3 concatenate.10.scal
  8.2 0.8 fusion.5
  9.0 0.2 reduce-window.8
  9.1 0.1 select_reduce_fusion.2
  10.0 0.6 fusion
  10.5 0.0 copy-start.7
  10.5 0.0 copy-start.8
  10.5 0.0 copy-start.9
  10.5 0.7 reshape.193.again
  11.3 0.7 reshape.195.mgain
  12.0 0.7 reshape.197.bqkv
  12.7 0.7 reshape.194.abias
  13.4 0.7 reshape.196.mbias
  14.0 1.3 copy-done.1
  15.3 1.0 copy-done.4
  16.3 1.0 copy-done.6
  17.3 4.0 %shard_map.287 = (bf16[24,192,128]{2,1,0:T(8,128)(2,1)S(1)}, bf16[8,448,128]{2,1,0:T(8,128)(2,1)S(1)}, bf16[256,768]{1,0:T(8,128)(2,1)S(1)}, bf16[256,768]{1,0:T(8,128)(2,1)S(1)}) custom-call(s32[72]{0:T(128)S(1)} %concatenate.10.scal, bf16[256,768]{1,0:T(8,128)(2,1)S(1)} %copy-done.6, bf16[256,768]{1,0:T(8,128)(2,1)S(1)} %copy-done.4, ...), custom_call_target="tpu_custom_call" | custom-call | tf_op jit(solution)/shard_map/pallas_call | solution.py:126
  21.3 0.0 copy-start.14
  21.3 38.7 %shard_map.288 = (bf16[32,192,128]{2,1,0:T(8,128)(2,1)S(1)}, bf16[32,448,128]{2,1,0:T(8,128)(2,1)S(1)}) custom-call(bf16[24,192,128]{2,1,0:T(8,128)(2,1)S(1)} %get-tuple-element.43.l_ref, bf16[8,448,128]{2,1,0:T(8,128)(2,1)S(1)} %get-tuple-element.44.s_ref), custom_call_target="tpu_custom_call" | custom-call | tf_op jit(solution)/shard_map/pallas_call | solution.py:235
  60.0 0.0 copy-done.14
  60.0 0.0 copy-start.3
  60.1 1.8 copy-done.3
  61.9 0.1 select_reduce_fusion
  62.0 0.1 reshape.201
  62.1 0.1 fusion.4
  62.2 0.1 select_n.135.starts_half
  62.3 0.0 copy-start.22
  62.3 0.0 copy-start.5
  62.3 42.1 %shard_map.289 = (bf16[32,192,128]{2,1,0:T(8,128)(2,1)S(1)}, bf16[32,448,128]{2,1,0:T(8,128)(2,1)}) custom-call(s32[72]{0:T(128)S(1)} %concatenate.10.scal, bf16[32,192,128]{2,1,0:T(8,128)(2,1)S(1)} %get-tuple-element.45.lrx, bf16[32,448,128]{2,1,0:T(8,128)(2,1)} %copy-done.3, s32[16,256]{1,0:T(8,128)S(1)} %reshape.200.starts_full, ...), custom_call_target="tpu_custom_call" | custom-call | tf_op jit(solution)/shard_map/pallas_call | solution.py:399
  104.4 0.0 copy-done.7
  104.4 0.0 copy-done.8
  104.4 0.0 copy-done.9
  104.4 0.0 copy-done.15
  104.4 0.0 copy-start.2
  104.4 2.0 copy-done.2
  106.5 43.4 %shard_map.290 = (bf16[24,192,128]{2,1,0:T(8,128)(2,1)S(1)}, bf16[8,448,128]{2,1,0:T(8,128)(2,1)S(1)}) custom-call(bf16[32,192,128]{2,1,0:T(8,128)(2,1)S(1)} %get-tuple-element.47.l_ref, bf16[32,448,128]{2,1,0:T(8,128)(2,1)S(1)} %copy-done.2), custom_call_target="tpu_custom_call" | custom-call | tf_op jit(solution)/shard_map/pallas_call | solution.py:235
  149.9 0.0 copy-start.10
  149.9 1.0 copy-done.10
  150.9 0.9 copy-done.11
  151.9 0.0 copy-start.23
  151.9 13.2 %shard_map.291 = (bf16[36864,128]{1,0:T(8,128)(2,1)}, f32[256,768]{1,0:T(8,128)S(1)}, f32[256,768]{1,0:T(8,128)S(1)}, f32[24,128]{1,0:T(8,128)S(1)}) custom-call(s32[72]{0:T(128)S(1)} %concatenate.10.scal, bf16[256,768]{1,0:T(8,128)(2,1)S(1)} %get-tuple-element.51.hm, bf16[256,768]{1,0:T(8,128)(2,1)S(1)} %copy-done.5, bf16[768,3072]{1,0:T(8,128)(2,1)} %up.1, ...), custom_call_target="tpu_custom_call" | custom-call | tf_op jit(solution)/shard_map/pallas_call | solution.py:455
  165.0 0.9 copy-done.12
  165.9 0.9 copy-done.13
  166.9 0.6 reshape.199.outb
  167.4 0.0 copy-done.18
  167.5 10.0 %shard_map.292 = (bf16[256,768]{1,0:T(8,128)(2,1)}, f32[256,768]{1,0:T(8,128)}, bf16[18432,128]{1,0:T(8,128)(2,1)}, f32[80,128]{1,0:T(8,128)}) custom-call(s32[72]{0:T(128)} %copy-done.17, bf16[256,768]{1,0:T(8,128)(2,1)} %tok.3, bf16[256,768]{1,0:T(8,128)(2,1)} %cot.5, bf16[256,768]{1,0:T(8,128)(2,1)} %copy-done.14, bf16[1,768]{1,0:T(2,128)(2,1)} %copy-done.15, ...), custom_call_target="tpu_custom_call" | custom-call | tf_op jit(solution)/shard_map/pallas_call | solution.py:582
  177.5 61.5 %shard_map.293 = (bf16[18432,128]{1,0:T(8,128)(2,1)}, f32[80,128]{1,0:T(8,128)}) custom-call(bf16[18432,128]{1,0:T(8,128)(2,1)} %get-tuple-element.57.f_ref, f32[80,128]{1,0:T(8,128)} %get-tuple-element.58.s_ref), custom_call_target="tpu_custom_call" | custom-call | tf_op jit(solution)/shard_map/pallas_call | solution.py:725
  238.9 2.3 copy-done
  241.3 3.8 %shard_map.294 = (f32[768,2304]{1,0:T(8,128)}, f32[768,768]{1,0:T(8,128)}) custom-call(bf16[18432,128]{1,0:T(8,128)(2,1)S(1)} %copy-done, bf16[18432,128]{1,0:T(8,128)(2,1)S(1)} %copy-done), custom_call_target="tpu_custom_call" | custom-call | tf_op jit(solution)/shard_map/pallas_call | solution.py:767
  245.1 0.6 broadcast_in_dim.87.s_ref
  245.7 80.7 %shard_map.295 = (bf16[36864,128]{1,0:T(8,128)(2,1)}, f32[8,128]{1,0:T(8,128)}) custom-call(bf16[36864,128]{1,0:T(8,128)(2,1)} %get-tuple-element.63.f_ref, f32[8,128]{1,0:T(8,128)} %broadcast_in_dim.87.s_ref), custom_call_target="tpu_custom_call" | custom-call | tf_op jit(solution)/shard_map/pallas_call | solution.py:725
  326.3 11.1 %shard_map.296 = (f32[768,3072]{1,0:T(8,128)}, f32[3072,768]{1,0:T(8,128)}) custom-call(bf16[36864,128]{1,0:T(8,128)(2,1)} %get-tuple-element.64.a), custom_call_target="tpu_custom_call" | custom-call | tf_op jit(solution)/shard_map/pallas_call | solution.py:749
  337.5 0.6 slice_bitcast_fusion.2
  338.1 0.6 slice_bitcast_fusion
  338.7 0.6 slice_bitcast_fusion.1
  339.3 0.1 slice_reduce_fusion.1
  339.4 0.6 fusion.11
  340.0 0.6 copy.34
  (32 shorter events, 0.1 us)
Async XLA Ops:
  7.5 144.4 %copy-start.17 = (s32[72]{0:T(128)}, s32[72]{0:T(128)S(1)}, u32[]{:S(2)}) copy-start(s32[72]{0:T(128)S(1)} %concatenate.10.scal) | copy-start | bytes 868
  10.5 93.9 %copy-start.7 = (f32[256,128]{1,0:T(8,128)}, f32[256,128]{1,0:T(8,128)S(1)}, u32[]{:S(2)}) copy-start(f32[256,128]{1,0:T(8,128)S(1)} %get-tuple-element.74.s2_ref) | copy-start | bytes 393220
  10.5 93.9 %copy-start.8 = (f32[256,128]{1,0:T(8,128)}, f32[256,128]{1,0:T(8,128)S(1)}, u32[]{:S(2)}) copy-start(f32[256,128]{1,0:T(8,128)S(1)} %get-tuple-element.75.s1_ref) | copy-start | bytes 393220
  10.5 93.9 %copy-start.9 = (f32[256,128]{1,0:T(8,128)}, f32[256,128]{1,0:T(8,128)S(1)}, u32[]{:S(2)}) copy-start(f32[256,128]{1,0:T(8,128)S(1)} %get-tuple-element.76.c_ref) | copy-start | bytes 393220
  11.3 93.1 %copy-start.15 = (bf16[1,768]{1,0:T(2,128)(2,1)}, bf16[1,768]{1,0:T(2,128)(2,1)S(1)}, u32[]{:S(2)}) copy-start(bf16[1,768]{1,0:T(2,128)(2,1)S(1)} %reshape.193.again) | copy-start | bytes 4612
  12.0 92.4 %copy-start.16 = (bf16[1,768]{1,0:T(2,128)(2,1)}, bf16[1,768]{1,0:T(2,128)(2,1)S(1)}, u32[]{:S(2)}) copy-start(bf16[1,768]{1,0:T(2,128)(2,1)S(1)} %reshape.195.mgain) | copy-start | bytes 4612
  14.0 1.3 copy-start.1
  15.3 1.0 copy-start.4
  16.3 1.0 copy-start.6
  21.3 38.7 %copy-start.14 = (bf16[256,768]{1,0:T(8,128)(2,1)}, bf16[256,768]{1,0:T(8,128)(2,1)S(1)}, u32[]{:S(2)}) copy-start(bf16[256,768]{1,0:T(8,128)(2,1)S(1)} %get-tuple-element.42.ha) | copy-start | bytes 1179652
  60.0 1.8 copy-start.3
  62.3 89.5 %copy-start.21 = (bf16[3072]{0:T(1024)(128)(2,1)S(1)}, bf16[3072]{0:T(1024)(128)(2,1)}, u32[]{:S(2)}) copy-start(bf16[3072]{0:T(1024)(128)(2,1)} %param.26) | copy-start | bytes 18436
  62.3 89.5 %copy-start.22 = (bf16[768]{0:T(1024)(128)(2,1)S(1)}, bf16[768]{0:T(1024)(128)(2,1)}, u32[]{:S(2)}) copy-start(bf16[768]{0:T(1024)(128)(2,1)} %param.28) | copy-start | bytes 4612
  62.3 89.6 %copy-start.5 = (bf16[256,768]{1,0:T(8,128)(2,1)S(1)}, bf16[256,768]{1,0:T(8,128)(2,1)}, u32[]{:S(2)}) copy-start(bf16[256,768]{1,0:T(8,128)(2,1)} %cot.5) | copy-start | bytes 1179652
  104.4 2.0 copy-start.2
  149.9 1.0 copy-start.10
  150.9 0.9 copy-start.11
  151.9 15.0 %copy-start.23 = (bf16[768]{0:T(1024)(128)(2,1)S(1)}, bf16[768]{0:T(1024)(128)(2,1)}, u32[]{:S(2)}) copy-start(bf16[768]{0:T(1024)(128)(2,1)} %param.24) | copy-start | bytes 4612
  165.0 0.9 copy-start.12
  165.9 0.9 copy-start.13
  166.9 0.6 copy-start.18
  238.9 2.3 copy-start
  326.3 11.2 %copy-start.19 = (f32[80,128]{1,0:T(8,128)S(1)}, f32[80,128]{1,0:T(8,128)}, u32[]{:S(2)}) copy-start(f32[80,128]{1,0:T(8,128)} %get-tuple-element.59) | copy-start | bytes 122884
  338.1 2.5 copy-start.20

commit v2 on v0

v2 whole, which is shorter than its diff:
```python
import math

import jax
import jax.numpy as jnp
from jax import lax
from jax.experimental import pallas as pl
from jax.experimental.pallas import tpu as pltpu
from jax.sharding import PartitionSpec as P


D = 768
HEADS = 12
ROT = 16
FF = 3072
HALF = 4096
SPANS = 32
LROWS = 192
SROWS = 448
EPS = 1e-05
NEG = -1e30
SMALL = 80
STEPS = 5
BF = jnp.bfloat16
F32 = jnp.float32
MESH = pl.DeviceIdType.MESH
NT = (((1,), (1,)), ((), ()))
TN = (((0,), (0,)), ((), ()))


def mm(a, b):
    return jnp.dot(a, b, preferred_element_type=F32)


def mm_nt(a, b):
    return lax.dot_general(a, b, NT, preferred_element_type=F32)


def mm_tn(a, b):
    return lax.dot_general(a, b, TN, preferred_element_type=F32)


def halves(ref, first_long):
    top, bottom = ref[0:128, :], ref[128:256, :]
    return jnp.concatenate(
        [jnp.where(first_long, top, bottom), jnp.where(first_long, bottom, top)], axis=0
    )


def low_lanes(shape):
    return lax.broadcasted_iota(jnp.int32, shape, 1) < 64


def swap64(v):
    return pltpu.roll(v, 64, 1)


def turn(v, c, s1, s2, sign):
    return v * c + sign * (pltpu.roll(v, 120, 1) * s1 + pltpu.roll(v, 8, 1) * s2)


def role(dp, me):
    shift = 2 * lax.rem(dp, 2) + dp // 2
    y, z, part = me // 8, lax.rem(me // 2, 4), lax.rem(me, 2)
    return y, z, part, shift, lax.rem(z - y - shift + 12, 4)


def walk(y, z, part, i):
    y2 = lax.rem(y + i // 8, 4)
    z2 = lax.rem(z + lax.rem(i // 2, 4), 4)
    p2 = lax.rem(part + lax.rem(i, 2), 2)
    return y2, z2, p2, y2 * 8 + z2 * 2 + p2


def place_id(core, x, y, z):
    return (lax.rem(x, 2) * 2 + core, y * 8 + z * 2 + x // 2)


def cube_partners(dp, blk):
    core = lax.rem(dp, 2)
    at = {"x": lax.rem(blk, 2) * 2 + dp // 2, "y": blk // 8, "z": lax.rem(blk // 2, 4)}
    out = []
    for axis in ("x", "y", "z"):
        v = at[axis]
        hi, lo = v // 2, lax.rem(v, 2)
        for nv, bit in ((v + 1 - 2 * lo, lax.rem(hi + lo, 2)), (3 - v, hi)):
            there = dict(at)
            there[axis] = nv
            out.append((place_id(core, there["x"], there["y"], there["z"]), bit))
    return core, place_id(1 - core, at["x"], at["y"], at["z"]), out


def remote(src, dst, send, recv, d):
    return pltpu.make_async_remote_copy(src, dst, send, recv, device_id=d, device_id_type=MESH)


def sum_stages(rows, cube, f_ref, a_ref, rx0, rxs, rxe, sems, small):
    core_s, core_r, rs_s, rs_r, ex_s, ex_r, ag_s, ag_r, fin_s, fin_r, loc = sems
    part, half_rows, steps = rows // 12, rows // 2, STEPS
    core, other, partners = cube
    base = [pl.multiple_of(core * half_rows + p * part, 16) for p in range(6)]
    obase = [pl.multiple_of((1 - core) * half_rows + p * part, 16) for p in range(6)]

    def add(off, n, src):
        w = 96
        while n % w:
            w //= 2

        @pl.loop(0, n // w)
        def _(i):
            here = pl.ds(pl.multiple_of(off + i * w, 16), w)
            there = pl.ds(pl.multiple_of(i * w, 16), w)
            f_ref[here, :] = (f_ref[here, :].astype(F32) + src[there, :].astype(F32)).astype(BF)

    if small is not None:
        so_ref, srx, sm_s, sm_r = small
        to = [other] + [q[0] for q in partners]

        def small_copy(t):
            return remote(so_ref, srx.at[t], sm_s.at[t], sm_r.at[t], to[t])

    def small_start(t):
        if small is not None:
            small_copy(t).start()

    def small_next(t):
        if small is not None:
            small_copy(t).wait()
            so_ref[...] += srx[t]
            if t < 6:
                small_copy(t + 1).start()

    def landing(ref, p, n):
        return ref.at[p, pl.ds(0, n)]

    pend = [
        remote(f_ref.at[pl.ds(obase[p], part)], landing(rx0, p, part), core_s.at[p], core_r.at[p], other)
        for p in range(6)
    ]
    small_start(0)
    for p in range(6):
        pend[p].start()
    yield
    offs, size = list(base), part
    for t in range(steps):
        h = size // 2
        for p in range(6):
            pend[p].wait_recv()
            add(offs[p], size, (rx0 if t == 0 else rxs[t - 1]).at[p])
            dev, bit = partners[(p + t) % 6]
            out = pl.multiple_of(offs[p] + (1 - bit) * h, 16)
            c = remote(f_ref.at[pl.ds(out, h)], landing(rxs[t], p, h), rs_s.at[t, p], rs_r.at[t, p], dev)
            c.start()
            pend[p].wait_send()
            pend[p] = c
            offs[p] = pl.multiple_of(offs[p] + bit * h, 16)
        small_next(t)
        size = h
        yield
    both = []
    for p in range(6):
        pend[p].wait_recv()
        add(offs[p], size, rxs[steps - 1].at[p])
        here = f_ref.at[pl.ds(offs[p], size)]
        c = remote(here, landing(rxe, p, size), ex_s.at[p], ex_r.at[p], partners[(p + steps) % 6][0])
        c.start()
        pend[p].wait_send()
        both.append(c)
    small_next(steps)
    yield
    own = []
    for p in range(6):
        both[p].wait()
        add(offs[p], size, rxe.at[p])
        here = pl.ds(offs[p], size)
        c = pltpu.make_async_copy(f_ref.at[here], a_ref.at[here], loc.at[p])
        c.start()
        own.append(c)
    for p in range(6):
        own[p].wait()
    prev = [None] * 6
    for t in reversed(range(steps)):
        for p in range(6):
            if prev[p] is not None:
                prev[p].wait()
            dev, bit = partners[(p + t) % 6]
            here = a_ref.at[pl.ds(offs[p], size)]
            prev[p] = remote(here, here, ag_s.at[t, p], ag_r.at[t, p], dev)
            prev[p].start()
            offs[p] = pl.multiple_of(offs[p] - bit * size, 16)
        size *= 2
        yield
    last = []
    for p in range(6):
        prev[p].wait()
        here = a_ref.at[pl.ds(base[p], part)]
        c = remote(here, here, fin_s.at[p], fin_r.at[p], other)
        c.start()
        last.append(c)
    small_next(6)
    yield
    for p in range(6):
        last[p].wait()
    yield


def sine_cosine(angle):
    k = jnp.floor(angle * (2.0 / math.pi) + 0.5)
    r = angle - k * 1.5703125 - k * 4.837512969970703125e-4 - k * 7.54978995489188216e-8
    r2 = r * r
    s = r + r * r2 * (-1.6666654611e-1 + r2 * (8.3321608736e-3 - r2 * 1.9515295891e-4))
    c = 1.0 - 0.5 * r2 + r2 * r2 * (4.166664568298827e-2 + r2 * (-1.388731625493765e-3 + r2 * 2.443315711809948e-5))
    q = k - 4.0 * jnp.floor(k * 0.25)
    odd = (q == 1.0) | (q == 3.0)
    sine = jnp.where(odd, c, s)
    cosine = jnp.where(odd, s, c)
    return jnp.where(q >= 2.0, -sine, sine), jnp.where((q == 1.0) | (q == 2.0), -cosine, cosine)


def gelu_both(u):
    phi = 0.5 * (1.0 + lax.erf(u * (1.0 / math.sqrt(2.0))))
    density = jnp.exp(-0.5 * u * u) * (1.0 / math.sqrt(2.0 * math.pi))
    return u * phi, phi + u * density


def layer_kernel(
    source, order, lens, tok, cot, again, abias, mgain, mbias, bqkv, outb, upb, downb, wqkv_h, wout_h, up_h, down_h,
    mixed_o, tgrad_o, small_o, a_mlp, a_attn,
    wqkv, wout, up, down, tx_l, tx_s, rx_l, rx_s, ret_l, ret_s, ha_r, hm_r, hmt, tabs, branch, dh, ub, grads,
    kv, kvt, qg, qo, dkv, sc, gqkv, att, rx0, rxa, rxb, rxc, rxd, rxf, rxe, srx,
    wq_sem, wo_sem, up_sem, dn_sem, e1_s, e1_r, e2_s, e2_r, sm_s, sm_r, *sum_sems,
):
    dp, me = lax.axis_index("dp"), lax.axis_index("blk")
    y, z, part, shift, mine = role(dp, me)
    is_short, is_long = mine == 3, mine != 3
    cube = cube_partners(dp, me)
    sems_m, sems_a = sum_sems[:11], sum_sems[11:]
    rxs = [rxa, rxb, rxc, rxd, rxf]

    def f(v):
        return v.astype(F32)

    bar = pltpu.get_barrier_semaphore()

    @pl.loop(1, 32)
    def _(i):
        pl.semaphore_signal(bar, inc=1, device_id=(dp, lax.rem(me + i, 32)), device_id_type=MESH)

    for d in [cube[1], cube[2][0][0], cube[2][1][0]]:
        pl.semaphore_signal(bar, inc=1, device_id=d, device_id_type=MESH)

    def qkv_copy(c):
        cols = pl.ds(256 * c, 256)
        return pltpu.make_async_copy(wqkv_h.at[:, cols], wqkv.at[:, cols], wq_sem.at[c])

    out_copy = pltpu.make_async_copy(wout_h, wout, wo_sem)

    def ff_copies(i, slot):
        cols = pl.ds(pl.multiple_of(512 * i, 512), 512)
        return (
            pltpu.make_async_copy(up_h.at[:, cols], up.at[slot], up_sem.at[slot]),
            pltpu.make_async_copy(down_h.at[cols, :], down.at[slot], dn_sem.at[slot]),
        )

    for wide in range(3):
        for kind in range(3):
            qkv_copy(3 * kind + wide).start()
    out_copy.start()
    for i in range(3):
        for c in ff_copies(i, i):
            c.start()

    first_long = lens[0, 0] > 512

    def span_of(i):
        a = order[0, 2 * i]
        return jnp.where(first_long, a, 31 - a)

    def begin_of(place):
        end = jnp.int32(0)
        begin = jnp.zeros_like(place)
        for j in range(15):
            end = end + jnp.where(first_long, lens[0, j + 1], lens[0, j])
            begin = jnp.maximum(begin, jnp.where(end <= place, end, 0))
        return begin

    own_span = span_of(me)
    row = lax.broadcasted_iota(jnp.int32, (128, 128), 0)
    lane = lax.broadcasted_iota(jnp.int32, (256, 128), 1)
    short_place = (31 - own_span) * 128 + row
    position = jnp.concatenate([own_span * 128 + row, short_place - begin_of(short_place)], axis=0)
    dim = lax.rem(lane, 64)
    step = lax.rem(lane, 8)
    inverse = jnp.full((256, 128), 1.0, F32)
    for j in range(1, 8):
        inverse = jnp.where(step == j, 10000.0 ** (-2.0 * j / ROT), inverse)
    sine, cosine = sine_cosine(f(position) * inverse)
    tabs[0] = jnp.where(dim < ROT, cosine, 1.0)
    tabs[1] = jnp.where(dim < ROT // 2, -sine, 0.0)
    tabs[2] = jnp.where((dim >= ROT // 2) & (dim < ROT), sine, 0.0)
    low = lane < 64

    def norm_parts():
        x = f(halves(tok, first_long))
        center = x - jnp.mean(x, axis=-1, keepdims=True)
        r = lax.rsqrt(jnp.mean(center * center, axis=-1, keepdims=True) + EPS)
        return x, center * r, r

    unused_x, znorm, unused_r = norm_parts()
    ha_r[...] = (znorm * f(again[...]) + f(abias[...])).astype(BF)
    hm_r[...] = (znorm * f(mgain[...]) + f(mbias[...])).astype(BF)
    dyb = halves(cot, first_long)
    ha = ha_r[...]

    def put(head, kvb, qgb):
        tx_l[2 * head, 0:128, :] = kvb[0:128]
        tx_l[2 * head + 1, 0:128, :] = kvb[0:128]
        tx_l[2 * head, 128:192, :] = qgb[0:64]
        tx_l[2 * head + 1, 128:192, :] = qgb[64:128]
        pair, kind = head // 3, head % 3
        if kind == 1:
            for p in range(2):
                tx_s[2 * pair + p, 256:384, :] = kvb[128:256]
                tx_s[2 * pair + p, 384:448, :] = qgb[128 + 64 * p : 192 + 64 * p]
        else:
            slot = 2 * pair + kind // 2
            tx_s[slot, 0:128, :] = kvb[128:256]
            tx_s[slot, 128:256, :] = qgb[128:256]

    for wide in range(3):
        for kind in range(3):
            qkv_copy(3 * kind + wide).wait()
        if wide == 0:
            out_copy.wait()
        q2, k2, v2 = [
            mm(ha, wqkv[:, 768 * kind + 256 * wide : 768 * kind + 256 * wide + 256])
            + f(bqkv[:, 768 * kind + 256 * wide : 768 * kind + 256 * wide + 256])
            for kind in range(3)
        ]
        g2 = mm_nt(dyb, wout[256 * wide : 256 * wide + 256, :])
        for b in range(2):
            lanes = slice(128 * b, 128 * b + 128)
            q = f(turn(q2[:, lanes], tabs[0], tabs[1], tabs[2], 1.0).astype(BF)) * 0.125
            k = turn(k2[:, lanes], tabs[0], tabs[1], tabs[2], 1.0)
            v, g = v2[:, lanes], g2[:, lanes]
            head = 4 * wide + 2 * b
            put(head, jnp.where(low, k, swap64(v)).astype(BF), jnp.where(low, q, swap64(g)).astype(BF))
            put(head + 1, jnp.where(low, swap64(k), v).astype(BF), jnp.where(low, swap64(q), g).astype(BF))

    pl.semaphore_wait(bar, 34)

    def there(i, run):
        y2, z2, p2, d = walk(y, z, part, i)
        q = lax.rem(z2 - y2 - shift + 12, 4)

        @pl.when(q == 3)
        def _():
            run(tx_s.at[y2 * 2 + p2], rx_s.at[me], e1_r.at[1], d)

        @pl.when(q != 3)
        def _():
            run(tx_l.at[(y2 * 3 + q) * 2 + p2], rx_l.at[me], e1_r.at[0], d)

    there(0, lambda src, dst, sem, d: pltpu.make_async_copy(src, dst, sem).start())

    @pl.loop(1, 32)
    def _(i):
        there(i, lambda src, dst, sem, d: remote(src, dst, e1_s.at[i], sem, (dp, d)).start())

    hmt[...] = f(hm_r[...]).T.astype(BF)
    dh[...] = jnp.zeros_like(dh)
    branch[...] = jnp.broadcast_to(f(downb[...]), branch.shape)

    @pl.loop(0, 6)
    def _(i):
        slot = lax.rem(i, 3)
        for c in ff_copies(i, slot):
            c.wait()
        u = mm(hm_r[...], up[slot]) + f(upb[:, pl.ds(pl.multiple_of(512 * i, 512), 512)])
        value, slope = gelu_both(u)
        hid = value.astype(BF)
        branch[...] += mm(hid, down[slot])
        gub = (mm_nt(halves(cot, first_long), down[slot]) * slope).astype(BF)
        sums = jnp.sum(f(gub), axis=0, keepdims=True)
        for c in range(4):
            ub[pl.ds(4 * i + c, 1), :] = sums[:, 128 * c : 128 * c + 128]
        dh[...] += mm_nt(gub, up[slot])
        gup = mm(hmt[...], gub).astype(BF)
        at = pl.multiple_of(6144 * i, 512)
        for c in range(4):
            grads[pl.ds(at + 768 * c, 768), :] = gup[:, 128 * c : 128 * c + 128]
        gdown = mm_tn(hid, halves(cot, first_long)).astype(BF)
        for c in range(6):
            grads[pl.ds(at + 3072 + 512 * c, 512), :] = gdown[:, 128 * c : 128 * c + 128]

        @pl.when(i < 3)
        def _():
            for c in ff_copies(i + 3, slot):
                c.start()

    sum_mlp = sum_stages(36864, cube, grads, a_mlp, rx0, rxs, rxe, sems_m, None)
    next(sum_mlp)

    def fold(v, op):
        return op(v.reshape(v.shape[0] // 8, 8, v.shape[1]), axis=0)

    lowq = low_lanes((256, 128))

    def load_tile(at):
        tile = qg[pl.ds(pl.multiple_of(at, 256), 256), :]
        zero = jnp.zeros_like(tile)
        gt = f(tile).T[64:128]
        return jnp.where(lowq, tile, zero), jnp.where(lowq, zero, tile), gt

    def store_tile(at, dqt, ot):
        both = jnp.concatenate([dqt * 0.125, ot], axis=0)
        qo[pl.ds(at // 64, 4)] = both.T.astype(BF).reshape(4, 64, 128)

    def key_rows(start, n):
        return lax.broadcasted_iota(jnp.int32, (n, 256), 0) + start

    def strided_places(t):
        col = lax.broadcasted_iota(jnp.int32, (1, 256), 1)
        return (4 * t + col // 64) * 128 + 64 * part + lax.rem(col, 64)

    def get_keys(ref, at, rows, flip):
        @pl.loop(0, 32)
        def _(i):
            src = source[31 - i] if flip else source[i]
            kv[pl.ds(pl.multiple_of(i * 128, 128), 128), :] = ref[src, at : at + 128, :]
            qg[pl.ds(pl.multiple_of(i * rows, rows), rows), :] = ref[src, at + 128 : at + 128 + rows, :]

        @pl.loop(0, 32)
        def _(i):
            block = pl.ds(pl.multiple_of(i * 128, 128), 128)
            kvt[:, block] = f(kv[block, :]).T.astype(BF)

        dkv[...] = jnp.zeros_like(dkv)

    def put_back(ref, at, rows, flip):
        @pl.loop(0, 32)
        def _(i):
            rel = 31 - span_of(i) if flip else span_of(i)
            ref[i, at : at + 128, :] = dkv[rel].astype(BF)
            if rows == 64:
                ref[i, at + 128 : at + 192, :] = qo[rel]
            else:
                ref[i, at + 128 : at + 192, :] = qo[2 * rel]
                ref[i, at + 192 : at + 256, :] = qo[2 * rel + 1]

    def long_tile(t):
        qz, zg, gt = load_tile(t * 256)

        def chunk(c):
            return pl.ds(pl.multiple_of(c * 512, 512), 512)

        def score(c, m8):
            s = mm_nt(kv[chunk(c), :], qz)
            sc[chunk(c), :] = s
            return jnp.maximum(m8, fold(s, jnp.max))

        m8 = lax.fori_loop(0, t, score, jnp.full((8, 256), NEG, F32))
        s = mm_nt(kv[chunk(t), :], qz)
        s = jnp.where(key_rows(t * 512, 512) <= strided_places(t), s, NEG)
        sc[chunk(t), :] = s
        m8 = jnp.maximum(m8, fold(s, jnp.max))
        m = jnp.max(m8, axis=0, keepdims=True)

        def weigh(c, carry):
            l8, ot = carry
            p = jnp.exp(sc[chunk(c), :] - m)
            return l8 + fold(p, jnp.sum), ot + mm(kvt[64:128, chunk(c)], p.astype(BF))

        l8, ot = lax.fori_loop(
            0, t + 1, weigh, (jnp.zeros((8, 256), F32), jnp.zeros((64, 256), F32))
        )
        total = jnp.sum(l8, axis=0, keepdims=True)
        ot = ot * (1.0 / total)
        lse = m + jnp.log(total)
        delta = jnp.sum(gt * ot, axis=0, keepdims=True)

        def back(c, dqt):
            p = jnp.exp(sc[chunk(c), :] - lse)
            ds = (p * (mm_nt(kv[chunk(c), :], zg) - delta)).astype(BF)
            dkv[pl.ds(4 * c, 4)] += (mm(ds, qz) + mm(p.astype(BF), zg)).reshape(4, 128, 128)
            return dqt + mm(kvt[0:64, chunk(c)], ds)

        dqt = lax.fori_loop(0, t + 1, back, jnp.zeros((64, 256), F32))
        store_tile(t * 256, dqt, ot)

    def short_tile(at, start, n, places):
        qz, zg, gt = load_tile(at)
        keys = pl.ds(pl.multiple_of(start, 256), n)
        k = kv[keys, :]
        place = key_rows(start, n)
        s = jnp.where((place <= places) & (place >= begin_of(places)), mm_nt(k, qz), NEG)
        m = jnp.max(fold(s, jnp.max), axis=0, keepdims=True)
        e = jnp.exp(s - m)
        inv = 1.0 / jnp.sum(fold(e, jnp.sum), axis=0, keepdims=True)
        p = e * inv
        pb = p.astype(BF)
        ot = mm(kvt[64:128, keys], pb)
        delta = jnp.sum(gt * ot, axis=0, keepdims=True)
        ds = (p * (mm_nt(k, zg) - delta)).astype(BF)
        dkv[pl.ds(start // 128, n // 128)] += (mm(ds, qz) + mm(pb, zg)).reshape(n // 128, 128, 128)
        dqt = mm(kvt[0:64, keys], ds)
        store_tile(at, dqt, ot)

    def full_tile(t):
        places = lax.broadcasted_iota(jnp.int32, (1, 256), 1) + 256 * t
        short_tile(t * 256, 256 * (t - 2) * ((t + 14) // 16), 768, places)

    def half_tile(t):
        short_tile(t * 256, 512 * (t - 1) * ((t + 7) // 8), 1024, strided_places(t))

    def tiles(lo, hi, body):
        pl.loop(lo, hi)(body)

    long_at = [0, 3, 5, 6, 7, 8]
    short_at = [0, 5, 10, 16]
    half_at = [0, 4, 8]
    for slot in range(5):
        @pl.when(is_long)
        def _():
            if slot == 0:
                pltpu.make_async_copy(rx_l, rx_l, e1_r.at[0]).wait()
                get_keys(rx_l, 0, 64, False)
            tiles(long_at[slot], long_at[slot + 1], long_tile)
            if slot == 4:
                put_back(rx_l, 0, 64, False)

        @pl.when(is_short)
        def _():
            if slot == 0:
                pltpu.make_async_copy(rx_s, rx_s, e1_r.at[1]).wait()
                get_keys(rx_s, 0, 128, True)
            if slot < 3:
                tiles(short_at[slot], short_at[slot + 1], full_tile)
                if slot == 2:
                    put_back(rx_s, 0, 128, True)
                    get_keys(rx_s, 256, 64, True)
            else:
                tiles(half_at[slot - 3], half_at[slot - 2], half_tile)
                if slot == 4:
                    put_back(rx_s, 256, 64, True)

        next(sum_mlp)

    def home(i, run):
        d = walk(y, z, part, i)[3]

        @pl.when(is_short)
        def _():
            run(rx_s.at[d], ret_s.at[y * 2 + part], e2_r.at[1], d)

        @pl.when(is_long)
        def _():
            run(rx_l.at[d], ret_l.at[(y * 3 + mine) * 2 + part], e2_r.at[0], d)

    home(0, lambda src, dst, sem, d: pltpu.make_async_copy(src, dst, sem).start())

    @pl.loop(1, 32)
    def _(i):
        home(i, lambda src, dst, sem, d: remote(src, dst, e2_s.at[i], sem, (dp, d)).start())

    for unused in sum_mlp:
        pass
    pltpu.make_async_copy(ret_s, ret_s, e2_r.at[1]).wait()
    pltpu.make_async_copy(ret_l, ret_l, e2_r.at[0]).wait()

    def gather(head):
        pair, kind = head // 3, head % 3
        kv_l = f(ret_l[2 * head, 0:128, :]) + f(ret_l[2 * head + 1, 0:128, :])
        qo_l = [f(ret_l[2 * head, 128:192, :]), f(ret_l[2 * head + 1, 128:192, :])]
        if kind == 1:
            kv_s = f(ret_s[2 * pair, 256:384, :]) + f(ret_s[2 * pair + 1, 256:384, :])
            qo_s = [f(ret_s[2 * pair, 384:448, :]), f(ret_s[2 * pair + 1, 384:448, :])]
        else:
            slot = 2 * pair + kind // 2
            kv_s = f(ret_s[slot, 0:128, :])
            qo_s = [f(ret_s[slot, 128:256, :])]
        return jnp.concatenate([kv_l, kv_s], axis=0), jnp.concatenate(qo_l + qo_s, axis=0)

    for j in range(6):
        kv_a, qo_a = gather(2 * j)
        kv_b, qo_b = gather(2 * j + 1)
        dq = jnp.where(low, qo_a, swap64(qo_b))
        ov = jnp.where(low, swap64(qo_a), qo_b)
        dk = jnp.where(low, kv_a, swap64(kv_b))
        dv = jnp.where(low, swap64(kv_a), kv_b)
        cols = slice(128 * j, 128 * j + 128)
        att[:, cols] = ov.astype(BF)
        gqkv[:, cols] = turn(dq, tabs[0], tabs[1], tabs[2], -1.0).astype(BF)
        gqkv[:, 768 + 128 * j : 896 + 128 * j] = turn(dk, tabs[0], tabs[1], tabs[2], -1.0).astype(BF)
        gqkv[:, 1536 + 128 * j : 1664 + 128 * j] = dv.astype(BF)

    def rows(v, at, n):
        for c in range(n):
            small_o[at + c : at + c + 1, :] = v[:, 128 * c : 128 * c + 128]

    def square(v, at):
        s = jnp.sum(v * v, axis=0, keepdims=True)
        t = s[:, 0:128]
        for c in range(1, 6):
            t = t + s[:, 128 * c : 128 * c + 128]
        small_o[at : at + 1, :] = t

    def put_rows(ref, v):
        ref[0:128, :] = jnp.where(first_long, v[0:128], v[128:256])
        ref[128:256, :] = jnp.where(first_long, v[128:256], v[0:128])

    attT = f(att[...]).T.astype(BF)
    haT = f(ha_r[...]).T.astype(BF)
    dy_b = halves(cot, first_long)
    for w in range(3):
        t = mm(attT, dy_b[:, 256 * w : 256 * w + 256]).astype(BF)
        for b in range(2):
            grads[768 * (18 + 2 * w + b) : 768 * (19 + 2 * w + b), :] = t[:, 128 * b : 128 * b + 128]
    d_attn = jnp.zeros((256, D), F32)
    for w in range(9):
        cols = slice(256 * w, 256 * w + 256)
        piece = gqkv[:, cols]
        rows(jnp.sum(f(piece), axis=0, keepdims=True), 24 + 2 * w, 2)
        t = mm(haT, piece).astype(BF)
        for b in range(2):
            grads[768 * (2 * w + b) : 768 * (2 * w + b + 1), :] = t[:, 128 * b : 128 * b + 128]
        d_attn = d_attn + mm_nt(piece, wqkv[:, cols])

    x, znorm, r = norm_parts()
    dy = f(dy_b)
    attn = mm(att[...], wout[...]) + f(outb[...])
    out = x + attn + branch[...]
    put_rows(mixed_o, out.astype(BF))
    small_o[72:80, :] = jnp.zeros((8, 128), F32)
    square(out, 72)
    square(attn, 73)
    square(branch[...], 74)
    rows(jnp.sum(dy, axis=0, keepdims=True), 42, 6)
    small_o[48:72, :] = ub[...]

    def norm_back(d, gain, at):
        rows(jnp.sum(d * znorm, axis=0, keepdims=True), at, 6)
        rows(jnp.sum(d, axis=0, keepdims=True), at + 6, 6)
        e = d * f(gain[...])
        return r * (
            e - jnp.mean(e, axis=-1, keepdims=True) - znorm * jnp.mean(e * znorm, axis=-1, keepdims=True)
        )

    put_rows(tgrad_o, dy + norm_back(d_attn, again, 0) + norm_back(dh[...], mgain, 12))

    for unused in sum_stages(
        18432, cube, grads, a_attn, rx0, rxs, rxe, sems_a, (small_o, srx, sm_s, sm_r)
    ):
        pass

    @pl.loop(1, 32)
    def _(i):
        there(i, lambda src, dst, sem, d: remote(src, dst, e1_s.at[i], sem, (dp, d)).wait_send())
        home(i, lambda src, dst, sem, d: remote(src, dst, e2_s.at[i], sem, (dp, d)).wait_send())


def layer_call(*args):
    def vm(n):
        return [pl.BlockSpec(memory_space=pltpu.VMEM)] * n

    def vb(*shape):
        return pltpu.VMEM(shape, BF)

    def vf(*shape):
        return pltpu.VMEM(shape, F32)

    dma = pltpu.SemaphoreType.DMA
    sum_sems = [dma((6,)), dma((6,)), dma((STEPS, 6)), dma((STEPS, 6)), dma((6,)), dma((6,))]
    sum_sems += [dma((STEPS, 6)), dma((STEPS, 6)), dma((6,)), dma((6,)), dma((6,))]
    anywhere = pl.BlockSpec(memory_space=pl.ANY)
    return pl.pallas_call(
        layer_kernel,
        out_shape=(
            jax.ShapeDtypeStruct((256, D), BF),
            jax.ShapeDtypeStruct((256, D), F32),
            jax.ShapeDtypeStruct((SMALL, 128), F32),
            jax.ShapeDtypeStruct((36864, 128), BF),
            jax.ShapeDtypeStruct((18432, 128), BF),
        ),
        in_specs=[pl.BlockSpec(memory_space=pltpu.SMEM)] * 3 + vm(10) + [anywhere] * 4,
        out_specs=vm(3) + [anywhere] * 2,
        scratch_shapes=[
            vb(D, 3 * D), vb(D, D), vb(3, D, 512), vb(3, 512, D),
            vb(24, LROWS, 128), vb(8, SROWS, 128), vb(32, LROWS, 128), vb(32, SROWS, 128),
            vb(24, LROWS, 128), vb(8, SROWS, 128),
            vb(256, D), vb(256, D), vb(D, 256), vf(3, 256, 128), vf(256, D), vf(256, D), vf(24, 128),
            vb(36864, 128),
            vb(HALF, 128), vb(128, HALF), vb(HALF, 128), vb(64, 64, 128), vf(32, 128, 128), vf(HALF, 256),
            vb(256, 3 * D), vb(256, D),
            vb(6, 3072, 128),
        ]
        + [vb(6, 3072 >> (t + 1), 128) for t in range(STEPS)]
        + [vb(6, 3072 >> STEPS, 128), vf(7, SMALL, 128)]
        + [dma((9,)), dma, dma((3,)), dma((3,)), dma((32,)), dma((2,)), dma((32,)), dma((2,)), dma((7,)), dma((7,))]
        + sum_sems * 2,
        compiler_params=pltpu.CompilerParams(
            collective_id=0, has_side_effects=True, vmem_limit_bytes=62 << 20
        ),
    )(*args)


def unpack_mlp_kernel(a, up_o, down_o):
    for c in range(4):
        up_o[:, 128 * c : 128 * c + 128] = a[768 * c : 768 * c + 768, :].astype(F32)
    for c in range(6):
        down_o[:, 128 * c : 128 * c + 128] = a[3072 + 512 * c : 3584 + 512 * c, :].astype(F32)


def unpack_mlp(a):
    return pl.pallas_call(
        unpack_mlp_kernel,
        grid=(6,),
        out_shape=(jax.ShapeDtypeStruct((D, FF), F32), jax.ShapeDtypeStruct((FF, D), F32)),
        in_specs=[pl.BlockSpec((6144, 128), lambda i: (i, 0))],
        out_specs=[pl.BlockSpec((D, 512), lambda i: (0, i)), pl.BlockSpec((512, D), lambda i: (i, 0))],
        compiler_params=pltpu.CompilerParams(vmem_limit_bytes=48 << 20),
    )(a)


def unpack_attn_kernel(a, b, qkv_o, out_o):
    for c in range(6):
        qkv_o[:, 128 * c : 128 * c + 128] = a[768 * c : 768 * c + 768, :].astype(F32)
    for c in range(2):
        out_o[:, 128 * c : 128 * c + 128] = b[768 * c : 768 * c + 768, :].astype(F32)


def unpack_attn(a):
    return pl.pallas_call(
        unpack_attn_kernel,
        grid=(3,),
        out_shape=(jax.ShapeDtypeStruct((D, 3 * D), F32), jax.ShapeDtypeStruct((D, D), F32)),
        in_specs=[
            pl.BlockSpec((4608, 128), lambda i: (i, 0)),
            pl.BlockSpec((1536, 128), lambda i: (9 + i, 0)),
        ],
        out_specs=[pl.BlockSpec((D, 768), lambda i: (0, i)), pl.BlockSpec((D, 256), lambda i: (0, i))],
        compiler_params=pltpu.CompilerParams(vmem_limit_bytes=48 << 20),
    )(a, a)


def on_device(tokens, attn_gain, attn_bias, mlp_gain, mlp_bias, qkv_weight, qkv_bias, out_weight, out_bias,
              up_weight, up_bias, down_weight, down_bias, cotangent, doc_lengths, span_order):
    first_long = doc_lengths[0, 0] > 512
    spans = span_order.reshape(SPANS, 2)[:, 0]
    long_span = jnp.where(first_long, spans, 31 - spans)
    index = jnp.arange(SPANS, dtype=jnp.int32)
    source = jnp.sum(jnp.where(long_span[None, :] == index[:, None], index[None, :], 0), axis=1)
    vectors = (attn_gain, attn_bias, mlp_gain, mlp_bias, qkv_bias, out_bias, up_bias, down_bias)
    mixed, tokens_grad, small_sum, mlp_sum, attn_sum = layer_call(
        source, span_order, doc_lengths, tokens, cotangent, *[v.reshape(1, -1) for v in vectors],
        qkv_weight, out_weight, up_weight, down_weight,
    )
    grad_up, grad_down = unpack_mlp(mlp_sum)
    grad_qkv, grad_out = unpack_attn(attn_sum)

    def vector(at, n):
        return small_sum[at : at + n].reshape(128 * n)

    roots = jnp.sqrt(jnp.sum(small_sum[72:75], axis=1) / (D * 256 * 128))
    branch_bias = vector(42, 6)
    return (
        mixed, tokens_grad, vector(0, 6), vector(6, 6), vector(12, 6), vector(18, 6), grad_qkv, vector(24, 18),
        grad_out, branch_bias, grad_up, vector(48, 24), grad_down, branch_bias, roots[0], roots[1], roots[2],
    )


def solution(mesh):
    rows, split = P(("dp", "blk"), None), P("dp", None)
    return jax.shard_map(
        on_device,
        mesh=mesh,
        in_specs=(rows,) + (P(),) * 12 + (rows, split, split),
        out_specs=(rows, rows) + (P(),) * 15,
        check_vma=False,
    )
```

time: 2770 us -> 259 us (0.09)
  waiting for transfers between devices: 1420 us -> 0 us
  matrix products: 716 us -> 0 us
  Pallas kernels: 0 us -> 237 us
  other arithmetic: 227 us -> 2.75 us
  local copies, waits for them, and re-layouts: 225 us -> 17.8 us
  blocking collectives: 93.6 us -> 0 us
    ppermute x126 -> x0, waiting for transfers between devices: 1080 us -> none  [from_behind(): return lax.ppermute(block, axis, route)]
    dot_general x236 -> x0, matrix products: 716 us -> none  [the longest x64 229 us: score_block(): jnp.einsum('qhd,khd->hqk', query_part, key_part, preferred_element_type=j...]
    pallas_call x0 -> x3, Pallas kernels: none -> 237 us  [the longest x1 222 us: layer_call(): pl.pallas_call(layer_kernel, out_shape=(jax.ShapeDtypeStruct((256, D), BF...]
    all_gather x2 -> x0, waiting for transfers between devices: 189 us -> none  [the longest x1 115 us: on_device(): lax.all_gather(key_b, 'blk', axis=0, tiled=True)]
    psum x1 -> x0, waiting for transfers between devices: 151 us -> none  [on_device(): lax.psum((grad_attn_gain, grad_attn_bias, grad_mlp_gain, grad_mlp_bias, g...]
    reduce_sum x149 -> x2, other arithmetic: 144 us -> 1.41 us  [the longest x1 0.79 us: on_device(): roots = jnp.sqrt(jnp.sum(small_sum[72:75], axis=1) / (D * 256 * 128))]
    while x836 -> x0, local copies, waits for them, and re-layouts: 132 us -> none
    psum x1 -> x0, blocking collectives: 93.6 us -> none  [on_device(): lax.psum((grad_attn_gain, grad_attn_bias, grad_mlp_gain, grad_mlp_bias, g...]
  transfers between devices with their start and end apart: 129 -> 0, of which waited for: 129 -> 0; matrix products, arithmetic and copies ran while one was open for 19% -> 0% of each run, Pallas kernels for 0% -> 0%
where the time goes in v2:
time: 259 us
  Pallas kernels  237 us (92%)
  local copies, waits for them, and re-layouts  17.8 us (7%)
  other arithmetic  2.75 us (1%)
    pallas_call x1, Pallas kernels, layer_call(): pl.pallas_call(layer_kernel, out_shape=(jax.ShapeDtypeStruct((256, D), BF...  222 us
    pallas_call x1, Pallas kernels, unpack_mlp(): pl.pallas_call(unpack_mlp_kernel, grid=(6,), out_shape=(jax.ShapeDtypeStr...  11.2 us
    reshape x8, local copies, waits for them, and re-layouts, on_device(): v.reshape(1, -1)  10.2 us

profile of v2, /device:TPU:1, one launch (start us, length us, event | category | flops | bytes accessed | tf_op | source)
XLA Modules:
  0.0 258.6 jit_solution(12236325542105731504)
XLA Ops:
  0.7 0.5 broadcast.18
  1.2 1.3 reduce.5
  2.5 0.1 reshape.93
  2.6 0.1 slice_reduce_fusion
  3.4 0.6 select_reduce_fusion.source
  4.0 1.3 reshape.100.upb
  5.3 1.3 reshape.98.bqkv
  6.6 1.3 reshape.101.downb
  7.9 1.3 reshape.94.again
  9.1 1.3 reshape.95.abias
  10.4 1.3 reshape.96.mgain
  11.6 1.3 reshape.97.mbias
  12.9 1.3 reshape.99.outb
  14.2 221.6 %shard_map.287 = (bf16[256,768]{1,0:T(8,128)(2,1)}, f32[256,768]{1,0:T(8,128)}, f32[80,128]{1,0:T(8,128)}, bf16[36864,128]{1,0:T(8,128)(2,1)}, bf16[18432,128]{1,0:T(8,128)(2,1)}) custom-call(s32[32]{0:T(128)} %select_reduce_fusion.source, s32[1,64]{1,0:T(1,128)} %order.1, s32[1,16]{1,0:T(1,128)} %lens.1, bf16[256,768]{1,0:T(8,128)(2,1)} %tok.1, ...), custom_call_target="tpu_custom_call" | custom-call | tf_op jit(solution)/shard_map/pallas_call | solution.py:675
  235.8 0.0 slice-start
  235.8 1.5 slice_bitcast_fusion.2
  237.3 0.0 copy-start.2
  237.3 0.8 slice_reduce_fusion.1
  238.1 0.6 fusion
  238.7 1.3 slice_bitcast_fusion
  240.0 1.3 slice_bitcast_fusion.1
  241.3 0.0 slice-start.1
  241.3 11.2 %shard_map.289 = (f32[768,3072]{1,0:T(8,128)}, f32[3072,768]{1,0:T(8,128)}) custom-call(bf16[36864,128]{1,0:T(8,128)(2,1)} %get-tuple-element.32.a), custom_call_target="tpu_custom_call" | custom-call | tf_op jit(solution)/shard_map/pallas_call | solution.py:714
  252.5 0.0 slice-done
  252.5 0.0 slice-done.1
  252.5 0.0 copy-start.1
  252.5 0.0 copy-start
  252.5 3.8 %shard_map.288 = (f32[768,2304]{1,0:T(8,128)}, f32[768,768]{1,0:T(8,128)}) custom-call(bf16[18432,128]{1,0:T(8,128)(2,1)S(1)} %bitcast.20, bf16[18432,128]{1,0:T(8,128)(2,1)S(1)} %bitcast.20), custom_call_target="tpu_custom_call" | custom-call | tf_op jit(solution)/shard_map/pallas_call | solution.py:732
  256.3 0.0 copy-done.2
  256.4 0.6 copy.36
  256.9 0.0 copy-done.1
  256.9 0.7 copy.37
  257.7 0.0 copy-done
  257.7 0.9 copy.38
  (3 shorter events, 0.0 us)
Async XLA Ops:
  235.8 16.7 %slice-start = ((s8[4718592]{0:T(1024)(128)(4,1)}), s8[4194304]{0:T(1024)(128)(4,1)S(1)}, s32[]{:S(2)}) async-start(s8[4718592]{0:T(1024)(128)(4,1)} %bitcast.19), calls=%async_computation | async-start | bytes 8388608
  237.3 19.1 %copy-start.2 = (f32[768]{0:T(1024)}, f32[768]{0:T(1024)S(1)}, u32[]{:S(2)}) copy-start(f32[768]{0:T(1024)S(1)} %get-tuple-element.103) | copy-start | bytes 9220
  241.3 11.2 %slice-start.1 = ((s8[4718592]{0:T(1024)(128)(4,1)}), s8[524288]{0:T(1024)(128)(4,1)S(1)}, s32[]{:S(2)}) async-start(s8[4718592]{0:T(1024)(128)(4,1)} %bitcast.19), calls=%async_computation.1 | async-start | bytes 1048576
  252.5 4.5 %copy-start.1 = (bf16[256,768]{1,0:T(8,128)(2,1)S(1)}, bf16[256,768]{1,0:T(8,128)(2,1)}, u32[]{:S(2)}) copy-start(bf16[256,768]{1,0:T(8,128)(2,1)} %get-tuple-element.94) | copy-start | bytes 1179652
  252.5 5.2 %copy-start = (f32[256,768]{1,0:T(8,128)S(1)}, f32[256,768]{1,0:T(8,128)}, u32[]{:S(2)}) copy-start(f32[256,768]{1,0:T(8,128)} %get-tuple-element.95) | copy-start | bytes 2359300

commit v3 on v2

--- a/solution.py
+++ b/solution.py
@@ -14,8 +14,6 @@
 FF = 3072
 HALF = 4096
 SPANS = 32
-LROWS = 192
-SROWS = 448
 EPS = 1e-05
 NEG = -1e30
 SMALL = 80
@@ -44,6 +42,10 @@
     return jnp.concatenate(
         [jnp.where(first_long, top, bottom), jnp.where(first_long, bottom, top)], axis=0
     )
+
+
+def line(ref):
+    return ref[...].astype(F32).reshape(1, -1)
 
 
 def low_lanes(shape):
@@ -118,10 +120,6 @@
         def small_copy(t):
             return remote(so_ref, srx.at[t], sm_s.at[t], sm_r.at[t], to[t])
 
-    def small_start(t):
-        if small is not None:
-            small_copy(t).start()
-
     def small_next(t):
         if small is not None:
             small_copy(t).wait()
@@ -136,10 +134,11 @@
         remote(f_ref.at[pl.ds(obase[p], part)], landing(rx0, p, part), core_s.at[p], core_r.at[p], other)
         for p in range(6)
     ]
-    small_start(0)
     for p in range(6):
         pend[p].start()
     yield
+    if small is not None:
+        small_copy(0).start()
     offs, size = list(base), part
     for t in range(steps):
         h = size // 2
@@ -187,6 +186,8 @@
             prev[p] = remote(here, here, ag_s.at[t, p], ag_r.at[t, p], dev)
             prev[p].start()
             offs[p] = pl.multiple_of(offs[p] - bit * size, 16)
+        if t == steps - 1:
+            small_next(6)
         size *= 2
         yield
     last = []
@@ -196,7 +197,6 @@
         c = remote(here, here, fin_s.at[p], fin_r.at[p], other)
         c.start()
         last.append(c)
-    small_next(6)
     yield
     for p in range(6):
         last[p].wait()
@@ -223,11 +223,12 @@
 
 
 def layer_kernel(
-    source, order, lens, tok, cot, again, abias, mgain, mbias, bqkv, outb, upb, downb, wqkv_h, wout_h, up_h, down_h,
+    order, lens, tok, cot, again, abias, mgain, mbias, bqkv, outb, upb, downb, wqkv_h, wout_h, up_h, down_h,
     mixed_o, tgrad_o, small_o, a_mlp, a_attn,
-    wqkv, wout, up, down, tx_l, tx_s, rx_l, rx_s, ret_l, ret_s, ha_r, hm_r, hmt, tabs, branch, dh, ub, grads,
-    kv, kvt, qg, qo, dkv, sc, gqkv, att, rx0, rxa, rxb, rxc, rxd, rxf, rxe, srx,
-    wq_sem, wo_sem, up_sem, dn_sem, e1_s, e1_r, e2_s, e2_r, sm_s, sm_r, *sum_sems,
+    source, wqkv, wout, up, down, tx_l, tx_a, tx_b, rx_l, rx_a, rx_b, ret_l, ret_a, ret_b,
+    ha_r, hm_r, hmt, tabs, branch, dh, zn, rn, ub, ubias, grads,
+    kv, kvt, qg, qo, dkv, sc, gqkv, att, rx0, rx1, rxa, rxb, rxc, rxd, rxf, rxe, srx,
+    wq_sem, wo_sem, up_sem, dn_sem, e1_s, e1b_s, e1_r, e2_s, e2a_s, e2_r, sm_s, sm_r, *sum_sems,
 ):
     dp, me = lax.axis_index("dp"), lax.axis_index("blk")
     y, z, part, shift, mine = role(dp, me)
@@ -306,8 +307,11 @@
         return x, center * r, r
 
     unused_x, znorm, unused_r = norm_parts()
-    ha_r[...] = (znorm * f(again[...]) + f(abias[...])).astype(BF)
-    hm_r[...] = (znorm * f(mgain[...]) + f(mbias[...])).astype(BF)
+    ha_r[...] = (znorm * line(again) + line(abias)).astype(BF)
+    hm_r[...] = (znorm * line(mgain) + line(mbias)).astype(BF)
+    bq, bu = line(bqkv), line(upb)
+    for i in range(6):
+        ubias[i : i + 1, :] = bu[:, 512 * i : 512 * i + 512]
     dyb = halves(cot, first_long)
     ha = ha_r[...]
 
@@ -319,12 +323,12 @@
         pair, kind = head // 3, head % 3
         if kind == 1:
             for p in range(2):
-                tx_s[2 * pair + p, 256:384, :] = kvb[128:256]
-                tx_s[2 * pair + p, 384:448, :] = qgb[128 + 64 * p : 192 + 64 * p]
+                tx_b[2 * pair + p, 0:128, :] = kvb[128:256]
+                tx_b[2 * pair + p, 128:192, :] = qgb[128 + 64 * p : 192 + 64 * p]
         else:
             slot = 2 * pair + kind // 2
-            tx_s[slot, 0:128, :] = kvb[128:256]
-            tx_s[slot, 128:256, :] = qgb[128:256]
+            tx_a[slot, 0:128, :] = kvb[128:256]
+            tx_a[slot, 128:256, :] = qgb[128:256]
 
     for wide in range(3):
         for kind in range(3):
@@ -333,7 +337,7 @@
             out_copy.wait()
         q2, k2, v2 = [
             mm(ha, wqkv[:, 768 * kind + 256 * wide : 768 * kind + 256 * wide + 256])
-            + f(bqkv[:, 768 * kind + 256 * wide : 768 * kind + 256 * wide + 256])
+            + bq[:, 768 * kind + 256 * wide : 768 * kind + 256 * wide + 256]
             for kind in range(3)
         ]
         g2 = mm_nt(dyb, wout[256 * wide : 256 * wide + 256, :])
@@ -354,28 +358,51 @@
 
         @pl.when(q == 3)
         def _():
-            run(tx_s.at[y2 * 2 + p2], rx_s.at[me], e1_r.at[1], d)
+            run(tx_a.at[y2 * 2 + p2], rx_a.at[me], e1_r.at[1], d)
 
         @pl.when(q != 3)
         def _():
             run(tx_l.at[(y2 * 3 + q) * 2 + p2], rx_l.at[me], e1_r.at[0], d)
 
-    there(0, lambda src, dst, sem, d: pltpu.make_async_copy(src, dst, sem).start())
+    def there_half(i, run):
+        y2, z2, p2, d = walk(y, z, part, i)
+        q = lax.rem(z2 - y2 - shift + 12, 4)
+
+        @pl.when(q == 3)
+        def _():
+            run(tx_b.at[y2 * 2 + p2], rx_b.at[me], e1_r.at[2], d)
+
+    def local(src, dst, sem, d):
+        pltpu.make_async_copy(src, dst, sem).start()
+
+    def start_by(sems, i):
+        return lambda src, dst, sem, d: remote(src, dst, sems.at[i], sem, (dp, d)).start()
+
+    def end_by(sems, i):
+        return lambda src, dst, sem, d: remote(src, dst, sems.at[i], sem, (dp, d)).wait_send()
+
+    there(0, local)
 
     @pl.loop(1, 32)
     def _(i):
-        there(i, lambda src, dst, sem, d: remote(src, dst, e1_s.at[i], sem, (dp, d)).start())
+        there(i, start_by(e1_s, i))
+
+    there_half(0, local)
+
+    @pl.loop(1, 32)
+    def _(i):
+        there_half(i, start_by(e1b_s, i))
 
     hmt[...] = f(hm_r[...]).T.astype(BF)
     dh[...] = jnp.zeros_like(dh)
-    branch[...] = jnp.broadcast_to(f(downb[...]), branch.shape)
+    branch[...] = jnp.broadcast_to(line(downb), branch.shape)
 
     @pl.loop(0, 6)
     def _(i):
         slot = lax.rem(i, 3)
         for c in ff_copies(i, slot):
             c.wait()
-        u = mm(hm_r[...], up[slot]) + f(upb[:, pl.ds(pl.multiple_of(512 * i, 512), 512)])
+        u = mm(hm_r[...], up[slot]) + ubias[pl.ds(i, 1), :]
         value, slope = gelu_both(u)
         hid = value.astype(BF)
         branch[...] += mm(hid, down[slot])
@@ -400,6 +427,45 @@
     sum_mlp = sum_stages(36864, cube, grads, a_mlp, rx0, rxs, rxe, sems_m, None)
     next(sum_mlp)
 
+    def rows(v, at, n):
+        for c in range(n):
+            small_o[at + c : at + c + 1, :] = v[:, 128 * c : 128 * c + 128]
+
+    def square(v, at):
+        s = jnp.sum(v * v, axis=0, keepdims=True)
+        t = s[:, 0:128]
+        for c in range(1, 6):
+            t = t + s[:, 128 * c : 128 * c + 128]
+        small_o[at : at + 1, :] = t
+
+    def norm_back(d, gain, at):
+        znorm, r = zn[...], rn[:, 0:1]
+        rows(jnp.sum(d * znorm, axis=0, keepdims=True), at, 6)
+        rows(jnp.sum(d, axis=0, keepdims=True), at + 6, 6)
+        e = d * line(gain)
+        return r * (
+            e - jnp.mean(e, axis=-1, keepdims=True) - znorm * jnp.mean(e * znorm, axis=-1, keepdims=True)
+        )
+
+    @pl.loop(0, 32)
+    def _(i):
+        found = jnp.int32(0)
+        for j in range(32):
+            found = jnp.where(span_of(j) == i, j, found)
+        source[i] = found
+
+    x, znorm, r = norm_parts()
+    zn[...] = znorm
+    rn[...] = jnp.broadcast_to(r, rn.shape)
+    dy = f(halves(cot, first_long))
+    small_o[72:80, :] = jnp.zeros((8, 128), F32)
+    square(branch[...], 74)
+    rows(jnp.sum(dy, axis=0, keepdims=True), 42, 6)
+    small_o[48:72, :] = ub[...]
+    branch[...] = branch[...] + x
+    dh[...] = dy + norm_back(dh[...], mgain, 12)
+    hmt[...] = f(ha_r[...]).T.astype(BF)
+
     def fold(v, op):
         return op(v.reshape(v.shape[0] // 8, 8, v.shape[1]), axis=0)
 
@@ -422,12 +488,12 @@
         col = lax.broadcasted_iota(jnp.int32, (1, 256), 1)
         return (4 * t + col // 64) * 128 + 64 * part + lax.rem(col, 64)
 
-    def get_keys(ref, at, rows, flip):
+    def get_keys(ref, rows, flip):
         @pl.loop(0, 32)
         def _(i):
             src = source[31 - i] if flip else source[i]
-            kv[pl.ds(pl.multiple_of(i * 128, 128), 128), :] = ref[src, at : at + 128, :]
-            qg[pl.ds(pl.multiple_of(i * rows, rows), rows), :] = ref[src, at + 128 : at + 128 + rows, :]
+            kv[pl.ds(pl.multiple_of(i * 128, 128), 128), :] = ref[src, 0:128, :]
+            qg[pl.ds(pl.multiple_of(i * rows, rows), rows), :] = ref[src, 128 : 128 + rows, :]
 
         @pl.loop(0, 32)
         def _(i):
@@ -436,16 +502,16 @@
 
         dkv[...] = jnp.zeros_like(dkv)
 
-    def put_back(ref, at, rows, flip):
+    def put_back(ref, rows, flip):
         @pl.loop(0, 32)
         def _(i):
             rel = 31 - span_of(i) if flip else span_of(i)
-            ref[i, at : at + 128, :] = dkv[rel].astype(BF)
+            ref[i, 0:128, :] = dkv[rel].astype(BF)
             if rows == 64:
-                ref[i, at + 128 : at + 192, :] = qo[rel]
+                ref[i, 128:192, :] = qo[rel]
             else:
-                ref[i, at + 128 : at + 192, :] = qo[2 * rel]
-                ref[i, at + 192 : at + 256, :] = qo[2 * rel + 1]
+                ref[i, 128:192, :] = qo[2 * rel]
+                ref[i, 192:256, :] = qo[2 * rel + 1]
 
     def long_tile(t):
         qz, zg, gt = load_tile(t * 256)
@@ -512,72 +578,95 @@
     def half_tile(t):
         short_tile(t * 256, 512 * (t - 1) * ((t + 7) // 8), 1024, strided_places(t))
 
-    def tiles(lo, hi, body):
-        pl.loop(lo, hi)(body)
-
-    long_at = [0, 3, 5, 6, 7, 8]
-    short_at = [0, 5, 10, 16]
-    half_at = [0, 4, 8]
-    for slot in range(5):
-        @pl.when(is_long)
-        def _():
-            if slot == 0:
-                pltpu.make_async_copy(rx_l, rx_l, e1_r.at[0]).wait()
-                get_keys(rx_l, 0, 64, False)
-            tiles(long_at[slot], long_at[slot + 1], long_tile)
-            if slot == 4:
-                put_back(rx_l, 0, 64, False)
+    def home_full(i, run):
+        d = walk(y, z, part, i)[3]
 
         @pl.when(is_short)
         def _():
-            if slot == 0:
-                pltpu.make_async_copy(rx_s, rx_s, e1_r.at[1]).wait()
-                get_keys(rx_s, 0, 128, True)
-            if slot < 3:
-                tiles(short_at[slot], short_at[slot + 1], full_tile)
-                if slot == 2:
-                    put_back(rx_s, 0, 128, True)
-                    get_keys(rx_s, 256, 64, True)
-            else:
-                tiles(half_at[slot - 3], half_at[slot - 2], half_tile)
-                if slot == 4:
-                    put_back(rx_s, 256, 64, True)
-
-        next(sum_mlp)
+            run(rx_a.at[d], ret_a.at[y * 2 + part], e2_r.at[1], d)
 
     def home(i, run):
         d = walk(y, z, part, i)[3]
 
         @pl.when(is_short)
         def _():
-            run(rx_s.at[d], ret_s.at[y * 2 + part], e2_r.at[1], d)
+            run(rx_b.at[d], ret_b.at[y * 2 + part], e2_r.at[2], d)
 
         @pl.when(is_long)
         def _():
             run(rx_l.at[d], ret_l.at[(y * 3 + mine) * 2 + part], e2_r.at[0], d)
 
-    home(0, lambda src, dst, sem, d: pltpu.make_async_copy(src, dst, sem).start())
+    def tiles(of, body):
+        pl.loop(0, len(of))(lambda i: body(of[0] + (of[-1] - of[0]) // max(len(of) - 1, 1) * i))
+
+    long_tiles = [[7], [6], [5], [4], [3, 0], [2, 1]]
+    full_tiles = [range(0, 6), range(6, 11), range(11, 16)]
+    half_tiles = [range(0, 3), range(3, 5), range(5, 8)]
+
+    @pl.when(is_long)
+    def _():
+        pltpu.make_async_copy(rx_l, rx_l, e1_r.at[0]).wait()
+        get_keys(rx_l, 64, False)
+
+    @pl.when(is_short)
+    def _():
+        pltpu.make_async_copy(rx_a, rx_a, e1_r.at[1]).wait()
+        get_keys(rx_a, 128, True)
+
+    next(sum_mlp)
+    for slot in range(6):
+        @pl.when(is_long)
+        def _():
+            tiles(long_tiles[slot], long_tile)
+            if slot == 5:
+                put_back(rx_l, 64, False)
+
+        @pl.when(is_short)
+        def _():
+            if slot < 3:
+                tiles(full_tiles[slot], full_tile)
+            else:
+                tiles(half_tiles[slot - 3], half_tile)
+            if slot == 2:
+                put_back(rx_a, 128, True)
+                home_full(0, local)
+
+                @pl.loop(1, 32)
+                def _(i):
+                    home_full(i, start_by(e2a_s, i))
+
+                pltpu.make_async_copy(rx_b, rx_b, e1_r.at[2]).wait()
+                get_keys(rx_b, 64, True)
+            if slot == 5:
+                put_back(rx_b, 64, True)
+
+        if slot < 5:
+            next(sum_mlp)
+
+    home(0, local)
 
     @pl.loop(1, 32)
     def _(i):
-        home(i, lambda src, dst, sem, d: remote(src, dst, e2_s.at[i], sem, (dp, d)).start())
-
-    for unused in sum_mlp:
-        pass
-    pltpu.make_async_copy(ret_s, ret_s, e2_r.at[1]).wait()
+        home(i, start_by(e2_s, i))
+
+    for unused in range(4):
+        next(sum_mlp)
+    pltpu.make_async_copy(ret_a, ret_a, e2_r.at[1]).wait()
+    pltpu.make_async_copy(ret_b, ret_b, e2_r.at[2]).wait()
     pltpu.make_async_copy(ret_l, ret_l, e2_r.at[0]).wait()
+    next(sum_mlp)
 
     def gather(head):
         pair, kind = head // 3, head % 3
         kv_l = f(ret_l[2 * head, 0:128, :]) + f(ret_l[2 * head + 1, 0:128, :])
         qo_l = [f(ret_l[2 * head, 128:192, :]), f(ret_l[2 * head + 1, 128:192, :])]
         if kind == 1:
-            kv_s = f(ret_s[2 * pair, 256:384, :]) + f(ret_s[2 * pair + 1, 256:384, :])
-            qo_s = [f(ret_s[2 * pair, 384:448, :]), f(ret_s[2 * pair + 1, 384:448, :])]
+            kv_s = f(ret_b[2 * pair, 0:128, :]) + f(ret_b[2 * pair + 1, 0:128, :])
+            qo_s = [f(ret_b[2 * pair, 128:192, :]), f(ret_b[2 * pair + 1, 128:192, :])]
         else:
             slot = 2 * pair + kind // 2
-            kv_s = f(ret_s[slot, 0:128, :])
-            qo_s = [f(ret_s[slot, 128:256, :])]
+            kv_s = f(ret_a[slot, 0:128, :])
+            qo_s = [f(ret_a[slot, 128:256, :])]
         return jnp.concatenate([kv_l, kv_s], axis=0), jnp.concatenate(qo_l + qo_s, axis=0)
 
     for j in range(6):
@@ -593,69 +682,48 @@
         gqkv[:, 768 + 128 * j : 896 + 128 * j] = turn(dk, tabs[0], tabs[1], tabs[2], -1.0).astype(BF)
         gqkv[:, 1536 + 128 * j : 1664 + 128 * j] = dv.astype(BF)
 
-    def rows(v, at, n):
-        for c in range(n):
-            small_o[at + c : at + c + 1, :] = v[:, 128 * c : 128 * c + 128]
-
-    def square(v, at):
-        s = jnp.sum(v * v, axis=0, keepdims=True)
-        t = s[:, 0:128]
-        for c in range(1, 6):
-            t = t + s[:, 128 * c : 128 * c + 128]
-        small_o[at : at + 1, :] = t
-
     def put_rows(ref, v):
         ref[0:128, :] = jnp.where(first_long, v[0:128], v[128:256])
         ref[128:256, :] = jnp.where(first_long, v[128:256], v[0:128])
 
     attT = f(att[...]).T.astype(BF)
-    haT = f(ha_r[...]).T.astype(BF)
     dy_b = halves(cot, first_long)
     for w in range(3):
         t = mm(attT, dy_b[:, 256 * w : 256 * w + 256]).astype(BF)
         for b in range(2):
             grads[768 * (18 + 2 * w + b) : 768 * (19 + 2 * w + b), :] = t[:, 128 * b : 128 * b + 128]
+    for w in range(9):
+        t = mm(hmt[...], gqkv[:, 256 * w : 256 * w + 256]).astype(BF)
+        for b in range(2):
+            grads[768 * (2 * w + b) : 768 * (2 * w + b + 1), :] = t[:, 128 * b : 128 * b + 128]
+    sum_attn = sum_stages(18432, cube, grads, a_attn, rx1, rxs, rxe, sems_a, (small_o, srx, sm_s, sm_r))
+    next(sum_attn)
+
+    attn = mm(att[...], wout[...]) + line(outb)
+    out = attn + branch[...]
+    put_rows(mixed_o, out.astype(BF))
+    square(out, 72)
+    square(attn, 73)
     d_attn = jnp.zeros((256, D), F32)
     for w in range(9):
-        cols = slice(256 * w, 256 * w + 256)
-        piece = gqkv[:, cols]
+        piece = gqkv[:, 256 * w : 256 * w + 256]
         rows(jnp.sum(f(piece), axis=0, keepdims=True), 24 + 2 * w, 2)
-        t = mm(haT, piece).astype(BF)
-        for b in range(2):
-            grads[768 * (2 * w + b) : 768 * (2 * w + b + 1), :] = t[:, 128 * b : 128 * b + 128]
-        d_attn = d_attn + mm_nt(piece, wqkv[:, cols])
-
-    x, znorm, r = norm_parts()
-    dy = f(dy_b)
-    attn = mm(att[...], wout[...]) + f(outb[...])
-    out = x + attn + branch[...]
-    put_rows(mixed_o, out.astype(BF))
-    small_o[72:80, :] = jnp.zeros((8, 128), F32)
-    square(out, 72)
-    square(attn, 73)
-    square(branch[...], 74)
-    rows(jnp.sum(dy, axis=0, keepdims=True), 42, 6)
-    small_o[48:72, :] = ub[...]
-
-    def norm_back(d, gain, at):
-        rows(jnp.sum(d * znorm, axis=0, keepdims=True), at, 6)
-        rows(jnp.sum(d, axis=0, keepdims=True), at + 6, 6)
-        e = d * f(gain[...])
-        return r * (
-            e - jnp.mean(e, axis=-1, keepdims=True) - znorm * jnp.mean(e * znorm, axis=-1, keepdims=True)
-        )
-
-    put_rows(tgrad_o, dy + norm_back(d_attn, again, 0) + norm_back(dh[...], mgain, 12))
-
-    for unused in sum_stages(
-        18432, cube, grads, a_attn, rx0, rxs, rxe, sems_a, (small_o, srx, sm_s, sm_r)
-    ):
+        d_attn = d_attn + mm_nt(piece, wqkv[:, 256 * w : 256 * w + 256])
+    put_rows(tgrad_o, dh[...] + norm_back(d_attn, again, 0))
+
+    next(sum_mlp)
+    next(sum_attn)
+    for unused in sum_attn:
+        pass
+    for unused in sum_mlp:
         pass
 
     @pl.loop(1, 32)
     def _(i):
-        there(i, lambda src, dst, sem, d: remote(src, dst, e1_s.at[i], sem, (dp, d)).wait_send())
-        home(i, lambda src, dst, sem, d: remote(src, dst, e2_s.at[i], sem, (dp, d)).wait_send())
+        there(i, end_by(e1_s, i))
+        there_half(i, end_by(e1b_s, i))
+        home_full(i, end_by(e2a_s, i))
+        home(i, end_by(e2_s, i))
 
 
 def layer_call(*args):
@@ -681,21 +749,24 @@
             jax.ShapeDtypeStruct((36864, 128), BF),
             jax.ShapeDtypeStruct((18432, 128), BF),
         ),
-        in_specs=[pl.BlockSpec(memory_space=pltpu.SMEM)] * 3 + vm(10) + [anywhere] * 4,
+        in_specs=[pl.BlockSpec(memory_space=pltpu.SMEM)] * 2 + vm(10) + [anywhere] * 4,
         out_specs=vm(3) + [anywhere] * 2,
         scratch_shapes=[
+            pltpu.SMEM((32,), jnp.int32),
             vb(D, 3 * D), vb(D, D), vb(3, D, 512), vb(3, 512, D),
-            vb(24, LROWS, 128), vb(8, SROWS, 128), vb(32, LROWS, 128), vb(32, SROWS, 128),
-            vb(24, LROWS, 128), vb(8, SROWS, 128),
-            vb(256, D), vb(256, D), vb(D, 256), vf(3, 256, 128), vf(256, D), vf(256, D), vf(24, 128),
-            vb(36864, 128),
+            vb(24, 192, 128), vb(8, 256, 128), vb(8, 192, 128),
+            vb(32, 192, 128), vb(32, 256, 128), vb(32, 192, 128),
+            vb(24, 192, 128), vb(8, 256, 128), vb(8, 192, 128),
+            vb(256, D), vb(256, D), vb(D, 256), vf(3, 256, 128), vf(256, D), vf(256, D), vf(256, D), vf(256, 128),
+            vf(24, 128), vf(6, 512), vb(36864, 128),
             vb(HALF, 128), vb(128, HALF), vb(HALF, 128), vb(64, 64, 128), vf(32, 128, 128), vf(HALF, 256),
             vb(256, 3 * D), vb(256, D),
-            vb(6, 3072, 128),
+            vb(6, 3072, 128), vb(6, 1536, 128),
         ]
         + [vb(6, 3072 >> (t + 1), 128) for t in range(STEPS)]
         + [vb(6, 3072 >> STEPS, 128), vf(7, SMALL, 128)]
-        + [dma((9,)), dma, dma((3,)), dma((3,)), dma((32,)), dma((2,)), dma((32,)), dma((2,)), dma((7,)), dma((7,))]
+        + [dma((9,)), dma, dma((3,)), dma((3,)), dma((32,)), dma((32,)), dma((3,))]
+        + [dma((32,)), dma((32,)), dma((3,)), dma((7,)), dma((7,))]
         + sum_sems * 2,
         compiler_params=pltpu.CompilerParams(
             collective_id=0, has_side_effects=True, vmem_limit_bytes=62 << 20
@@ -703,69 +774,84 @@
     )(*args)
 
 
-def unpack_mlp_kernel(a, up_o, down_o):
+VECTORS = ((0, 6), (6, 6), (12, 6), (18, 6), (24, 18), (42, 6), (48, 24), (42, 6))
+
+
+def unpack_kernel(small, a_mlp, a_qkv, a_out, mixed, tgrad, mixed_o, tgrad_o, up_o, down_o, qkv_o, out_o, *rest):
+    vectors, roots = rest[:8], rest[8:]
+    mixed_o[...] = mixed[...]
+    tgrad_o[...] = tgrad[...]
     for c in range(4):
-        up_o[:, 128 * c : 128 * c + 128] = a[768 * c : 768 * c + 768, :].astype(F32)
+        up_o[:, 128 * c : 128 * c + 128] = a_mlp[768 * c : 768 * c + 768, :].astype(F32)
     for c in range(6):
-        down_o[:, 128 * c : 128 * c + 128] = a[3072 + 512 * c : 3584 + 512 * c, :].astype(F32)
-
-
-def unpack_mlp(a):
+        down_o[:, 128 * c : 128 * c + 128] = a_mlp[3072 + 512 * c : 3584 + 512 * c, :].astype(F32)
+    for c in range(3):
+        qkv_o[:, 128 * c : 128 * c + 128] = a_qkv[768 * c : 768 * c + 768, :].astype(F32)
+    out_o[...] = a_out[...].astype(F32)
+
+    @pl.when(pl.program_id(0) == 0)
+    def _():
+        for ref, (at, n) in zip(vectors, VECTORS):
+            for c in range(n):
+                ref[pl.ds(128 * c, 128)] = small[at + c, :]
+        for ref, at in zip(roots, (72, 73, 74)):
+            total = jnp.sum(small[at : at + 1, :], axis=1, keepdims=True)
+            ref[0] = jnp.sqrt(total * (1.0 / (D * 256 * 128)))[0, 0]
+
+
+def unpack_call(small, a_mlp, a_attn, mixed, tgrad):
+    def whole(n):
+        return pl.BlockSpec((n,), lambda i: (0,))
+
+    sizes = [128 * n for at, n in VECTORS]
+    scalar = pl.BlockSpec(memory_space=pltpu.SMEM)
+    columns = pl.BlockSpec((256, 128), lambda i: (0, i))
     return pl.pallas_call(
-        unpack_mlp_kernel,
+        unpack_kernel,
         grid=(6,),
-        out_shape=(jax.ShapeDtypeStruct((D, FF), F32), jax.ShapeDtypeStruct((FF, D), F32)),
-        in_specs=[pl.BlockSpec((6144, 128), lambda i: (i, 0))],
-        out_specs=[pl.BlockSpec((D, 512), lambda i: (0, i)), pl.BlockSpec((512, D), lambda i: (i, 0))],
-        compiler_params=pltpu.CompilerParams(vmem_limit_bytes=48 << 20),
-    )(a)
-
-
-def unpack_attn_kernel(a, b, qkv_o, out_o):
-    for c in range(6):
-        qkv_o[:, 128 * c : 128 * c + 128] = a[768 * c : 768 * c + 768, :].astype(F32)
-    for c in range(2):
-        out_o[:, 128 * c : 128 * c + 128] = b[768 * c : 768 * c + 768, :].astype(F32)
-
-
-def unpack_attn(a):
-    return pl.pallas_call(
-        unpack_attn_kernel,
-        grid=(3,),
-        out_shape=(jax.ShapeDtypeStruct((D, 3 * D), F32), jax.ShapeDtypeStruct((D, D), F32)),
+        out_shape=(
+            jax.ShapeDtypeStruct((256, D), BF),
+            jax.ShapeDtypeStruct((256, D), F32),
+            jax.ShapeDtypeStruct((D, FF), F32),
+            jax.ShapeDtypeStruct((FF, D), F32),
+            jax.ShapeDtypeStruct((D, 3 * D), F32),
+            jax.ShapeDtypeStruct((D, D), F32),
+        )
+        + tuple(jax.ShapeDtypeStruct((n,), F32) for n in sizes)
+        + tuple(jax.ShapeDtypeStruct((1,), F32) for unused in range(3)),
         in_specs=[
-            pl.BlockSpec((4608, 128), lambda i: (i, 0)),
-            pl.BlockSpec((1536, 128), lambda i: (9 + i, 0)),
+            pl.BlockSpec((SMALL, 128), lambda i: (0, 0)),
+            pl.BlockSpec((6144, 128), lambda i: (i, 0)),
+            pl.BlockSpec((2304, 128), lambda i: (i, 0)),
+            pl.BlockSpec((768, 128), lambda i: (18 + i, 0)),
+            columns,
+            columns,
         ],
-        out_specs=[pl.BlockSpec((D, 768), lambda i: (0, i)), pl.BlockSpec((D, 256), lambda i: (0, i))],
-        compiler_params=pltpu.CompilerParams(vmem_limit_bytes=48 << 20),
-    )(a, a)
+        out_specs=[
+            columns,
+            columns,
+            pl.BlockSpec((D, 512), lambda i: (0, i)),
+            pl.BlockSpec((512, D), lambda i: (i, 0)),
+            pl.BlockSpec((D, 384), lambda i: (0, i)),
+            pl.BlockSpec((D, 128), lambda i: (0, i)),
+        ]
+        + [whole(n) for n in sizes]
+        + [scalar] * 3,
+        compiler_params=pltpu.CompilerParams(vmem_limit_bytes=62 << 20),
+    )(small, a_mlp, a_attn, a_attn, mixed, tgrad)
 
 
 def on_device(tokens, attn_gain, attn_bias, mlp_gain, mlp_bias, qkv_weight, qkv_bias, out_weight, out_bias,
               up_weight, up_bias, down_weight, down_bias, cotangent, doc_lengths, span_order):
-    first_long = doc_lengths[0, 0] > 512
-    spans = span_order.reshape(SPANS, 2)[:, 0]
-    long_span = jnp.where(first_long, spans, 31 - spans)
-    index = jnp.arange(SPANS, dtype=jnp.int32)
-    source = jnp.sum(jnp.where(long_span[None, :] == index[:, None], index[None, :], 0), axis=1)
-    vectors = (attn_gain, attn_bias, mlp_gain, mlp_bias, qkv_bias, out_bias, up_bias, down_bias)
-    mixed, tokens_grad, small_sum, mlp_sum, attn_sum = layer_call(
-        source, span_order, doc_lengths, tokens, cotangent, *[v.reshape(1, -1) for v in vectors],
-        qkv_weight, out_weight, up_weight, down_weight,
+    mixed, tokens_grad, small, mlp_sum, attn_sum = layer_call(
+        span_order, doc_lengths, tokens, cotangent, attn_gain, attn_bias, mlp_gain, mlp_bias, qkv_bias, out_bias,
+        up_bias, down_bias, qkv_weight, out_weight, up_weight, down_weight,
     )
-    grad_up, grad_down = unpack_mlp(mlp_sum)
-    grad_qkv, grad_out = unpack_attn(attn_sum)
-
-    def vector(at, n):
-        return small_sum[at : at + n].reshape(128 * n)
-
-    roots = jnp.sqrt(jnp.sum(small_sum[72:75], axis=1) / (D * 256 * 128))
-    branch_bias = vector(42, 6)
-    return (
-        mixed, tokens_grad, vector(0, 6), vector(6, 6), vector(12, 6), vector(18, 6), grad_qkv, vector(24, 18),
-        grad_out, branch_bias, grad_up, vector(48, 24), grad_down, branch_bias, roots[0], roots[1], roots[2],
+    mixed, tokens_grad, up, down, qkv, out, ag, ab, mg, mb, bq, bo, bu, bd, *roots = unpack_call(
+        small, mlp_sum, attn_sum, mixed, tokens_grad
     )
+    rms = [root.reshape(()) for root in roots]
+    return (mixed, tokens_grad, ag, ab, mg, mb, qkv, bq, out, bo, up, bu, down, bd, *rms)
 
 
 def solution(mesh):

time: 259 us -> 217 us (0.84)
  Pallas kernels: 237 us -> 216 us
  local copies, waits for them, and re-layouts: 17.8 us -> 0 us
  other arithmetic: 2.75 us -> 0 us
    pallas_call x1, Pallas kernels: 222 us -> 199 us  [layer_call(): pl.pallas_call(layer_kernel, out_shape=(jax.ShapeDtypeStruct((256, D), BF...]
    reshape x12 -> x0, local copies, waits for them, and re-layouts: 14.4 us -> none  [the longest x8 10.2 us: on_device(): v.reshape(1, -1)]
    unnamed x14 -> x0, local copies, waits for them, and re-layouts: 2.75 us -> none
    pallas_call x2 -> x1, Pallas kernels: 15 us -> 16.7 us  [unpack_call(): pl.pallas_call(unpack_kernel, grid=(6,), out_shape=(jax.ShapeDtypeStruct(...]
where the time goes in v3:
time: 217 us
  Pallas kernels  216 us (100%)
    pallas_call x1, Pallas kernels, layer_call(): pl.pallas_call(layer_kernel, out_shape=(jax.ShapeDtypeStruct((256, D), BF...  199 us
    pallas_call x1, Pallas kernels, unpack_call(): pl.pallas_call(unpack_kernel, grid=(6,), out_shape=(jax.ShapeDtypeStruct(...  16.7 us

profile of v3, /device:TPU:1, one launch (start us, length us, event | category | flops | bytes accessed | tf_op | source)
XLA Modules:
  0.0 216.7 jit_solution(15414403154825539800)
XLA Ops:
  0.7 199.2 %shard_map.287 = (bf16[256,768]{1,0:T(8,128)(2,1)}, f32[256,768]{1,0:T(8,128)}, f32[80,128]{1,0:T(8,128)}, bf16[36864,128]{1,0:T(8,128)(2,1)}, bf16[18432,128]{1,0:T(8,128)(2,1)}) custom-call(s32[1,64]{1,0:T(1,128)} %order.1, s32[1,16]{1,0:T(1,128)} %lens.1, bf16[256,768]{1,0:T(8,128)(2,1)} %tok.1, bf16[256,768]{1,0:T(8,128)(2,1)} %cot.1, ...), custom_call_target="tpu_custom_call" | custom-call | tf_op jit(solution)/shard_map/pallas_call | solution.py:743
  199.8 16.7 %shard_map.288 = (bf16[256,768]{1,0:T(8,128)(2,1)}, f32[256,768]{1,0:T(8,128)}, f32[768,3072]{1,0:T(8,128)}, f32[3072,768]{1,0:T(8,128)}, f32[768,2304]{1,0:T(8,...) custom-call(f32[80,128]{1,0:T(8,128)} %get-tuple-element.39.small, ...), custom_call_target="tpu_custom_call" | custom-call | tf_op jit(solution)/shard_map/pallas_call | solution.py:809

commit v4 on v3

--- a/solution.py
+++ b/solution.py
@@ -17,7 +17,6 @@
 EPS = 1e-05
 NEG = -1e30
 SMALL = 80
-STEPS = 5
 BF = jnp.bfloat16
 F32 = jnp.float32
 MESH = pl.DeviceIdType.MESH
@@ -77,129 +76,201 @@
     return (lax.rem(x, 2) * 2 + core, y * 8 + z * 2 + x // 2)
 
 
-def cube_partners(dp, blk):
+def rings_of(dp, blk):
     core = lax.rem(dp, 2)
     at = {"x": lax.rem(blk, 2) * 2 + dp // 2, "y": blk // 8, "z": lax.rem(blk // 2, 4)}
-    out = []
+    rings = []
     for axis in ("x", "y", "z"):
-        v = at[axis]
-        hi, lo = v // 2, lax.rem(v, 2)
-        for nv, bit in ((v + 1 - 2 * lo, lax.rem(hi + lo, 2)), (3 - v, hi)):
+        peers = []
+        for k in range(1, 4):
             there = dict(at)
-            there[axis] = nv
-            out.append((place_id(core, there["x"], there["y"], there["z"]), bit))
-    return core, place_id(1 - core, at["x"], at["y"], at["z"]), out
+            there[axis] = lax.rem(at[axis] + k, 4)
+            peers.append(place_id(core, there["x"], there["y"], there["z"]))
+        rings.append((at[axis], peers))
+    return core, place_id(1 - core, at["x"], at["y"], at["z"]), rings
 
 
 def remote(src, dst, send, recv, d):
     return pltpu.make_async_remote_copy(src, dst, send, recv, device_id=d, device_id_type=MESH)
 
 
-def sum_stages(rows, cube, f_ref, a_ref, rx0, rxs, rxe, sems, small):
-    core_s, core_r, rs_s, rs_r, ex_s, ex_r, ag_s, ag_r, fin_s, fin_r, loc = sems
-    part, half_rows, steps = rows // 12, rows // 2, STEPS
-    core, other, partners = cube
-    base = [pl.multiple_of(core * half_rows + p * part, 16) for p in range(6)]
-    obase = [pl.multiple_of((1 - core) * half_rows + p * part, 16) for p in range(6)]
-
-    def add(off, n, src):
-        w = 96
+ORDER = (2, 1, 3, 0)
+
+
+def sum_stages(rows, places, f_ref, a_ref, bufs, sems, small):
+    rx0, rxa, rxb, rxx = bufs
+    core_s, core_r, a_s, a_r, b_s, b_r, x_s, x_r, gb_s, gb_r, ga_s, ga_r, fin_s, fin_r, loc = sems
+    core, other, rings = places
+    part, n1, n2 = rows // 6, rows // 24, rows // 96
+    base = [core * (rows // 2) + r * part for r in range(3)]
+    there = [(1 - core) * (rows // 2) + r * part for r in range(3)]
+    at = [[rings[(r + j) % 3][0] for j in range(3)] for r in range(3)]
+    peer = [[rings[(r + j) % 3][1] for j in range(3)] for r in range(3)]
+
+    def span(start, n):
+        return pl.ds(pl.multiple_of(start, 16), n)
+
+    def step(n):
+        w = min(n, 384)
         while n % w:
-            w //= 2
+            w -= 16
+        return w
+
+    def add(start, n, sources):
+        w = step(n)
 
         @pl.loop(0, n // w)
         def _(i):
-            here = pl.ds(pl.multiple_of(off + i * w, 16), w)
-            there = pl.ds(pl.multiple_of(i * w, 16), w)
-            f_ref[here, :] = (f_ref[here, :].astype(F32) + src[there, :].astype(F32)).astype(BF)
-
-    if small is not None:
-        so_ref, srx, sm_s, sm_r = small
-        to = [other] + [q[0] for q in partners]
-
-        def small_copy(t):
-            return remote(so_ref, srx.at[t], sm_s.at[t], sm_r.at[t], to[t])
-
-    def small_next(t):
-        if small is not None:
-            small_copy(t).wait()
-            so_ref[...] += srx[t]
-            if t < 6:
-                small_copy(t + 1).start()
-
-    def landing(ref, p, n):
-        return ref.at[p, pl.ds(0, n)]
-
-    pend = [
-        remote(f_ref.at[pl.ds(obase[p], part)], landing(rx0, p, part), core_s.at[p], core_r.at[p], other)
-        for p in range(6)
-    ]
-    for p in range(6):
-        pend[p].start()
+            here = span(start + i * w, w)
+            total = f_ref[here, :].astype(F32)
+            for ref in sources:
+                total = total + ref[span(i * w, w), :].astype(F32)
+            f_ref[here, :] = total.astype(BF)
+
+    def first(r, k):
+        return lax.rem(at[r][0] + k, 4) * n1
+
+    def second(r, k):
+        return lax.rem(at[r][1] + k, 4) * n2
+
+    own1 = [base[r] + first(r, 0) for r in range(3)]
+    own2 = [own1[r] + second(r, 0) for r in range(3)]
+
+    cores = {}
+    for k in ORDER:
+        for r in range(3):
+            cores[r, k] = remote(
+                f_ref.at[span(there[r] + first(r, k), n1)], rx0.at[r, k, pl.ds(0, n1)],
+                core_s.at[r, k], core_r.at[r, k], other,
+            )
+            cores[r, k].start()
     yield
     if small is not None:
-        small_copy(0).start()
-    offs, size = list(base), part
-    for t in range(steps):
-        h = size // 2
-        for p in range(6):
-            pend[p].wait_recv()
-            add(offs[p], size, (rx0 if t == 0 else rxs[t - 1]).at[p])
-            dev, bit = partners[(p + t) % 6]
-            out = pl.multiple_of(offs[p] + (1 - bit) * h, 16)
-            c = remote(f_ref.at[pl.ds(out, h)], landing(rxs[t], p, h), rs_s.at[t, p], rs_r.at[t, p], dev)
+        so_ref, mail, sm_s, sm_r = small
+        cross = remote(so_ref, mail.at[0, 0], sm_s.at[0, 0], sm_r.at[0, 0], other)
+        cross.start()
+    sent = {}
+    for k in ORDER:
+        for r in range(3):
+            cores[r, k].wait_recv()
+            here = base[r] + first(r, k)
+            add(here, n1, [rx0.at[r, k]])
+            if k:
+                sent[r, k] = remote(
+                    f_ref.at[span(here, n1)], rxa.at[r, k - 1, pl.ds(0, n1)],
+                    a_s.at[r, k - 1], a_r.at[r, k - 1], peer[r][0][k - 1],
+                )
+                sent[r, k].start()
+
+    letters = []
+
+    def small_send(j):
+        mail[j + 1, rings[j][0]] = so_ref[...]
+        for k in range(3):
+            c = remote(so_ref, mail.at[j + 1, rings[j][0]], sm_s.at[j + 1, k], sm_r.at[j + 1, k], rings[j][1][k])
             c.start()
-            pend[p].wait_send()
-            pend[p] = c
-            offs[p] = pl.multiple_of(offs[p] + bit * h, 16)
-        small_next(t)
-        size = h
-        yield
-    both = []
-    for p in range(6):
-        pend[p].wait_recv()
-        add(offs[p], size, rxs[steps - 1].at[p])
-        here = f_ref.at[pl.ds(offs[p], size)]
-        c = remote(here, landing(rxe, p, size), ex_s.at[p], ex_r.at[p], partners[(p + steps) % 6][0])
+            letters.append(c)
+
+    def small_take(j):
+        if j < 0:
+            cross.wait()
+            so_ref[...] += mail[0, 0]
+        else:
+            for c in letters[3 * j : 3 * j + 3]:
+                c.wait()
+            so_ref[...] = (mail[j + 1, 0] + mail[j + 1, 1]) + (mail[j + 1, 2] + mail[j + 1, 3])
+
+    def small_next(j):
+        if small is not None:
+            small_take(j - 1)
+            if j < 3:
+                small_send(j)
+
+    small_next(0)
+    yield
+    came, sent = sent, {}
+    for r in range(3):
+        for k in range(1, 4):
+            came[r, k].wait_recv()
+        add(own1[r], n1, [rxa.at[r, k] for k in range(3)])
+        for k in (2, 1, 3):
+            sent[r, k] = remote(
+                f_ref.at[span(own1[r] + second(r, k), n2)], rxb.at[r, k - 1, pl.ds(0, n2)],
+                b_s.at[r, k - 1], b_r.at[r, k - 1], peer[r][1][k - 1],
+            )
+            sent[r, k].start()
+    small_next(1)
+    for c in cores.values():
+        c.wait_send()
+    yield
+    before, came, sent = came, sent, {}
+    for r in range(3):
+        for k in range(1, 4):
+            came[r, k].wait_recv()
+        add(own2[r], n2, [rxb.at[r, k] for k in range(3)])
+        mine = rxx.at[r, at[r][2], pl.ds(0, n2)]
+        mine[...] = f_ref[span(own2[r], n2), :]
+        for k in (2, 1, 3):
+            sent[r, k] = remote(
+                f_ref.at[span(own2[r], n2)], mine, x_s.at[r, k - 1], x_r.at[r, k - 1], peer[r][2][k - 1]
+            )
+            sent[r, k].start()
+    small_next(2)
+    for c in before.values():
+        c.wait_send()
+    yield
+    before, came, sent, kept = came, sent, {}, []
+    for r in range(3):
+        for k in range(1, 4):
+            came[r, k].wait()
+        w = step(n2)
+
+        @pl.loop(0, n2 // w)
+        def _(i):
+            q = [rxx[r, j, span(i * w, w), :].astype(F32) for j in range(4)]
+            f_ref[span(own2[r] + i * w, w), :] = ((q[0] + q[1]) + (q[2] + q[3])).astype(BF)
+
+        here = span(own2[r], n2)
+        for k in (2, 1, 3):
+            sent[r, k] = remote(
+                f_ref.at[here], a_ref.at[here], gb_s.at[r, k - 1], gb_r.at[r, k - 1], peer[r][1][k - 1]
+            )
+            sent[r, k].start()
+        c = pltpu.make_async_copy(f_ref.at[here], a_ref.at[here], loc.at[r])
         c.start()
-        pend[p].wait_send()
-        both.append(c)
-    small_next(steps)
+        kept.append(c)
+    small_next(3)
+    for c in before.values():
+        c.wait_send()
     yield
-    own = []
-    for p in range(6):
-        both[p].wait()
-        add(offs[p], size, rxe.at[p])
-        here = pl.ds(offs[p], size)
-        c = pltpu.make_async_copy(f_ref.at[here], a_ref.at[here], loc.at[p])
-        c.start()
-        own.append(c)
-    for p in range(6):
-        own[p].wait()
-    prev = [None] * 6
-    for t in reversed(range(steps)):
-        for p in range(6):
-            if prev[p] is not None:
-                prev[p].wait()
-            dev, bit = partners[(p + t) % 6]
-            here = a_ref.at[pl.ds(offs[p], size)]
-            prev[p] = remote(here, here, ag_s.at[t, p], ag_r.at[t, p], dev)
-            prev[p].start()
-            offs[p] = pl.multiple_of(offs[p] - bit * size, 16)
-        if t == steps - 1:
-            small_next(6)
-        size *= 2
-        yield
-    last = []
-    for p in range(6):
-        prev[p].wait()
-        here = a_ref.at[pl.ds(base[p], part)]
-        c = remote(here, here, fin_s.at[p], fin_r.at[p], other)
+    came, sent, last = sent, {}, []
+
+    def to_other(r, k):
+        here = a_ref.at[span(base[r] + first(r, k), n1)]
+        c = remote(here, here, fin_s.at[r, k], fin_r.at[r, k], other)
         c.start()
         last.append(c)
+
+    for r in range(3):
+        for k in range(1, 4):
+            came[r, k].wait()
+        kept[r].wait()
+        here = a_ref.at[span(own1[r], n1)]
+        for k in (2, 1, 3):
+            sent[r, k] = remote(here, here, ga_s.at[r, k - 1], ga_r.at[r, k - 1], peer[r][0][k - 1])
+            sent[r, k].start()
+    for r in range(3):
+        to_other(r, 0)
     yield
-    for p in range(6):
-        last[p].wait()
+    for k in (1, 3, 2):
+        for r in range(3):
+            sent[r, k].wait_recv()
+            to_other(r, 4 - k)
+    yield
+    for c in list(sent.values()) + last:
+        c.wait_send()
+    for c in last:
+        c.wait_recv()
     yield
 
 
@@ -227,15 +298,14 @@
     mixed_o, tgrad_o, small_o, a_mlp, a_attn,
     source, wqkv, wout, up, down, tx_l, tx_a, tx_b, rx_l, rx_a, rx_b, ret_l, ret_a, ret_b,
     ha_r, hm_r, hmt, tabs, branch, dh, zn, rn, ub, ubias, grads,
-    kv, kvt, qg, qo, dkv, sc, gqkv, att, rx0, rx1, rxa, rxb, rxc, rxd, rxf, rxe, srx,
+    kv, kvt, qg, qo, dkv, sc, gqkv, att, rx0, rx1, rxa, rxb, rxx, mail,
     wq_sem, wo_sem, up_sem, dn_sem, e1_s, e1b_s, e1_r, e2_s, e2a_s, e2_r, sm_s, sm_r, *sum_sems,
 ):
     dp, me = lax.axis_index("dp"), lax.axis_index("blk")
     y, z, part, shift, mine = role(dp, me)
     is_short, is_long = mine == 3, mine != 3
-    cube = cube_partners(dp, me)
-    sems_m, sems_a = sum_sems[:11], sum_sems[11:]
-    rxs = [rxa, rxb, rxc, rxd, rxf]
+    places_of = rings_of(dp, me)
+    sems_m, sems_a = sum_sems[:15], sum_sems[15:]
 
     def f(v):
         return v.astype(F32)
@@ -246,7 +316,7 @@
     def _(i):
         pl.semaphore_signal(bar, inc=1, device_id=(dp, lax.rem(me + i, 32)), device_id_type=MESH)
 
-    for d in [cube[1], cube[2][0][0], cube[2][1][0]]:
+    for d in [places_of[1], places_of[2][0][1][0], places_of[2][0][1][2]]:
         pl.semaphore_signal(bar, inc=1, device_id=d, device_id_type=MESH)
 
     def qkv_copy(c):
@@ -424,7 +494,7 @@
             for c in ff_copies(i + 3, slot):
                 c.start()
 
-    sum_mlp = sum_stages(36864, cube, grads, a_mlp, rx0, rxs, rxe, sems_m, None)
+    sum_mlp = sum_stages(36864, places_of, grads, a_mlp, (rx0, rxa, rxb, rxx), sems_m, None)
     next(sum_mlp)
 
     def rows(v, at, n):
@@ -603,6 +673,8 @@
     full_tiles = [range(0, 6), range(6, 11), range(11, 16)]
     half_tiles = [range(0, 3), range(3, 5), range(5, 8)]
 
+    next(sum_mlp)
+
     @pl.when(is_long)
     def _():
         pltpu.make_async_copy(rx_l, rx_l, e1_r.at[0]).wait()
@@ -613,7 +685,6 @@
         pltpu.make_async_copy(rx_a, rx_a, e1_r.at[1]).wait()
         get_keys(rx_a, 128, True)
 
-    next(sum_mlp)
     for slot in range(6):
         @pl.when(is_long)
         def _():
@@ -640,7 +711,7 @@
             if slot == 5:
                 put_back(rx_b, 64, True)
 
-        if slot < 5:
+        if slot in (1, 3):
             next(sum_mlp)
 
     home(0, local)
@@ -649,8 +720,7 @@
     def _(i):
         home(i, start_by(e2_s, i))
 
-    for unused in range(4):
-        next(sum_mlp)
+    next(sum_mlp)
     pltpu.make_async_copy(ret_a, ret_a, e2_r.at[1]).wait()
     pltpu.make_async_copy(ret_b, ret_b, e2_r.at[2]).wait()
     pltpu.make_async_copy(ret_l, ret_l, e2_r.at[0]).wait()
@@ -696,7 +766,9 @@
         t = mm(hmt[...], gqkv[:, 256 * w : 256 * w + 256]).astype(BF)
         for b in range(2):
             grads[768 * (2 * w + b) : 768 * (2 * w + b + 1), :] = t[:, 128 * b : 128 * b + 128]
-    sum_attn = sum_stages(18432, cube, grads, a_attn, rx1, rxs, rxe, sems_a, (small_o, srx, sm_s, sm_r))
+    sum_attn = sum_stages(
+        18432, places_of, grads, a_attn, (rx1, rxa, rxb, rxx), sems_a, (small_o, mail, sm_s, sm_r)
+    )
     next(sum_attn)
 
     attn = mm(att[...], wout[...]) + line(outb)
@@ -737,8 +809,7 @@
         return pltpu.VMEM(shape, F32)
 
     dma = pltpu.SemaphoreType.DMA
-    sum_sems = [dma((6,)), dma((6,)), dma((STEPS, 6)), dma((STEPS, 6)), dma((6,)), dma((6,))]
-    sum_sems += [dma((STEPS, 6)), dma((STEPS, 6)), dma((6,)), dma((6,)), dma((6,))]
+    sum_sems = [dma((3, 4))] * 2 + [dma((3, 3))] * 10 + [dma((3, 4))] * 2 + [dma((3,))]
     anywhere = pl.BlockSpec(memory_space=pl.ANY)
     return pl.pallas_call(
         layer_kernel,
@@ -761,12 +832,11 @@
             vf(24, 128), vf(6, 512), vb(36864, 128),
             vb(HALF, 128), vb(128, HALF), vb(HALF, 128), vb(64, 64, 128), vf(32, 128, 128), vf(HALF, 256),
             vb(256, 3 * D), vb(256, D),
-            vb(6, 3072, 128), vb(6, 1536, 128),
+            vb(3, 4, 1536, 128), vb(3, 4, 768, 128), vb(3, 3, 1536, 128), vb(3, 3, 384, 128), vb(3, 4, 384, 128),
+            vf(4, 4, SMALL, 128),
         ]
-        + [vb(6, 3072 >> (t + 1), 128) for t in range(STEPS)]
-        + [vb(6, 3072 >> STEPS, 128), vf(7, SMALL, 128)]
         + [dma((9,)), dma, dma((3,)), dma((3,)), dma((32,)), dma((32,)), dma((3,))]
-        + [dma((32,)), dma((32,)), dma((3,)), dma((7,)), dma((7,))]
+        + [dma((32,)), dma((32,)), dma((3,)), dma((4, 3)), dma((4, 3))]
         + sum_sems * 2,
         compiler_params=pltpu.CompilerParams(
             collective_id=0, has_side_effects=True, vmem_limit_bytes=62 << 20

time: 217 us -> 199 us (0.917)
  Pallas kernels: 216 us -> 196 us
    pallas_call x1, Pallas kernels: 199 us -> 179 us  [layer_call(): pl.pallas_call(layer_kernel, out_shape=(jax.ShapeDtypeStruct((256, D), BF...]
where the time goes in v4:
time: 199 us; the launch traced here: 197 us
  Pallas kernels  196 us (98%)
    pallas_call x1, Pallas kernels, layer_call(): pl.pallas_call(layer_kernel, out_shape=(jax.ShapeDtypeStruct((256, D), BF...  179 us
    pallas_call x1, Pallas kernels, unpack_call(): pl.pallas_call(unpack_kernel, grid=(6,), out_shape=(jax.ShapeDtypeStruct(...  16.7 us

profile of v4, /device:TPU:1, one launch (start us, length us, event | category | flops | bytes accessed | tf_op | source)
XLA Modules:
  0.0 197.0 jit_solution(13449061154401642761)
XLA Ops:
  0.7 179.5 %shard_map.287 = (bf16[256,768]{1,0:T(8,128)(2,1)}, f32[256,768]{1,0:T(8,128)}, f32[80,128]{1,0:T(8,128)}, bf16[36864,128]{1,0:T(8,128)(2,1)}, bf16[18432,128]{1,0:T(8,128)(2,1)}) custom-call(s32[1,64]{1,0:T(1,128)} %order.1, s32[1,16]{1,0:T(1,128)} %lens.1, bf16[256,768]{1,0:T(8,128)(2,1)} %tok.1, bf16[256,768]{1,0:T(8,128)(2,1)} %cot.1, ...), custom_call_target="tpu_custom_call" | custom-call | tf_op jit(solution)/shard_map/pallas_call | solution.py:814
  180.1 16.7 %shard_map.288 = (bf16[256,768]{1,0:T(8,128)(2,1)}, f32[256,768]{1,0:T(8,128)}, f32[768,3072]{1,0:T(8,128)}, f32[3072,768]{1,0:T(8,128)}, f32[768,2304]{1,0:T(8,...) custom-call(f32[80,128]{1,0:T(8,128)} %get-tuple-element.39.small, ...), custom_call_target="tpu_custom_call" | custom-call | tf_op jit(solution)/shard_map/pallas_call | solution.py:879
